TPU v7x, 32 devices: a whole 2x2x4 slice. The times are simulated.
32 devices in a mesh: dp: 4 (over x, core), seq: 8 (over z, y).
Axes of the slice: x: 2, y: 2, z: 4, core: 2. Of those that a mesh axis runs over, the one named last changes fastest.
Arguments:
- inputs: bfloat16 [4, 4096, 1024], P('dp', 'seq'), may hold values from -6 to 6
- first_values: bfloat16 [4, 4096, 1024], P('dp', 'seq'), may hold values from -6 to 6
- lengths: int32 [4, 8], P('dp'), may hold values from 1 to 4096, as said below
- w_query: bfloat16 [1024, 1024], P(('dp', 'seq')), may hold values from -0.1875 to 0.1875
- w_key: bfloat16 [1024, 1024], P(('dp', 'seq')), may hold values from -0.1875 to 0.1875
- w_value: bfloat16 [1024, 1024], P(('dp', 'seq')), may hold values from -0.1875 to 0.1875
- w_out: bfloat16 [1024, 1024], P(('dp', 'seq')), may hold values from -2 to 2
- gain_attn: bfloat16 [1024], P(('dp', 'seq')), may hold values from 0.5 to 1.5
- w_gate: bfloat16 [1024, 2816], P(('dp', 'seq')), may hold values from -0.1875 to 0.1875
- w_up: bfloat16 [1024, 2816], P(('dp', 'seq')), may hold values from -0.1875 to 0.1875
- w_down: bfloat16 [2816, 1024], P(('dp', 'seq')), may hold values from -0.109375 to 0.109375
- gain_mlp: bfloat16 [1024], P(('dp', 'seq')), may hold values from 0.5 to 1.5
- cotangent: bfloat16 [4, 4096, 1024], P('dp', 'seq'), may hold values from -6 to 6
Outputs:
- output: bfloat16 [4, 4096, 1024], P('dp', 'seq')
- grad_inputs: float32 [4, 4096, 1024], P('dp', 'seq')
- grad_first_values: float32 [4, 4096, 1024], P('dp', 'seq')
- grad_w_query: float32 [1024, 1024], P(('dp', 'seq'))
- grad_w_key: float32 [1024, 1024], P(('dp', 'seq'))
- grad_w_value: float32 [1024, 1024], P(('dp', 'seq'))
- grad_w_out: float32 [1024, 1024], P(('dp', 'seq'))
- grad_gain_attn: float32 [1024], P(('dp', 'seq'))
- grad_w_gate: float32 [1024, 2816], P(('dp', 'seq'))
- grad_w_up: float32 [1024, 2816], P(('dp', 'seq'))
- grad_w_down: float32 [2816, 1024], P(('dp', 'seq'))
- grad_gain_mlp: float32 [1024], P(('dp', 'seq'))
Inputs may be any that keep to these rules, and one draw needn't show every extreme that they name: Each row's 8 lengths sum to 4096; one of them, at a place drawn for each row, is longer than 3584; each of the others is below 73.
All inputs are finite; a program needn't handle non-finite values.
Results may differ from a plain program's by a relative error of at most 0.023.
Values may be sent and summed in bfloat16 or wider, within the bound.
A program may use at most 192 MiB of HBM per device.

v0:
```python
import jax
import jax.numpy as jnp
from jax import lax
from jax.sharding import PartitionSpec as P

HEAD_DIM = 64


EPS = 1e-06
THETA = 10000.0


def passed_along(value, axis, steps):
    count = lax.axis_size(axis)
    pairs = [(source, (source + steps) % count) for source in range(count)]
    return lax.ppermute(value, axis, pairs)


def passed_along_2(value, axis, steps):
    count = lax.axis_size(axis)
    initial, last = (max(0, -steps), min(count, count - steps))
    return lax.ppermute(value, axis, [(source, source + steps) for source in range(initial, last)])


def doc_tables(lengths, full_len):
    row_count, doc_count = lengths.shape
    doc_ends = jnp.cumsum(lengths, axis=1)
    doc_starts = doc_ends - lengths
    position = jnp.arange(full_len, dtype=jnp.int32)
    segment = jnp.sum((position[None, :, None] >= doc_ends[:, None, :]).astype(jnp.int32), axis=2)
    chosen = segment[:, :, None] == jnp.arange(doc_count, dtype=jnp.int32)[None, None, :]
    offsets = jnp.sum(jnp.where(chosen, doc_starts[:, None, :], 0), axis=2)
    row_base = jnp.arange(row_count, dtype=jnp.int32)[:, None] * doc_count
    return (segment + row_base, position[None, :] - offsets)


def rotate(values, position, direction):
    half_dim = values.shape[-1] // 2
    freqs = THETA ** (-jnp.arange(half_dim, dtype=jnp.float32) * 2.0 / values.shape[-1])
    angles = position.astype(jnp.float32)[..., None] * freqs
    cosine = jnp.cos(angles)[..., None, :]
    sine = direction * jnp.sin(angles)[..., None, :]
    first = values[..., :half_dim]
    second = values[..., half_dim:]
    return jnp.concatenate(
        [first * cosine - second * sine, first * sine + second * cosine], axis=-1
    )


def norm_forward(values, gain):
    scale_inv = lax.rsqrt(jnp.mean(values * values, axis=-1, keepdims=True) + EPS)
    return values * scale_inv * gain


def norm_back(grad_normed, values, gain):
    scale_inv = lax.rsqrt(jnp.mean(values * values, axis=-1, keepdims=True) + EPS)
    normed = values * scale_inv
    grad_scaled = grad_normed * gain
    grad_values = scale_inv * (
        grad_scaled - normed * jnp.mean(grad_scaled * normed, axis=-1, keepdims=True)
    )
    grad_gain = jnp.sum(grad_normed * normed, axis=0)
    return (grad_values, grad_gain)


def across(left, right):
    return lax.dot_general(
        left, right, (((0,), (0,)), ((), ())), preferred_element_type=jnp.float32
    )


def against(left, right):
    return lax.dot_general(
        left, right, (((1,), (1,)), ((), ())), preferred_element_type=jnp.float32
    )


def allowed_pairs(query_meta, key_meta):
    return (query_meta[0][:, None] == key_meta[0][None, :]) & (
        query_meta[1][:, None] >= key_meta[1][None, :]
    )


def return_grads(grad_keys, grad_mixeds):
    return (
        passed_along(grad_keys.astype(jnp.bfloat16), "seq", 1).astype(grad_keys.dtype),
        passed_along(grad_mixeds.astype(jnp.bfloat16), "seq", 1).astype(grad_mixeds.dtype),
    )


def softmax_step(state, queries, query_meta, key_part, mixed_part, key_meta):
    best, total, accum = state
    heads, head_size = (queries.shape[1], queries.shape[2])
    key_heads = key_part.reshape(key_part.shape[0], heads, head_size)
    mixed_heads = mixed_part.reshape(mixed_part.shape[0], heads, head_size)
    scores = jnp.einsum(
        "nhd,khd->hnk", queries, key_heads, preferred_element_type=jnp.float32
    ) * head_size ** (-0.5)
    allowed = allowed_pairs(query_meta, key_meta)[None]
    scores = jnp.where(allowed, scores, -1e30)
    new_best = jnp.maximum(best, jnp.max(scores, axis=2))
    weights = jnp.where(allowed, jnp.exp(scores - new_best[:, :, None]), 0.0)
    factor = jnp.exp(best - new_best)
    total = total * factor + jnp.sum(weights, axis=2)
    update = jnp.einsum(
        "hnk,khd->nhd",
        weights.astype(jnp.bfloat16),
        mixed_heads,
        preferred_element_type=jnp.float32,
    )
    accum = accum * factor.T[:, :, None] + update
    return (new_best, total, accum)


def gradient_step(
    grad_query, queries, grad_att, log_total, delta, query_meta, key_part, mixed_part, key_meta
):
    heads, head_size = (queries.shape[1], queries.shape[2])
    scale = head_size ** (-0.5)
    key_heads = key_part.reshape(key_part.shape[0], heads, head_size)
    mixed_heads = mixed_part.reshape(mixed_part.shape[0], heads, head_size)
    scores = (
        jnp.einsum("nhd,khd->hnk", queries, key_heads, preferred_element_type=jnp.float32) * scale
    )
    allowed = allowed_pairs(query_meta, key_meta)[None]
    weights = jnp.where(
        allowed, jnp.exp(jnp.where(allowed, scores, -1e30) - log_total[:, :, None]), 0.0
    )
    grad_mixed = jnp.einsum(
        "hnk,nhd->khd", weights.astype(jnp.bfloat16), grad_att, preferred_element_type=jnp.float32
    )
    grad_weights = jnp.einsum(
        "nhd,khd->hnk", grad_att, mixed_heads, preferred_element_type=jnp.float32
    )
    grad_scores = (weights * (grad_weights - delta[:, :, None])).astype(jnp.bfloat16)
    grad_query = (
        grad_query
        + jnp.einsum("hnk,khd->nhd", grad_scores, key_heads, preferred_element_type=jnp.float32)
        * scale
    )
    grad_key = (
        jnp.einsum("hnk,nhd->khd", grad_scores, queries, preferred_element_type=jnp.float32) * scale
    )
    return (grad_query, grad_key.reshape(key_part.shape), grad_mixed.reshape(mixed_part.shape))


def shards(
    inputs,
    first_values,
    lengths,
    w_query,
    w_key,
    w_value,
    w_out,
    gain_attn,
    w_gate,
    w_up,
    w_down,
    gain_mlp,
    cotangent,
):
    row_count, group_len, width = inputs.shape
    tokens = row_count * group_len
    heads = width // HEAD_DIM
    seq_count = lax.axis_size("seq")
    seq_rank = lax.axis_index("seq")
    query_full, key_full, value_full, out_full, gain_one = (
        lax.all_gather(w_query, ("dp", "seq"), axis=0, tiled=True),
        lax.all_gather(w_key, ("dp", "seq"), axis=0, tiled=True),
        lax.all_gather(w_value, ("dp", "seq"), axis=0, tiled=True),
        lax.all_gather(w_out, ("dp", "seq"), axis=0, tiled=True),
        lax.all_gather(gain_attn, ("dp", "seq"), axis=0, tiled=True),
    )
    gain_one = gain_one.astype(jnp.float32)
    segment_all, position_all = doc_tables(lengths, group_len * seq_count)
    time_all = jnp.arange(group_len * seq_count, dtype=jnp.int32)[None, :]

    def device_major(table):
        return table.reshape(row_count, seq_count, group_len).transpose(1, 0, 2).reshape(-1)

    seg_major = device_major(segment_all)
    time_major = device_major(time_all)
    pos_major = device_major(position_all)

    def rows_meta(start, count):
        return (
            lax.dynamic_slice_in_dim(seg_major, start, count),
            lax.dynamic_slice_in_dim(time_major, start, count),
        )

    query_meta = rows_meta(seq_rank * tokens, tokens)
    own_position = lax.dynamic_slice_in_dim(pos_major, seq_rank * tokens, tokens)
    x_in = inputs.reshape(tokens, width).astype(jnp.float32)
    hidden_in = norm_forward(x_in, gain_one).astype(jnp.bfloat16)
    query_raw = jnp.dot(hidden_in, query_full, preferred_element_type=jnp.float32)
    key_raw = jnp.dot(hidden_in, key_full, preferred_element_type=jnp.float32)
    value_raw = jnp.dot(hidden_in, value_full, preferred_element_type=jnp.float32)
    queries = rotate(query_raw.reshape(tokens, heads, HEAD_DIM), own_position, 1.0).astype(
        jnp.bfloat16
    )
    key_low = (
        rotate(key_raw.reshape(tokens, heads, HEAD_DIM), own_position, 1.0)
        .astype(jnp.bfloat16)
        .reshape(tokens, width)
    )
    first_flat = first_values.reshape(tokens, width).astype(jnp.float32)
    mixed_low = (0.5 * value_raw + 0.5 * first_flat).astype(jnp.bfloat16)
    init_state = (
        jnp.full((heads, tokens), -1e30, jnp.float32),
        jnp.zeros((heads, tokens), jnp.float32),
        jnp.zeros((tokens, heads, HEAD_DIM), jnp.float32),
    )

    def visit(state, key_part, mixed_part, key_meta):

        def visit_compute(current):
            return softmax_step(current, queries, query_meta, key_part, mixed_part, key_meta)

        def visit_unchanged(current):
            return current

        reached = jnp.min(key_meta[1]) <= jnp.max(query_meta[1])
        return lax.cond(reached, visit_compute, visit_unchanged, state)

    key_store = None
    mixed_store = None
    first_state = visit(init_state, key_low, mixed_low, query_meta)
    store_zero = jnp.zeros((seq_count, tokens, width), jnp.bfloat16)
    key_store = lax.dynamic_update_index_in_dim(store_zero, key_low, 0, 0)
    mixed_store = lax.dynamic_update_index_in_dim(store_zero, mixed_low, 0, 0)

    def forward_turn(turn, carry):
        state, key_part, mixed_part, keys_kept, mixed_kept = carry
        key_part, mixed_part = passed_along_2((key_part, mixed_part), "seq", 1)
        index = (seq_rank - turn) % seq_count
        state = visit(state, key_part, mixed_part, rows_meta(index * tokens, tokens))
        return (state, key_part, mixed_part, keys_kept, mixed_kept)

    (best, total, accum), unused_key, unused_mixed, key_store, mixed_store = lax.fori_loop(
        1, seq_count, forward_turn, (first_state, key_low, mixed_low, key_store, mixed_store)
    )
    att_float = accum / total.T[:, :, None]
    log_total = best + jnp.log(total)
    attended = att_float.reshape(tokens, width).astype(jnp.bfloat16)
    middle = x_in + jnp.dot(attended, out_full, preferred_element_type=jnp.float32)
    gate_full, up_full, down_full, gain_two = (
        lax.all_gather(w_gate, ("dp", "seq"), axis=0, tiled=True),
        lax.all_gather(w_up, ("dp", "seq"), axis=0, tiled=True),
        lax.all_gather(w_down, ("dp", "seq"), axis=0, tiled=True),
        lax.all_gather(gain_mlp, ("dp", "seq"), axis=0, tiled=True),
    )
    gain_two = gain_two.astype(jnp.float32)
    hidden_mlp = norm_forward(middle, gain_two).astype(jnp.bfloat16)
    gate = jnp.dot(hidden_mlp, gate_full, preferred_element_type=jnp.float32)
    upward = jnp.dot(hidden_mlp, up_full, preferred_element_type=jnp.float32)
    sigma = jax.nn.sigmoid(gate)
    silu_gate = gate * sigma
    inner = (silu_gate * upward).astype(jnp.bfloat16)
    result = middle + jnp.dot(inner, down_full, preferred_element_type=jnp.float32)
    output = result.astype(jnp.bfloat16).reshape(row_count, group_len, width)
    grad_y = cotangent.reshape(tokens, width)
    grad_down = across(inner, grad_y)
    grad_inner = against(grad_y, down_full)
    grad_gate_low = (grad_inner * upward * sigma * (1.0 + gate * (1.0 - sigma))).astype(
        jnp.bfloat16
    )
    grad_up_low = (grad_inner * silu_gate).astype(jnp.bfloat16)
    grad_gate = across(hidden_mlp, grad_gate_low)
    grad_up = across(hidden_mlp, grad_up_low)
    grad_hidden_mlp = against(grad_gate_low, gate_full) + against(grad_up_low, up_full)
    grad_middle, grad_gain_two = norm_back(grad_hidden_mlp, middle, gain_two)
    grad_middle = grad_middle + grad_y.astype(jnp.float32)
    grad_branch = grad_middle.astype(jnp.bfloat16)
    grad_out = across(attended, grad_branch)
    grad_att = against(grad_branch, out_full).astype(jnp.bfloat16).reshape(tokens, heads, HEAD_DIM)
    delta = jnp.sum(grad_att.astype(jnp.float32) * att_float, axis=2).T
    zero_rows = jnp.zeros((tokens, width), jnp.float32)

    def back_visit(grad_query, key_part, mixed_part, key_meta):

        def back_compute(current):
            return gradient_step(
                current,
                queries,
                grad_att,
                log_total,
                delta,
                query_meta,
                key_part,
                mixed_part,
                key_meta,
            )

        def back_unchanged(current):
            return (
                current,
                jnp.zeros(key_part.shape, jnp.float32),
                jnp.zeros(mixed_part.shape, jnp.float32),
            )

        reached = jnp.min(key_meta[1]) <= jnp.max(query_meta[1])
        return lax.cond(reached, back_compute, back_unchanged, grad_query)

    grad_query_init = jnp.zeros((tokens, heads, HEAD_DIM), jnp.float32)

    def back_turn(turn, carry):
        grad_query, key_part, mixed_part, grad_keys, grad_mixeds = carry
        index = (seq_rank - turn) % seq_count
        grad_query, add_key, add_mixed = back_visit(
            grad_query, key_part, mixed_part, rows_meta(index * tokens, tokens)
        )
        grad_keys, grad_mixeds = return_grads(grad_keys + add_key, grad_mixeds + add_mixed)
        key_part, mixed_part = passed_along_2((key_part, mixed_part), "seq", 1)
        return (grad_query, key_part, mixed_part, grad_keys, grad_mixeds)

    grad_query_rot, unused_key, unused_mixed, grad_key_rot, grad_mixed = lax.fori_loop(
        0, seq_count, back_turn, (grad_query_init, key_low, mixed_low, zero_rows, zero_rows)
    )
    grad_first = 0.5 * grad_mixed
    grad_value_low = grad_first.astype(jnp.bfloat16)
    grad_query_low = (
        rotate(grad_query_rot, own_position, -1.0).reshape(tokens, width).astype(jnp.bfloat16)
    )
    grad_key_low = (
        rotate(grad_key_rot.reshape(tokens, heads, HEAD_DIM), own_position, -1.0)
        .reshape(tokens, width)
        .astype(jnp.bfloat16)
    )
    grad_query_w = across(hidden_in, grad_query_low)
    grad_key_w = across(hidden_in, grad_key_low)
    grad_value_w = across(hidden_in, grad_value_low)
    grad_hidden_in = (
        against(grad_query_low, query_full)
        + against(grad_key_low, key_full)
        + against(grad_value_low, value_full)
    )
    grad_x, grad_gain_one = norm_back(grad_hidden_in, x_in, gain_one)
    grad_x = grad_x + grad_middle
    shard_q, shard_k, shard_v, shard_o, shard_g1, shard_gate, shard_up, shard_down, shard_g2 = (
        lax.psum_scatter(grad_query_w, ("dp", "seq"), scatter_dimension=0, tiled=True),
        lax.psum_scatter(grad_key_w, ("dp", "seq"), scatter_dimension=0, tiled=True),
        lax.psum_scatter(grad_value_w, ("dp", "seq"), scatter_dimension=0, tiled=True),
        lax.psum_scatter(grad_out, ("dp", "seq"), scatter_dimension=0, tiled=True),
        lax.psum_scatter(grad_gain_one, ("dp", "seq"), scatter_dimension=0, tiled=True),
        lax.psum_scatter(grad_gate, ("dp", "seq"), scatter_dimension=0, tiled=True),
        lax.psum_scatter(grad_up, ("dp", "seq"), scatter_dimension=0, tiled=True),
        lax.psum_scatter(grad_down, ("dp", "seq"), scatter_dimension=0, tiled=True),
        lax.psum_scatter(grad_gain_two, ("dp", "seq"), scatter_dimension=0, tiled=True),
    )
    return (
        output,
        grad_x.reshape(row_count, group_len, width),
        grad_first.reshape(row_count, group_len, width),
        shard_q,
        shard_k,
        shard_v,
        shard_o,
        shard_g1,
        shard_gate,
        shard_up,
        shard_down,
        shard_g2,
    )


def solution(mesh):
    placed = (
        P("dp", "seq", None),
        P("dp", "seq", None),
        P("dp", None),
        P(("dp", "seq"), None),
        P(("dp", "seq"), None),
        P(("dp", "seq"), None),
        P(("dp", "seq"), None),
        P(("dp", "seq")),
        P(("dp", "seq"), None),
        P(("dp", "seq"), None),
        P(("dp", "seq"), None),
        P(("dp", "seq")),
        P("dp", "seq", None),
    )
    return jax.shard_map(
        shards,
        mesh=mesh,
        in_specs=placed,
        out_specs=(
            P("dp", "seq", None),
            P("dp", "seq", None),
            P("dp", "seq", None),
            P(("dp", "seq"), None),
            P(("dp", "seq"), None),
            P(("dp", "seq"), None),
            P(("dp", "seq"), None),
            P(("dp", "seq")),
            P(("dp", "seq"), None),
            P(("dp", "seq"), None),
            P(("dp", "seq"), None),
            P(("dp", "seq")),
        ),
        check_vma=False,
    )
```

profile of v0, /device:TPU:0, one launch (start us, length us, event | category | flops | bytes accessed | tf_op | source)
XLA Modules:
  0.0 3176.8 jit_solution(10970300451406964845)
XLA Ops:
  17.2 42.2 %all-reduce.5 = (bf16[1024]{0:T(1024)(128)(2,1)S(1)}, bf16[1024]{0:T(1024)(128)(2,1)S(1)}) all-reduce(bf16[1024]{0:T(1024)(128)(2,1)S(1)} %dynamic-update-slice, bf16[1024]{0:T(1024)(128)(2,1)S(1)} %dynamic-update-slice.1), channel_id=1, replica_groups=mesh['dp'=4,'seq'=8] {'dp','seq'}, use_global_device_ids=true, to_apply=%add | all-reduce | flops 2048 | bytes 8192
  74.2 54.5 %all-gather.10.cloned.1.call-done = bf16[1024,1024]{1,0:T(8,128)(2,1)} async-done(((bf16[32,1024]{1,0:T(8,128)(2,1)}), bf16[1024,1024]{1,0:T(8,128)(2,1)}) %all-gather.10.cloned.1.call-update) | async-done | bytes 2097168 | tf_op jit(solution)/shard_map/all_gather | solution.py:169
  134.6 52.6 %all-gather.12.cloned.1.call-done = bf16[1024,1024]{1,0:T(8,128)(2,1)} async-done(((bf16[32,1024]{1,0:T(8,128)(2,1)}), bf16[1024,1024]{1,0:T(8,128)(2,1)}) %all-gather.12.cloned.1.call-update) | async-done | bytes 2097168 | tf_op jit(solution)/shard_map/all_gather | solution.py:170
  195.9 24.0 conditional.3
  219.9 453.8 %while.50 = (s32[]{:T(128)}, f32[16,512]{1,0:T(8,128)}, f32[16,512]{1,0:T(8,128)S(1)}, f32[512,16,64]{0,2,1:T(8,128)}, bf16[512,1024]{0,1:T(8,128)(2,1)}, /*inde...) while((s32[]{:T(128)}, f32[16,512]{1,0:T(8,128)}, ...), condition=%wide.region_16.17_spmd, body=%wide.region_10.16_spmd.sunk | while | flops 1130127872 | bytes 71844432 | solution.py:239
  250.8 23.1 collective-permute-done.1
  277.1 24.4 collective-permute-start
  329.8 23.3 collective-permute-done.1
  372.2 23.2 collective-permute-start.1
  431.0 27.1 collective-permute-start
  466.3 25.8 collective-permute-done
  729.2 1056.1 %while.51 = (s32[]{:T(128)}, f32[512,16,64]{0,2,1:T(8,128)}, bf16[512,1024]{0,1:T(8,128)(2,1)S(1)}, bf16[512,1024]{0,1:T(8,128)(2,1)}, f32[512,1024]{0,1:T(8,128...) while((s32[]{:T(128)}, f32[512,16,64]{0,2,1:T(8,128)}, ...), condition=%wide.region_24.25_spmd.clone, body=%wide.region_20.24_spmd.clone.sunk | while | flops 2741240320 | bytes 138265280 | solution.py:316
  733.7 35.8 %conditional.8 = (f32[512,16,64]{0,2,1:T(8,128)}, f32[512,1024]{0,1:T(8,128)S(1)}, f32[512,1024]{0,1:T(8,128)}) conditional(s32[]{:T(128)} %convert_element_type.361, f32[512,16,64]{0,2,1:T(8,128)} %get-tuple-element.1383, (s32[512]{0:T(512)S(1)}, s32[4096]{0:T(1024)S(1)}, s32[]{:T(128)}, s32[512]{0:T(512)S(1)}, s32[512]{0:T(512)S(1)}, ...), branch_computations={%region_22.22_spmd, %region_23.23_spmd} | conditional | flops 2737045504 | bytes 92123160 | solution.py:302
  822.4 48.3 %collective-permute-done.4 = bf16[512,1024]{0,1:T(8,128)(2,1)} collective-permute-done((bf16[512,1024]{0,1:T(8,128)(2,1)}, bf16[512,1024]{0,1:T(8,128)(2,1)}, u32[]{:S(2)}, u32[]{:S(2)}) %collective-permute-start.4) | collective-permute-done | bytes 1048608 | tf_op jit(solution)/shard_map/while/body/eval_jaxpr/ppermute | solution.py:16
  899.8 24.4 collective-permute-start.4
  969.0 32.9 %collective-permute-done.4 = bf16[512,1024]{0,1:T(8,128)(2,1)} collective-permute-done((bf16[512,1024]{0,1:T(8,128)(2,1)}, bf16[512,1024]{0,1:T(8,128)(2,1)}, u32[]{:S(2)}, u32[]{:S(2)}) %collective-permute-start.4) | collective-permute-done | bytes 1048608 | tf_op jit(solution)/shard_map/while/body/eval_jaxpr/ppermute | solution.py:16
  1036.1 39.9 %collective-permute-start.5 = (bf16[512,1024]{0,1:T(8,128)(2,1)}, bf16[512,1024]{0,1:T(8,128)(2,1)}, u32[]{:S(2)}, u32[]{:S(2)}) collective-permute-start(bf16[512,1024]{0,1:T(8,128)(2,1)} %fusion.145), channel_id=1, source_target_pairs={{0,1},{1,2},{2,3},{3,4},{4,5},{5,6},{6,7},{7,0},{8,9},{9,10},{10,1... | collective-permute-start | bytes 3145736 | tf_op jit(solution)/shard_map/while/body/eval_jaxpr/ppermute | solution.py:16
  1102.9 29.3 collective-permute-done.4
  1184.5 45.2 %collective-permute-start.2 = (bf16[512,1024]{0,1:T(8,128)(2,1)S(1)}, bf16[512,1024]{0,1:T(8,128)(2,1)S(1)}, u32[]{:S(2)}, u32[]{:S(2)}) collective-permute-start(bf16[512,1024]{0,1:T(8,128)(2,1)S(1)} %copy.110), channel_id=1, source_target_pairs={{0,1},{1,2},{2,3},{3,4},{4,5},{5,6},{6,7},{8,9},{9,10},{10,11},{11... | collective-permute-start | bytes 3145736 | tf_op jit(solution)/shard_map/while/body/eval_jaxpr/ppermute | solution.py:22
  1333.0 40.1 %collective-permute-start.3 = (bf16[512,1024]{0,1:T(8,128)(2,1)}, bf16[512,1024]{0,1:T(8,128)(2,1)}, u32[]{:S(2)}, u32[]{:S(2)}) collective-permute-start(bf16[512,1024]{0,1:T(8,128)(2,1)} %copy.111), channel_id=1, source_target_pairs={{0,1},{1,2},{2,3},{3,4},{4,5},{5,6},{6,7},{8,9},{9,10},{10,11},{11... | collective-permute-start | bytes 3145736 | tf_op jit(solution)/shard_map/while/body/eval_jaxpr/ppermute | solution.py:22
  1467.6 50.3 %collective-permute-done.4 = bf16[512,1024]{0,1:T(8,128)(2,1)} collective-permute-done((bf16[512,1024]{0,1:T(8,128)(2,1)}, bf16[512,1024]{0,1:T(8,128)(2,1)}, u32[]{:S(2)}, u32[]{:S(2)}) %collective-permute-start.4) | collective-permute-done | bytes 1048608 | tf_op jit(solution)/shard_map/while/body/eval_jaxpr/ppermute | solution.py:16
  1594.9 50.5 %collective-permute-done.4 = bf16[512,1024]{0,1:T(8,128)(2,1)} collective-permute-done((bf16[512,1024]{0,1:T(8,128)(2,1)}, bf16[512,1024]{0,1:T(8,128)(2,1)}, u32[]{:S(2)}, u32[]{:S(2)}) %collective-permute-start.4) | collective-permute-done | bytes 1048608 | tf_op jit(solution)/shard_map/while/body/eval_jaxpr/ppermute | solution.py:16
  1681.3 23.8 collective-permute-start.3
  1705.2 65.9 %collective-permute-done.4 = bf16[512,1024]{0,1:T(8,128)(2,1)} collective-permute-done((bf16[512,1024]{0,1:T(8,128)(2,1)}, bf16[512,1024]{0,1:T(8,128)(2,1)}, u32[]{:S(2)}, u32[]{:S(2)}) %collective-permute-start.4) | collective-permute-done | bytes 1048608 | tf_op jit(solution)/shard_map/while/body/eval_jaxpr/ppermute | solution.py:16
  1846.8 88.6 %all-reduce.4 = (f32[1024]{0:T(1024)S(1)}, f32[1024]{0:T(1024)S(1)}) all-reduce(f32[1024]{0:T(1024)S(1)} %get-tuple-element.991, f32[1024]{0:T(1024)S(1)} %copy-done.38), channel_id=6, replica_groups=mesh['dp'=4,'seq'=8] {'dp','seq'}, use_global_device_ids=true, to_apply=%region_31.32.clone | all-reduce | flops 2048 | bytes 16384
  1949.5 35.3 %reduce-scatter.8.cloned.1.call-done = f32[32,1024]{1,0:T(8,128)} async-done(((f32[1024,1024]{1,0:T(8,128)}), f32[32,1024]{1,0:T(8,128)}) %reduce-scatter.8.cloned.1.call-update) | async-done | bytes 131088 | tf_op jit(solution)/shard_map/reduce_scatter | solution.py:340
  1984.8 144.6 %reduce-scatter.10.cloned.1.call-done = f32[32,1024]{1,0:T(8,128)} async-done(((f32[1024,1024]{1,0:T(8,128)}), f32[32,1024]{1,0:T(8,128)}) %reduce-scatter.10.cloned.1.call-update) | async-done | bytes 131088 | tf_op jit(solution)/shard_map/reduce_scatter | solution.py:341
  2129.4 144.1 %reduce-scatter.12.cloned.1.call-done = f32[32,1024]{1,0:T(8,128)} async-done(((f32[1024,1024]{1,0:T(8,128)}), f32[32,1024]{1,0:T(8,128)}) %reduce-scatter.12.cloned.1.call-update) | async-done | bytes 131088 | tf_op jit(solution)/shard_map/reduce_scatter | solution.py:342
  2273.5 144.3 %reduce-scatter.14.cloned.1.call-done = f32[32,1024]{1,0:T(8,128)} async-done(((f32[1024,1024]{1,0:T(8,128)}), f32[32,1024]{1,0:T(8,128)}) %reduce-scatter.14.cloned.1.call-update) | async-done | bytes 131088 | tf_op jit(solution)/shard_map/reduce_scatter | solution.py:343
  2417.8 250.2 %reduce-scatter.16.cloned.1.call-done = f32[32,2816]{1,0:T(8,128)} async-done(((f32[1024,2816]{1,0:T(8,128)}), f32[32,2816]{1,0:T(8,128)}) %reduce-scatter.16.cloned.1.call-update) | async-done | bytes 360464 | tf_op jit(solution)/shard_map/reduce_scatter | solution.py:345
  2668.0 250.8 %reduce-scatter.18.cloned.1.call-done = f32[32,2816]{1,0:T(8,128)} async-done(((f32[1024,2816]{1,0:T(8,128)}), f32[32,2816]{1,0:T(8,128)}) %reduce-scatter.18.cloned.1.call-update) | async-done | bytes 360464 | tf_op jit(solution)/shard_map/reduce_scatter | solution.py:346
  2918.8 251.0 %reduce-scatter.20.cloned.1.call-done = f32[88,1024]{1,0:T(8,128)} async-done(((f32[2816,1024]{1,0:T(8,128)}), f32[88,1024]{1,0:T(8,128)}) %reduce-scatter.20.cloned.1.call-update) | async-done | bytes 360464 | tf_op jit(solution)/shard_map/reduce_scatter | solution.py:347
  (397 shorter events, 1097.2 us)
Async XLA Ops:
  7.9 120.9 %all-gather.10.cloned.1.call-start = ((), (), s32[]{:S(2)}) async-start(), calls=%async_computation.8 | async-start | bytes 2162688 | tf_op jit(solution)/shard_map/all_gather | solution.py:169
  8.7 178.5 %all-gather.12.cloned.1.call-start = ((), (), s32[]{:S(2)}) async-start(), calls=%async_computation.9 | async-start | bytes 2162688 | tf_op jit(solution)/shard_map/all_gather | solution.py:170
  9.4 666.3 %all-gather.14.cloned.1.call-start = ((), (), s32[]{:S(2)}) async-start(), calls=%async_computation.10 | async-start | bytes 2162688 | tf_op jit(solution)/shard_map/all_gather | solution.py:171
  10.0 670.7 %all-gather.16.cloned.1.call-start = ((), (), s32[]{:S(2)}) async-start(), calls=%async_computation.11 | async-start | bytes 5947392 | tf_op jit(solution)/shard_map/all_gather | solution.py:247
  10.6 677.9 %all-gather.18.cloned.1.call-start = ((), (), s32[]{:S(2)}) async-start(), calls=%async_computation.12 | async-start | bytes 5947392 | tf_op jit(solution)/shard_map/all_gather | solution.py:248
  11.1 685.0 %all-gather.20.cloned.1.call-start = ((), (), s32[]{:S(2)}) async-start(), calls=%async_computation.13 | async-start | bytes 5947392 | tf_op jit(solution)/shard_map/all_gather | solution.py:249
  11.9 1972.9 %reduce-scatter.8.cloned.1.call-start = ((), (), s32[]{:S(2)}) async-start(), calls=%async_computation.14 | async-start | bytes 4325376 | tf_op jit(solution)/shard_map/reduce_scatter | solution.py:340
  771.1 99.6 %collective-permute-start.4 = (bf16[512,1024]{0,1:T(8,128)(2,1)}, bf16[512,1024]{0,1:T(8,128)(2,1)}, u32[]{:S(2)}, u32[]{:S(2)}) collective-permute-start(bf16[512,1024]{0,1:T(8,128)(2,1)} %fusion.144), channel_id=1, source_target_pairs={{0,1},{1,2},{2,3},{3,4},{4,5},{5,6},{6,7},{7,0},{8,9},{9,10},{10,1... | collective-permute-start | bytes 3145736 | tf_op jit(solution)/shard_map/while/body/eval_jaxpr/ppermute | solution.py:16
  793.9 93.5 %collective-permute-start.5 = (bf16[512,1024]{0,1:T(8,128)(2,1)}, bf16[512,1024]{0,1:T(8,128)(2,1)}, u32[]{:S(2)}, u32[]{:S(2)}) collective-permute-start(bf16[512,1024]{0,1:T(8,128)(2,1)} %fusion.145), channel_id=1, source_target_pairs={{0,1},{1,2},{2,3},{3,4},{4,5},{5,6},{6,7},{7,0},{8,9},{9,10},{10,1... | collective-permute-start | bytes 3145736 | tf_op jit(solution)/shard_map/while/body/eval_jaxpr/ppermute | solution.py:16
  899.8 102.2 %collective-permute-start.4 = (bf16[512,1024]{0,1:T(8,128)(2,1)}, bf16[512,1024]{0,1:T(8,128)(2,1)}, u32[]{:S(2)}, u32[]{:S(2)}) collective-permute-start(bf16[512,1024]{0,1:T(8,128)(2,1)} %fusion.144), channel_id=1, source_target_pairs={{0,1},{1,2},{2,3},{3,4},{4,5},{5,6},{6,7},{7,0},{8,9},{9,10},{10,1... | collective-permute-start | bytes 3145736 | tf_op jit(solution)/shard_map/while/body/eval_jaxpr/ppermute | solution.py:16
  1030.0 102.1 %collective-permute-start.4 = (bf16[512,1024]{0,1:T(8,128)(2,1)}, bf16[512,1024]{0,1:T(8,128)(2,1)}, u32[]{:S(2)}, u32[]{:S(2)}) collective-permute-start(bf16[512,1024]{0,1:T(8,128)(2,1)} %fusion.144), channel_id=1, source_target_pairs={{0,1},{1,2},{2,3},{3,4},{4,5},{5,6},{6,7},{7,0},{8,9},{9,10},{10,1... | collective-permute-start | bytes 3145736 | tf_op jit(solution)/shard_map/while/body/eval_jaxpr/ppermute | solution.py:16
  1036.1 111.0 %collective-permute-start.5 = (bf16[512,1024]{0,1:T(8,128)(2,1)}, bf16[512,1024]{0,1:T(8,128)(2,1)}, u32[]{:S(2)}, u32[]{:S(2)}) collective-permute-start(bf16[512,1024]{0,1:T(8,128)(2,1)} %fusion.145), channel_id=1, source_target_pairs={{0,1},{1,2},{2,3},{3,4},{4,5},{5,6},{6,7},{7,0},{8,9},{9,10},{10,1... | collective-permute-start | bytes 3145736 | tf_op jit(solution)/shard_map/while/body/eval_jaxpr/ppermute | solution.py:16
  1159.4 102.1 %collective-permute-start.4 = (bf16[512,1024]{0,1:T(8,128)(2,1)}, bf16[512,1024]{0,1:T(8,128)(2,1)}, u32[]{:S(2)}, u32[]{:S(2)}) collective-permute-start(bf16[512,1024]{0,1:T(8,128)(2,1)} %fusion.144), channel_id=1, source_target_pairs={{0,1},{1,2},{2,3},{3,4},{4,5},{5,6},{6,7},{7,0},{8,9},{9,10},{10,1... | collective-permute-start | bytes 3145736 | tf_op jit(solution)/shard_map/while/body/eval_jaxpr/ppermute | solution.py:16
  1172.1 103.4 %collective-permute-start.5 = (bf16[512,1024]{0,1:T(8,128)(2,1)}, bf16[512,1024]{0,1:T(8,128)(2,1)}, u32[]{:S(2)}, u32[]{:S(2)}) collective-permute-start(bf16[512,1024]{0,1:T(8,128)(2,1)} %fusion.145), channel_id=1, source_target_pairs={{0,1},{1,2},{2,3},{3,4},{4,5},{5,6},{6,7},{7,0},{8,9},{9,10},{10,1... | collective-permute-start | bytes 3145736 | tf_op jit(solution)/shard_map/while/body/eval_jaxpr/ppermute | solution.py:16
  1184.5 93.9 %collective-permute-start.2 = (bf16[512,1024]{0,1:T(8,128)(2,1)S(1)}, bf16[512,1024]{0,1:T(8,128)(2,1)S(1)}, u32[]{:S(2)}, u32[]{:S(2)}) collective-permute-start(bf16[512,1024]{0,1:T(8,128)(2,1)S(1)} %copy.110), channel_id=1, source_target_pairs={{0,1},{1,2},{2,3},{3,4},{4,5},{5,6},{6,7},{8,9},{9,10},{10,11},{11... | collective-permute-start | bytes 3145736 | tf_op jit(solution)/shard_map/while/body/eval_jaxpr/ppermute | solution.py:22
  1287.8 102.1 %collective-permute-start.4 = (bf16[512,1024]{0,1:T(8,128)(2,1)}, bf16[512,1024]{0,1:T(8,128)(2,1)}, u32[]{:S(2)}, u32[]{:S(2)}) collective-permute-start(bf16[512,1024]{0,1:T(8,128)(2,1)} %fusion.144), channel_id=1, source_target_pairs={{0,1},{1,2},{2,3},{3,4},{4,5},{5,6},{6,7},{7,0},{8,9},{9,10},{10,1... | collective-permute-start | bytes 3145736 | tf_op jit(solution)/shard_map/while/body/eval_jaxpr/ppermute | solution.py:16
  1302.8 100.2 %collective-permute-start.5 = (bf16[512,1024]{0,1:T(8,128)(2,1)}, bf16[512,1024]{0,1:T(8,128)(2,1)}, u32[]{:S(2)}, u32[]{:S(2)}) collective-permute-start(bf16[512,1024]{0,1:T(8,128)(2,1)} %fusion.145), channel_id=1, source_target_pairs={{0,1},{1,2},{2,3},{3,4},{4,5},{5,6},{6,7},{7,0},{8,9},{9,10},{10,1... | collective-permute-start | bytes 3145736 | tf_op jit(solution)/shard_map/while/body/eval_jaxpr/ppermute | solution.py:16
  1415.4 102.6 %collective-permute-start.4 = (bf16[512,1024]{0,1:T(8,128)(2,1)}, bf16[512,1024]{0,1:T(8,128)(2,1)}, u32[]{:S(2)}, u32[]{:S(2)}) collective-permute-start(bf16[512,1024]{0,1:T(8,128)(2,1)} %fusion.144), channel_id=1, source_target_pairs={{0,1},{1,2},{2,3},{3,4},{4,5},{5,6},{6,7},{7,0},{8,9},{9,10},{10,1... | collective-permute-start | bytes 3145736 | tf_op jit(solution)/shard_map/while/body/eval_jaxpr/ppermute | solution.py:16
  1418.7 111.6 %collective-permute-start.5 = (bf16[512,1024]{0,1:T(8,128)(2,1)}, bf16[512,1024]{0,1:T(8,128)(2,1)}, u32[]{:S(2)}, u32[]{:S(2)}) collective-permute-start(bf16[512,1024]{0,1:T(8,128)(2,1)} %fusion.145), channel_id=1, source_target_pairs={{0,1},{1,2},{2,3},{3,4},{4,5},{5,6},{6,7},{7,0},{8,9},{9,10},{10,1... | collective-permute-start | bytes 3145736 | tf_op jit(solution)/shard_map/while/body/eval_jaxpr/ppermute | solution.py:16
  1542.6 102.8 %collective-permute-start.4 = (bf16[512,1024]{0,1:T(8,128)(2,1)}, bf16[512,1024]{0,1:T(8,128)(2,1)}, u32[]{:S(2)}, u32[]{:S(2)}) collective-permute-start(bf16[512,1024]{0,1:T(8,128)(2,1)} %fusion.144), channel_id=1, source_target_pairs={{0,1},{1,2},{2,3},{3,4},{4,5},{5,6},{6,7},{7,0},{8,9},{9,10},{10,1... | collective-permute-start | bytes 3145736 | tf_op jit(solution)/shard_map/while/body/eval_jaxpr/ppermute | solution.py:16
  1545.7 111.1 %collective-permute-start.5 = (bf16[512,1024]{0,1:T(8,128)(2,1)}, bf16[512,1024]{0,1:T(8,128)(2,1)}, u32[]{:S(2)}, u32[]{:S(2)}) collective-permute-start(bf16[512,1024]{0,1:T(8,128)(2,1)} %fusion.145), channel_id=1, source_target_pairs={{0,1},{1,2},{2,3},{3,4},{4,5},{5,6},{6,7},{7,0},{8,9},{9,10},{10,1... | collective-permute-start | bytes 3145736 | tf_op jit(solution)/shard_map/while/body/eval_jaxpr/ppermute | solution.py:16
  1549.7 110.0 %collective-permute-start.2 = (bf16[512,1024]{0,1:T(8,128)(2,1)S(1)}, bf16[512,1024]{0,1:T(8,128)(2,1)S(1)}, u32[]{:S(2)}, u32[]{:S(2)}) collective-permute-start(bf16[512,1024]{0,1:T(8,128)(2,1)S(1)} %copy.110), channel_id=1, source_target_pairs={{0,1},{1,2},{2,3},{3,4},{4,5},{5,6},{6,7},{8,9},{9,10},{10,11},{11... | collective-permute-start | bytes 3145736 | tf_op jit(solution)/shard_map/while/body/eval_jaxpr/ppermute | solution.py:22
  1669.1 101.9 %collective-permute-start.4 = (bf16[512,1024]{0,1:T(8,128)(2,1)}, bf16[512,1024]{0,1:T(8,128)(2,1)}, u32[]{:S(2)}, u32[]{:S(2)}) collective-permute-start(bf16[512,1024]{0,1:T(8,128)(2,1)} %fusion.144), channel_id=1, source_target_pairs={{0,1},{1,2},{2,3},{3,4},{4,5},{5,6},{6,7},{7,0},{8,9},{9,10},{10,1... | collective-permute-start | bytes 3145736 | tf_op jit(solution)/shard_map/while/body/eval_jaxpr/ppermute | solution.py:16
  1672.2 110.0 %collective-permute-start.5 = (bf16[512,1024]{0,1:T(8,128)(2,1)}, bf16[512,1024]{0,1:T(8,128)(2,1)}, u32[]{:S(2)}, u32[]{:S(2)}) collective-permute-start(bf16[512,1024]{0,1:T(8,128)(2,1)} %fusion.145), channel_id=1, source_target_pairs={{0,1},{1,2},{2,3},{3,4},{4,5},{5,6},{6,7},{7,0},{8,9},{9,10},{10,1... | collective-permute-start | bytes 3145736 | tf_op jit(solution)/shard_map/while/body/eval_jaxpr/ppermute | solution.py:16
  1672.3 112.8 %collective-permute-start.2 = (bf16[512,1024]{0,1:T(8,128)(2,1)S(1)}, bf16[512,1024]{0,1:T(8,128)(2,1)S(1)}, u32[]{:S(2)}, u32[]{:S(2)}) collective-permute-start(bf16[512,1024]{0,1:T(8,128)(2,1)S(1)} %copy.110), channel_id=1, source_target_pairs={{0,1},{1,2},{2,3},{3,4},{4,5},{5,6},{6,7},{8,9},{9,10},{10,11},{11... | collective-permute-start | bytes 3145736 | tf_op jit(solution)/shard_map/while/body/eval_jaxpr/ppermute | solution.py:22
  1681.3 103.8 %collective-permute-start.3 = (bf16[512,1024]{0,1:T(8,128)(2,1)}, bf16[512,1024]{0,1:T(8,128)(2,1)}, u32[]{:S(2)}, u32[]{:S(2)}) collective-permute-start(bf16[512,1024]{0,1:T(8,128)(2,1)} %copy.111), channel_id=1, source_target_pairs={{0,1},{1,2},{2,3},{3,4},{4,5},{5,6},{6,7},{8,9},{9,10},{10,11},{11... | collective-permute-start | bytes 3145736 | tf_op jit(solution)/shard_map/while/body/eval_jaxpr/ppermute | solution.py:22
  1793.3 336.1 %reduce-scatter.10.cloned.1.call-start = ((), (), s32[]{:S(2)}) async-start(), calls=%async_computation.15 | async-start | bytes 4325376 | tf_op jit(solution)/shard_map/reduce_scatter | solution.py:341
  1796.9 476.5 %reduce-scatter.12.cloned.1.call-start = ((), (), s32[]{:S(2)}) async-start(), calls=%async_computation.16 | async-start | bytes 4325376 | tf_op jit(solution)/shard_map/reduce_scatter | solution.py:342
  1805.2 612.5 %reduce-scatter.14.cloned.1.call-start = ((), (), s32[]{:S(2)}) async-start(), calls=%async_computation.17 | async-start | bytes 4325376 | tf_op jit(solution)/shard_map/reduce_scatter | solution.py:343
  1811.3 856.7 %reduce-scatter.16.cloned.1.call-start = ((), (), s32[]{:S(2)}) async-start(), calls=%async_computation.18 | async-start | bytes 11894784 | tf_op jit(solution)/shard_map/reduce_scatter | solution.py:345
  1820.3 1098.5 %reduce-scatter.18.cloned.1.call-start = ((), (), s32[]{:S(2)}) async-start(), calls=%async_computation.19 | async-start | bytes 11894784 | tf_op jit(solution)/shard_map/reduce_scatter | solution.py:346
  1828.1 1341.7 %reduce-scatter.20.cloned.1.call-start = ((), (), s32[]{:S(2)}) async-start(), calls=%async_computation.20 | async-start | bytes 11894784 | tf_op jit(solution)/shard_map/reduce_scatter | solution.py:347
  (78 other events, 4473.6 us)
Sparse Core Ops, SparseCore 0:
  11.0 59.2 all-gather.7
  73.3 55.4 all-gather.9
  131.8 55.3 all-gather.11
  190.0 57.7 all-gather.13
  250.6 71.9 all-gather.15
  325.3 73.6 all-gather.17
  401.9 89.2 all-gather.19
  1793.4 191.3 reduce-scatter.7
  1987.6 141.6 reduce-scatter.9
  2132.1 141.3 reduce-scatter.11
  2276.3 141.4 reduce-scatter.13
  2420.5 247.4 reduce-scatter.15
  2670.9 247.8 reduce-scatter.17
  2921.6 248.2 reduce-scatter.19
where the time goes:
time: 3190 us; the launch traced here: 3180 us
  waiting for transfers between devices  1970 us (62%)
  starting transfers between devices  666 us (21%)
  matrix products  153 us (5%)
  other arithmetic  131 us (4%)
  blocking collectives  131 us (4%)
  local copies, waits for them, and re-layouts  90.4 us (3%)
    ppermute x30, starting transfers between devices, passed_along_2(): lax.ppermute(value, axis, [(source, source + steps) for source in range(i...  481 us
    ppermute x16, waiting for transfers between devices, passed_along(): return lax.ppermute(value, axis, pairs)  398 us
    reduce_scatter x1, waiting for transfers between devices, shards(): lax.psum_scatter(grad_down, ('dp', 'seq'), scatter_dimension=0, tiled=True)  251 us
    reduce_scatter x1, waiting for transfers between devices, shards(): lax.psum_scatter(grad_up, ('dp', 'seq'), scatter_dimension=0, tiled=True)  251 us
    reduce_scatter x1, waiting for transfers between devices, shards(): lax.psum_scatter(grad_gate, ('dp', 'seq'), scatter_dimension=0, tiled=True)  250 us
    ppermute x30, waiting for transfers between devices, passed_along_2(): lax.ppermute(value, axis, [(source, source + steps) for source in range(i...  230 us
    ppermute x16, starting transfers between devices, passed_along(): return lax.ppermute(value, axis, pairs)  185 us
    reduce_scatter x1, waiting for transfers between devices, shards(): lax.psum_scatter(grad_key_w, ('dp', 'seq'), scatter_dimension=0, tiled=True)  145 us
  transfers between devices with their start and end apart: 60, of which 39 were waited for; matrix products, arithmetic and copies ran while one was open for 7% of the time, Pallas kernels for 0%

commit v1 on v0

v1 whole, which is shorter than its diff:
```python
import functools

import jax
import jax.numpy as jnp
from jax import lax
from jax.experimental import pallas as pl
from jax.experimental.pallas import tpu as pltpu
from jax.sharding import PartitionSpec as P

HEAD_DIM = 64
EPS = 1e-06
THETA = 10000.0
NEG = -1e30
MESH = pl.DeviceIdType.MESH
BF16 = jnp.bfloat16
F32 = jnp.float32
VMEM = pltpu.VMEM
MIB = 1 << 20


def dot(left, right, left_dim=1, right_dim=0):
    return lax.dot_general(
        left, right, (((left_dim,), (right_dim,)), ((), ())), preferred_element_type=F32
    )


def across(left, right):
    return dot(left, right, 0, 0)


def against(left, right):
    return dot(left, right, 1, 1)


def norm_back(grad_normed, values, gain):
    scale_inv = lax.rsqrt(jnp.mean(values * values, axis=-1, keepdims=True) + EPS)
    normed = values * scale_inv
    grad_scaled = grad_normed * gain
    grad_values = scale_inv * (
        grad_scaled - normed * jnp.mean(grad_scaled * normed, axis=-1, keepdims=True)
    )
    grad_gain = jnp.sum(grad_normed * normed, axis=0)
    return (grad_values, grad_gain)


def turned(values, cosine, sine):
    lane = lax.broadcasted_iota(jnp.int32, values.shape, 1) % HEAD_DIM
    other = jnp.where(
        lane < HEAD_DIM // 2,
        pltpu.roll(values, 128 - HEAD_DIM // 2, 1),
        pltpu.roll(values, HEAD_DIM // 2, 1),
    )
    return values * cosine + other * sine


def project_kernel(width, x, gain, wq, wk, wv, first, cosine, sine, q_out, k_out, v_out, h_out):
    @pl.when(pl.program_id(0) == 0)
    def _():
        values = x[...].astype(F32)
        scale = lax.rsqrt(jnp.mean(values * values, axis=-1, keepdims=True) + EPS)
        h_out[...] = (values * scale * gain[...]).astype(BF16)

    hidden = h_out[...]
    cos, sin = cosine[...], sine[...]
    for weight, out, scale in ((wq, q_out, HEAD_DIM**-0.5), (wk, k_out, 1.0)):
        raw = dot(hidden, weight[...])
        for part in range(2):
            done = turned(raw[:, part * 128 : part * 128 + 128], cos, sin) * scale
            for piece in range(128 // width):
                out[part * (128 // width) + piece] = done[
                    :, piece * width : (piece + 1) * width
                ].astype(BF16)
    mixed = (0.5 * dot(hidden, wv[...]) + 0.5 * first[...].astype(F32)).astype(BF16)
    for piece in range(256 // width):
        v_out[piece] = mixed[:, piece * width : (piece + 1) * width]


def project(x, gain, wq, wk, wv, first, cosine, sine, parts):
    tokens, dim = x.shape
    width = dim // parts
    whole = lambda shape: pl.BlockSpec(shape, lambda g: (0,) * len(shape))
    cols = lambda rows: pl.BlockSpec((rows, 256), lambda g: (0, g))
    out = pl.BlockSpec((256 // width, tokens, width), lambda g: (g, 0, 0))
    split = jax.ShapeDtypeStruct((parts, tokens, width), BF16)
    return pl.pallas_call(
        functools.partial(project_kernel, width),
        grid=(dim // 256,),
        in_specs=[
            whole((tokens, dim)),
            whole((1, dim)),
            cols(dim),
            cols(dim),
            cols(dim),
            cols(tokens),
            whole((tokens, 128)),
            whole((tokens, 128)),
        ],
        out_specs=[out, out, out, whole((tokens, dim))],
        out_shape=[split, split, split, jax.ShapeDtypeStruct((tokens, dim), BF16)],
        compiler_params=pltpu.CompilerParams(vmem_limit_bytes=40 * MIB),
        cost_estimate=pl.CostEstimate(
            flops=6 * tokens * dim * dim, bytes_accessed=16 * tokens * dim, transcendentals=0
        ),
        name="project",
    )(x, gain, wq, wk, wv, first, cosine, sine)


def unproject_kernel(width, dq, dk, dv, cosine, sine, q_out, k_out, v_out, first_out):
    cos, sin = cosine[...], sine[...]
    for part in range(2):
        lanes = slice(part * 128, part * 128 + 128)
        picks = range(part * (128 // width), (part + 1) * (128 // width))
        join = lambda ref: jnp.concatenate([ref[p] for p in picks], axis=1).astype(F32)
        q_out[:, lanes] = turned(join(dq), cos, -sin).astype(BF16)
        k_out[:, lanes] = turned(join(dk), cos, -sin).astype(BF16)
        value = 0.5 * join(dv)
        first_out[:, lanes] = value
        v_out[:, lanes] = value.astype(BF16)


def unproject(dq, dk, dv, cosine, sine):
    parts, tokens, width = dq.shape
    dim = parts * width
    split = pl.BlockSpec((256 // width, tokens, width), lambda g: (g, 0, 0))
    table = pl.BlockSpec((tokens, 128), lambda g: (0, 0))
    cols = pl.BlockSpec((tokens, 256), lambda g: (0, g))
    low = jax.ShapeDtypeStruct((tokens, dim), BF16)
    return pl.pallas_call(
        functools.partial(unproject_kernel, width),
        grid=(dim // 256,),
        in_specs=[split, split, split, table, table],
        out_specs=[cols, cols, cols, cols],
        out_shape=[low, low, low, jax.ShapeDtypeStruct((tokens, dim), F32)],
        compiler_params=pltpu.CompilerParams(vmem_limit_bytes=40 * MIB),
        name="unproject",
    )(dq, dk, dv, cosine, sine)


def greet(parts, me):
    barrier = pltpu.get_barrier_semaphore()
    for step in range(1, parts):
        pl.semaphore_signal(
            barrier, 1, device_id={"seq": lax.rem(me + step, parts)}, device_id_type=MESH
        )
    pl.semaphore_wait(barrier, parts - 1)


def send(source, target, send_sem, recv_sem, peer):
    return pltpu.make_async_remote_copy(
        src_ref=source,
        dst_ref=target,
        send_sem=send_sem,
        recv_sem=recv_sem,
        device_id={"seq": peer},
        device_id_type=MESH,
    )


def arrive(ref, sem):
    pltpu.make_async_copy(ref, ref, sem).wait()


def own_head(values, head, width):
    if width == HEAD_DIM:
        return values
    lane = lax.broadcasted_iota(jnp.int32, values.shape, 1)
    return jnp.where(lane // HEAD_DIM == head, values, jnp.zeros_like(values))


def allowed_tile(i, j, tokens, start):
    key = j * tokens + lax.broadcasted_iota(jnp.int32, (tokens, tokens), 0)
    query = i * tokens + lax.broadcasted_iota(jnp.int32, (tokens, tokens), 1)
    return (key <= query) & (key >= start[i])


def forward_kernel(
    parts, heads,
    q_in, k_in, v_in, start,
    q_all, k_all, v_all, o_all, lse_all, attended,
    v_turn, q_own, best, total, accum, o_send,
    in_send, in_recv, o_out, o_in,
):
    _, tokens, width = q_in.shape
    me = lax.axis_index("seq")
    greet(parts, me)
    pairs = ((q_in, q_all), (k_in, k_all), (v_in, v_all))
    for index, (source, target) in enumerate(pairs):
        pltpu.make_async_copy(source.at[me], target.at[me], in_recv.at[index, me]).start()

    def start_step(step, _):
        peer = lax.rem(me + step, parts)
        for index, (source, target) in enumerate(pairs):
            send(
                source.at[peer], target.at[me],
                in_send.at[index, peer], in_recv.at[index, me], peer,
            ).start()
        return 0

    lax.fori_loop(1, parts, start_step, 0)

    def tile(i, j, masked):
        if masked:
            allowed = allowed_tile(i, j, tokens, start)
        for head in range(heads):
            rows = slice(head * HEAD_DIM, (head + 1) * HEAD_DIM)
            scores = against(k_all[j], q_own[head])
            if masked:
                scores = jnp.where(allowed, scores, NEG)
            old = best[head]
            new = jnp.maximum(old, jnp.max(scores, axis=0, keepdims=True))
            weights = jnp.exp(scores - new)
            factor = jnp.exp(old - new)
            best[head] = new
            total[head] = total[head] * factor + jnp.sum(weights, axis=0, keepdims=True)
            accum[rows] = accum[rows] * factor + dot(v_turn[j, rows], weights.astype(BF16))

    def query_block(i, _):
        for index, (_, target) in enumerate(pairs):
            arrive(target.at[i], in_recv.at[index, i])
        v_turn[i] = v_all[i].T
        for head in range(heads):
            q_own[head] = own_head(q_all[i], head, width)
        best[...] = jnp.full(best.shape, NEG, F32)
        total[...] = jnp.zeros(total.shape, F32)
        accum[...] = jnp.zeros(accum.shape, F32)

        def key_block(j, _):
            masked = (j == 0) | (j == i) | (i == parts - 1)

            @pl.when(masked)
            def _():
                tile(i, j, True)

            @pl.when(jnp.logical_not(masked))
            def _():
                tile(i, j, False)

            return 0

        lax.fori_loop(0, i + 1, key_block, 0)
        for head in range(heads):
            rows = slice(head * HEAD_DIM, (head + 1) * HEAD_DIM)
            o_all[i, rows] = accum[rows] / total[head]
            lse_all[i, head] = best[head] + jnp.log(total[head])
        o_send[i] = o_all[i].T.astype(BF16)

        @pl.when(i == me)
        def _():
            pltpu.make_async_copy(o_send.at[i], attended.at[me], o_in.at[me]).start()

        @pl.when(i != me)
        def _():
            send(o_send.at[i], attended.at[me], o_out.at[i], o_in.at[me], i).start()

        return 0

    lax.fori_loop(0, parts, query_block, 0)

    def finish(step, _):
        peer = lax.rem(me + step, parts)
        for index, (source, _) in enumerate(pairs):
            arrive(source.at[peer], in_send.at[index, peer])
        arrive(o_send.at[peer], o_out.at[peer])
        arrive(attended.at[peer], o_in.at[peer])
        return 0

    lax.fori_loop(1, parts, finish, 0)
    arrive(attended.at[me], o_in.at[me])


def attend(q, k, v, start):
    parts, tokens, width = q.shape
    heads = width // HEAD_DIM
    whole = pl.BlockSpec(memory_space=VMEM)
    split = jax.ShapeDtypeStruct(q.shape, BF16)
    flops = 4 * parts * parts * tokens * tokens * width // 2
    return pl.pallas_call(
        functools.partial(forward_kernel, parts, heads),
        in_specs=[whole] * 4,
        out_specs=[whole] * 6,
        out_shape=[
            split,
            split,
            split,
            jax.ShapeDtypeStruct((parts, width, tokens), F32),
            jax.ShapeDtypeStruct((parts, heads, 1, tokens), F32),
            split,
        ],
        scratch_shapes=[
            VMEM((parts, width, tokens), BF16),
            VMEM((heads, tokens, width), BF16),
            VMEM((heads, 1, tokens), F32),
            VMEM((heads, 1, tokens), F32),
            VMEM((width, tokens), F32),
            VMEM((parts, tokens, width), BF16),
            pltpu.SemaphoreType.DMA((3, parts)),
            pltpu.SemaphoreType.DMA((3, parts)),
            pltpu.SemaphoreType.DMA((parts,)),
            pltpu.SemaphoreType.DMA((parts,)),
        ],
        compiler_params=pltpu.CompilerParams(
            collective_id=1, has_side_effects=True, vmem_limit_bytes=48 * MIB
        ),
        cost_estimate=pl.CostEstimate(
            flops=4 * flops, bytes_accessed=16 * q.size, transcendentals=flops // 256
        ),
        name="attend",
    )(q, k, v, start)


def backward_kernel(
    parts, heads,
    d_in, q_all, k_all, v_all, o_all, lse_all, start,
    dq_got, dk_got, dv_got,
    d_all, q_own, d_own, k_turn, delta, dq_turn, dk_sum, dv_sum, dq_send, dk_send, dv_send,
    in_send, in_recv, out_send, out_recv,
):
    _, tokens, width = d_in.shape
    me = lax.axis_index("seq")
    greet(parts, me)
    pltpu.make_async_copy(d_in.at[me], d_all.at[me], in_recv.at[me]).start()

    def start_step(step, _):
        peer = lax.rem(me + step, parts)
        send(d_in.at[peer], d_all.at[me], in_send.at[peer], in_recv.at[me], peer).start()
        return 0

    lax.fori_loop(1, parts, start_step, 0)
    sends = ((dq_send, dq_got), (dk_send, dk_got), (dv_send, dv_got))

    def give(index, block):
        source, target = sends[index]

        @pl.when(block == me)
        def _():
            pltpu.make_async_copy(
                source.at[block], target.at[me], out_recv.at[index, me]
            ).start()

        @pl.when(block != me)
        def _():
            send(
                source.at[block], target.at[me],
                out_send.at[index, block], out_recv.at[index, me], block,
            ).start()

    def tile(i, j, masked):
        if masked:
            allowed = allowed_tile(i, j, tokens, start)
        for head in range(heads):
            rows = slice(head * HEAD_DIM, (head + 1) * HEAD_DIM)
            query, grad = q_own[head, i], d_own[head, i]
            scores = against(k_all[j], query)
            if masked:
                scores = jnp.where(allowed, scores, NEG)
            weights = jnp.exp(scores - lse_all[i, head])
            dv_sum[...] += dot(weights.astype(BF16), grad)
            slope = against(v_all[j], grad) - delta[i, head]
            d_scores = (weights * slope).astype(BF16)
            dk_sum[...] += dot(d_scores, query)
            dq_turn[i, rows] += dot(k_turn[j, rows], d_scores)

    dq_turn[...] = jnp.zeros(dq_turn.shape, F32)

    def key_block(step, _):
        j = parts - 1 - step
        arrive(d_all.at[j], in_recv.at[j])
        got = d_all[j]
        product = got.astype(F32).T * o_all[j]
        for head in range(heads):
            rows = slice(head * HEAD_DIM, (head + 1) * HEAD_DIM)
            delta[j, head] = jnp.sum(product[rows], axis=0, keepdims=True)
            q_own[head, j] = own_head(q_all[j], head, width)
            d_own[head, j] = own_head(got, head, width)
        k_turn[j] = k_all[j].T
        dk_sum[...] = jnp.zeros(dk_sum.shape, F32)
        dv_sum[...] = jnp.zeros(dv_sum.shape, F32)

        def query_block(i, _):
            masked = (j == 0) | (j == i) | (i == parts - 1)

            @pl.when(masked)
            def _():
                tile(i, j, True)

            @pl.when(jnp.logical_not(masked))
            def _():
                tile(i, j, False)

            @pl.when(j == 0)
            def _():
                dq_send[i] = (dq_turn[i] * HEAD_DIM**-0.5).T.astype(BF16)
                give(0, i)

            return 0

        lax.fori_loop(j, parts, query_block, 0)
        dk_send[j] = dk_sum[...].astype(BF16)
        dv_send[j] = dv_sum[...].astype(BF16)
        give(1, j)
        give(2, j)
        return 0

    lax.fori_loop(0, parts, key_block, 0)

    def finish(step, _):
        peer = lax.rem(me + step, parts)
        arrive(d_in.at[peer], in_send.at[peer])
        for index, (source, target) in enumerate(sends):
            arrive(source.at[peer], out_send.at[index, peer])
            arrive(target.at[peer], out_recv.at[index, peer])
        return 0

    lax.fori_loop(1, parts, finish, 0)
    for index, (_, target) in enumerate(sends):
        arrive(target.at[me], out_recv.at[index, me])


def attend_back(d_att, q, k, v, o, lse, start):
    parts, tokens, width = q.shape
    heads = width // HEAD_DIM
    whole = pl.BlockSpec(memory_space=VMEM)
    split = jax.ShapeDtypeStruct(q.shape, BF16)
    flops = 10 * parts * parts * tokens * tokens * width // 2
    return pl.pallas_call(
        functools.partial(backward_kernel, parts, heads),
        in_specs=[whole] * 7,
        out_specs=[whole] * 3,
        out_shape=[split] * 3,
        scratch_shapes=[
            VMEM((parts, tokens, width), BF16),
            VMEM((heads, parts, tokens, width), BF16),
            VMEM((heads, parts, tokens, width), BF16),
            VMEM((parts, width, tokens), BF16),
            VMEM((parts, heads, 1, tokens), F32),
            VMEM((parts, width, tokens), F32),
            VMEM((tokens, width), F32),
            VMEM((tokens, width), F32),
            VMEM((parts, tokens, width), BF16),
            VMEM((parts, tokens, width), BF16),
            VMEM((parts, tokens, width), BF16),
            pltpu.SemaphoreType.DMA((parts,)),
            pltpu.SemaphoreType.DMA((parts,)),
            pltpu.SemaphoreType.DMA((3, parts)),
            pltpu.SemaphoreType.DMA((3, parts)),
        ],
        compiler_params=pltpu.CompilerParams(
            collective_id=2, has_side_effects=True, vmem_limit_bytes=48 * MIB
        ),
        cost_estimate=pl.CostEstimate(
            flops=4 * flops, bytes_accessed=20 * q.size, transcendentals=flops // 640
        ),
        name="attend_back",
    )(d_att, q, k, v, o, lse, start)


def shards(
    inputs, first_values, lengths, w_query, w_key, w_value, w_out, gain_attn,
    w_gate, w_up, w_down, gain_mlp, cotangent,
):
    row_count, tokens, width = inputs.shape
    assert row_count == 1
    parts = lax.axis_size("seq")
    rank = lax.axis_index("seq")
    both = ("dp", "seq")
    gather = lambda value: lax.all_gather(value, both, axis=0, tiled=True)

    qkv = gather(jnp.concatenate([w_query, w_key, w_value], axis=1))
    gains = gather(jnp.stack([gain_attn, gain_mlp], axis=1)).astype(F32)
    gain_one, gain_two = gains[:, 0], gains[:, 1]
    rest = gather(jnp.concatenate([w_out, w_gate, w_up], axis=1))
    down_full = gather(w_down)
    hidden_size = w_gate.shape[1]
    query_full, key_full, value_full = (qkv[:, n * width : (n + 1) * width] for n in range(3))
    out_full = rest[:, :width]
    gate_full = rest[:, width : width + hidden_size]
    up_full = rest[:, width + hidden_size :]

    ends = jnp.cumsum(lengths[0])
    begins = ends - lengths[0]
    time = jnp.arange(tokens * parts, dtype=jnp.int32)
    inside = (time[:, None] >= begins[None, :]) & (time[:, None] < ends[None, :])
    start_all = jnp.sum(jnp.where(inside, begins[None, :], 0), axis=1)
    own_start = lax.dynamic_slice_in_dim(start_all, rank * tokens, tokens)
    position = (rank * tokens + jnp.arange(tokens, dtype=jnp.int32) - own_start).astype(F32)
    half = HEAD_DIM // 2
    angles = position[:, None] * THETA ** (-jnp.arange(half, dtype=F32) * 2.0 / HEAD_DIM)
    cosine = jnp.tile(jnp.cos(angles), (1, 4))
    sine = jnp.sin(angles)
    sine = jnp.tile(jnp.concatenate([-sine, sine], axis=1), (1, 2))
    start = start_all.reshape(parts, 1, tokens)

    x_low = inputs.reshape(tokens, width)
    q, k, v, hidden_in = project(
        x_low, gain_one[None], query_full, key_full, value_full,
        first_values.reshape(tokens, width), cosine, sine, parts,
    )
    q_all, k_all, v_all, o_all, lse_all, attended = attend(q, k, v, start)
    attended = attended.transpose(1, 0, 2).reshape(tokens, width)

    x_in = x_low.astype(F32)
    middle = x_in + dot(attended, out_full)
    scale = lax.rsqrt(jnp.mean(middle * middle, axis=-1, keepdims=True) + EPS)
    hidden_mlp = (middle * scale * gain_two).astype(BF16)
    gate = dot(hidden_mlp, gate_full)
    upward = dot(hidden_mlp, up_full)
    sigma = jax.nn.sigmoid(gate)
    silu_gate = gate * sigma
    inner = (silu_gate * upward).astype(BF16)
    output = (middle + dot(inner, down_full)).astype(BF16).reshape(inputs.shape)
    grad_y = cotangent.reshape(tokens, width)
    grad_down = across(inner, grad_y)
    grad_inner = against(grad_y, down_full)
    grad_gate_low = (grad_inner * upward * sigma * (1.0 + gate * (1.0 - sigma))).astype(BF16)
    grad_up_low = (grad_inner * silu_gate).astype(BF16)
    grad_gate = across(hidden_mlp, grad_gate_low)
    grad_up = across(hidden_mlp, grad_up_low)
    grad_hidden_mlp = against(grad_gate_low, gate_full) + against(grad_up_low, up_full)
    grad_middle, grad_gain_two = norm_back(grad_hidden_mlp, middle, gain_two)
    grad_middle = grad_middle + grad_y.astype(F32)
    grad_branch = grad_middle.astype(BF16)
    grad_out = across(attended, grad_branch)
    d_att = against(grad_branch, out_full).astype(BF16)
    d_att = d_att.reshape(tokens, parts, width // parts).transpose(1, 0, 2)

    dq, dk, dv = attend_back(d_att, q_all, k_all, v_all, o_all, lse_all, start)
    dq, dk, dv, grad_first = unproject(dq, dk, dv, cosine, sine)
    grad_query_w = across(hidden_in, dq)
    grad_key_w = across(hidden_in, dk)
    grad_value_w = across(hidden_in, dv)
    grad_hidden_in = against(dq, query_full) + against(dk, key_full) + against(dv, value_full)
    grad_x, grad_gain_one = norm_back(grad_hidden_in, x_in, gain_one)
    grad_x = grad_x + grad_middle
    scatter = lambda value: lax.psum_scatter(value, both, scatter_dimension=0, tiled=True)
    return (
        output,
        grad_x.reshape(inputs.shape),
        grad_first.reshape(inputs.shape),
        scatter(grad_query_w),
        scatter(grad_key_w),
        scatter(grad_value_w),
        scatter(grad_out),
        scatter(grad_gain_one),
        scatter(grad_gate),
        scatter(grad_up),
        scatter(grad_down),
        scatter(grad_gain_two),
    )


def solution(mesh):
    tokens = P("dp", "seq", None)
    matrix = P(("dp", "seq"), None)
    vector = P(("dp", "seq"))
    return jax.shard_map(
        shards,
        mesh=mesh,
        in_specs=(
            tokens, tokens, P("dp", None), matrix, matrix, matrix, matrix, vector,
            matrix, matrix, matrix, vector, tokens,
        ),
        out_specs=(
            tokens, tokens, tokens, matrix, matrix, matrix, matrix, vector,
            matrix, matrix, matrix, vector,
        ),
        check_vma=False,
    )
```

time: 3190 us -> 1850 us (0.58)
  starting transfers between devices: 666 us -> 0.58 us
  waiting for transfers between devices: 1970 us -> 1320 us
  Pallas kernels: 0 us -> 253 us
  other arithmetic: 131 us -> 10.8 us
  local copies, waits for them, and re-layouts: 90.4 us -> 29.8 us
  matrix products: 153 us -> 101 us
    ppermute x46 -> x0, starting transfers between devices: 666 us -> none  [the longest x30 481 us: passed_along_2(): lax.ppermute(value, axis, [(source, source + steps) for source in range(i...]
    ppermute x46 -> x0, waiting for transfers between devices: 628 us -> none  [the longest x16 398 us: passed_along(): return lax.ppermute(value, axis, pairs)]
    pallas_call x0 -> x4, Pallas kernels: none -> 253 us  [the longest x1 128 us: attend_back(): pl.pallas_call(functools.partial(backward_kernel, parts, heads), in_specs...]
    convert_element_type x40 -> x3, other arithmetic: 97.5 us -> 0.33 us  [the longest x1 0.24 us: shards(): hidden_mlp = (middle * scale * gain_two).astype(BF16)]
    unnamed x2 -> x1, blocking collectives: 131 us -> 38.8 us
    all_gather x0 -> x1, blocking collectives: none -> 69.7 us  [shards(): gather = lambda value: lax.all_gather(value, both, axis=0, tiled=True)]
    dot_general x28 -> x18, matrix products: 153 us -> 101 us  [dot(): lax.dot_general(left, right, (((left_dim,), (right_dim,)), ((), ())), pre...]
    while x48 -> x0, local copies, waits for them, and re-layouts: 44.4 us -> none
  transfers between devices with their start and end apart: 60 -> 10, of which waited for: 39 -> 9; matrix products, arithmetic and copies ran while one was open for 7% -> 4% of each run, Pallas kernels for 0% -> 7%
where the time goes in v1:
time: 1850 us; the launch traced here: 1840 us
  waiting for transfers between devices  1320 us (71%)
  Pallas kernels  253 us (14%)
  blocking collectives  109 us (6%)
  matrix products  101 us (5%)
  local copies, waits for them, and re-layouts  29.8 us (2%)
    reduce_scatter x7, waiting for transfers between devices, shards(): lax.psum_scatter(value, both, scatter_dimension=0, tiled=True)  1220 us
    pallas_call x1, Pallas kernels, attend_back(): pl.pallas_call(functools.partial(backward_kernel, parts, heads), in_specs...  128 us
    pallas_call x1, Pallas kernels, attend(): pl.pallas_call(functools.partial(forward_kernel, parts, heads), in_specs=...  115 us
    dot_general x18, matrix products, dot(): lax.dot_general(left, right, (((left_dim,), (right_dim,)), ((), ())), pre...  101 us
    all_gather x3, waiting for transfers between devices, shards(): gather = lambda value: lax.all_gather(value, both, axis=0, tiled=True)  99.5 us
    all_gather x1, blocking collectives, shards(): gather = lambda value: lax.all_gather(value, both, axis=0, tiled=True)  69.7 us
    unnamed x1, blocking collectives  38.8 us
  transfers between devices with their start and end apart: 10, of which 9 were waited for; matrix products, arithmetic and copies ran while one was open for 4% of the time, Pallas kernels for 7%

profile of v1, /device:TPU:0, one launch (start us, length us, event | category | flops | bytes accessed | tf_op | source)
XLA Modules:
  0.0 1841.8 jit_solution(7771957997323088684)
XLA Ops:
  13.9 69.7 %all-gather = bf16[32,32,2]{1,2,0:T(2,128)(2,1)S(1)} all-gather(bf16[1,32,2]{1,2,0:T(2,128)(2,1)S(1)} %maximum_bitcast_fusion), channel_id=1, replica_groups=mesh['dp'=4,'seq'=8] {'dp','seq'}, dimensions={0}, use_global_device_ids=true | all-gather | bytes 4224 | tf_op jit(solution)/shard_map/all_gather | solution.py:466
  84.3 7.6 fusion.34
  91.9 61.1 %all-gather.5.cloned.1.call-done = bf16[1024,3072]{1,0:T(8,128)(2,1)} async-done(((bf16[32,3072]{1,0:T(8,128)(2,1)}), bf16[1024,3072]{1,0:T(8,128)(2,1)}) %all-gather.5.cloned.1.call-update) | async-done | bytes 6291472 | tf_op jit(solution)/shard_map/all_gather | solution.py:466
  153.0 3.7 fusion.47
  156.7 6.2 project.1
  164.9 115.4 %attend.1 = (bf16[8,512,128]{2,1,0:T(8,128)(2,1)S(1)}, bf16[8,512,128]{2,1,0:T(8,128)(2,1)S(1)}, bf16[8,512,128]{2,1,0:T(8,128)(2,1)S(1)}, f32[8,128,512]{2,1,0:...) custom-call(bf16[8,512,128]{2,1,0:T(8,128)(2,1)S(1)} %get-tuple-element.29.q_in, ...), custom_call_target="tpu_custom_call" | custom-call | flops 17179869184 | bytes 8388608 | tf_op jit(solution)/shard_map/attend/pallas_call | solution.py:277
  286.5 38.4 %all-gather.7.cloned.1.call-done = bf16[1024,6656]{1,0:T(8,128)(2,1)} async-done(((bf16[32,6656]{1,0:T(8,128)(2,1)}), bf16[1024,6656]{1,0:T(8,128)(2,1)}) %all-gather.7.cloned.1.call-update) | async-done | bytes 13631504 | tf_op jit(solution)/shard_map/all_gather | solution.py:466
  324.9 3.3 multiply_reduce_fusion.2
  328.5 8.8 fusion.3
  337.5 10.4 multiply_convert_fusion.1
  347.9 4.5 fusion.1
  352.4 6.0 multiply_reduce_fusion
  369.7 127.8 %attend_back.1 = (bf16[8,512,128]{2,1,0:T(8,128)(2,1)S(1)}, bf16[8,512,128]{2,1,0:T(8,128)(2,1)S(1)}, bf16[8,512,128]{2,1,0:T(8,128)(2,1)S(1)}) custom-call(bf16[8,512,128]{2,1,0:T(8,128)(2,1)S(1)} %bitcast.67, bf16[8,512,128]{2,1,0:T(8,128)(2,1)S(1)} %copy-done.13, bf16[8,512,128]{2,1,0:T(8,128)(2,1)} %copy-done.14, bf16[8,512,128]{2,1,0:T(8,128)(2,1)} %copy-done.15, ...), custom_call_target="tpu_custom_call" | custom-call | flops 42949672960 | bytes 10485760 | tf_op jit(solution)/shard_map/attend_back/pallas_call | solution.py:425
  497.5 3.5 unproject.1
  503.9 3.3 fusion.50
  507.5 4.6 fusion.51
  512.1 4.5 fusion.49
  517.8 4.8 fusion.36
  523.9 7.7 fusion.52
  531.7 7.7 fusion.53
  540.7 7.8 fusion.32
  555.7 4.7 fusion.17
  560.4 38.8 %all-reduce.2 = (f32[1024]{0:T(1024)S(1)}, f32[1024]{0:T(1024)S(1)}) all-reduce(f32[1024]{0:T(1024)S(1)} %get-tuple-element.48, f32[1024]{0:T(1024)S(1)} %get-tuple-element.46), channel_id=6, replica_groups=mesh['dp'=4,'seq'=8] {'dp','seq'}, use_global_device_ids=true, to_apply=%region_11.12.clone | all-reduce | flops 2048 | bytes 16384
  600.4 4.2 fusion.16
  604.7 6.8 fusion.31
  611.4 38.4 %reduce-scatter.10.cloned.1.call-done = f32[32,1024]{1,0:T(8,128)} async-done(((f32[1024,1024]{1,0:T(8,128)}), f32[32,1024]{1,0:T(8,128)}) %reduce-scatter.10.cloned.1.call-update) | async-done | bytes 131088 | tf_op jit(solution)/shard_map/reduce_scatter | solution.py:534
  649.8 144.0 %reduce-scatter.12.cloned.1.call-done = f32[32,1024]{1,0:T(8,128)} async-done(((f32[1024,1024]{1,0:T(8,128)}), f32[32,1024]{1,0:T(8,128)}) %reduce-scatter.12.cloned.1.call-update) | async-done | bytes 131088 | tf_op jit(solution)/shard_map/reduce_scatter | solution.py:534
  793.8 144.0 %reduce-scatter.8.cloned.1.call-done = f32[32,1024]{1,0:T(8,128)} async-done(((f32[1024,1024]{1,0:T(8,128)}), f32[32,1024]{1,0:T(8,128)}) %reduce-scatter.8.cloned.1.call-update) | async-done | bytes 131088 | tf_op jit(solution)/shard_map/reduce_scatter | solution.py:534
  937.8 144.7 %reduce-scatter.14.cloned.1.call-done = f32[32,1024]{1,0:T(8,128)} async-done(((f32[1024,1024]{1,0:T(8,128)}), f32[32,1024]{1,0:T(8,128)}) %reduce-scatter.14.cloned.1.call-update) | async-done | bytes 131088 | tf_op jit(solution)/shard_map/reduce_scatter | solution.py:534
  1082.5 250.1 %reduce-scatter.16.cloned.1.call-done = f32[32,2816]{1,0:T(8,128)} async-done(((f32[1024,2816]{1,0:T(8,128)}), f32[32,2816]{1,0:T(8,128)}) %reduce-scatter.16.cloned.1.call-update) | async-done | bytes 360464 | tf_op jit(solution)/shard_map/reduce_scatter | solution.py:534
  1332.6 250.7 %reduce-scatter.18.cloned.1.call-done = f32[32,2816]{1,0:T(8,128)} async-done(((f32[1024,2816]{1,0:T(8,128)}), f32[32,2816]{1,0:T(8,128)}) %reduce-scatter.18.cloned.1.call-update) | async-done | bytes 360464 | tf_op jit(solution)/shard_map/reduce_scatter | solution.py:534
  1583.3 251.4 %reduce-scatter.20.cloned.1.call-done = f32[88,1024]{1,0:T(8,128)} async-done(((f32[2816,1024]{1,0:T(8,128)}), f32[88,1024]{1,0:T(8,128)}) %reduce-scatter.20.cloned.1.call-update) | async-done | bytes 360464 | tf_op jit(solution)/shard_map/reduce_scatter | solution.py:534
  (122 shorter events, 42.3 us)
Async XLA Ops:
  7.2 6.7 copy-start.27
  7.2 6.7 copy-start.26
  7.2 77.1 %copy-start.22 = (bf16[1,512,1024]{2,1,0:T(8,128)(2,1)S(1)}, bf16[1,512,1024]{2,1,0:T(8,128)(2,1)}, u32[]{:S(2)}) copy-start(bf16[1,512,1024]{2,1,0:T(8,128)(2,1)} %param.25) | copy-start | bytes 3145732
  7.2 77.1 %all-gather.9.cloned.1.call-start = ((), (), s32[]{:S(2)}) async-start(), calls=%async_computation.9 | async-start | bytes 5947392 | tf_op jit(solution)/shard_map/all_gather | solution.py:466
  7.9 145.1 %all-gather.5.cloned.1.call-start = ((), (), s32[]{:S(2)}) async-start(), calls=%async_computation.7 | async-start | bytes 6488064 | tf_op jit(solution)/shard_map/all_gather | solution.py:466
  9.6 315.3 %all-gather.7.cloned.1.call-start = ((), (), s32[]{:S(2)}) async-start(), calls=%async_computation.8 | async-start | bytes 14057472 | tf_op jit(solution)/shard_map/all_gather | solution.py:466
  11.5 638.3 %reduce-scatter.10.cloned.1.call-start = ((), (), s32[]{:S(2)}) async-start(), calls=%async_computation.11 | async-start | bytes 4325376 | tf_op jit(solution)/shard_map/reduce_scatter | solution.py:534
  91.9 64.8 %copy-start = (bf16[1,512,1024]{2,1,0:T(8,128)(2,1)S(1)}, bf16[1,512,1024]{2,1,0:T(8,128)(2,1)}, u32[]{:S(2)}) copy-start(bf16[1,512,1024]{2,1,0:T(8,128)(2,1)} %param.13) | copy-start | bytes 3145732
  153.0 3.7 copy-start.9
  328.2 30.3 %copy-start.17 = (f32[512,1024]{1,0:T(8,128)}, f32[512,1024]{1,0:T(8,128)S(1)}, u32[]{:S(2)}) copy-start(f32[512,1024]{1,0:T(8,128)S(1)} %get-tuple-element.65) | copy-start | bytes 6291460
  328.2 9.1 slice-start
  328.4 8.9 copy-start.20
  328.4 8.9 slice-start.1
  328.5 8.8 slice-start.2
  328.5 9.0 slice-start.3
  347.9 4.5 copy-start.28
  352.4 6.0 copy-start.23
  359.1 1.3 copy-start.16
  507.3 286.5 %reduce-scatter.12.cloned.1.call-start = ((), (), s32[]{:S(2)}) async-start(), calls=%async_computation.12 | async-start | bytes 4325376 | tf_op jit(solution)/shard_map/reduce_scatter | solution.py:534
  512.1 425.7 %reduce-scatter.8.cloned.1.call-start = ((), (), s32[]{:S(2)}) async-start(), calls=%async_computation.10 | async-start | bytes 4325376 | tf_op jit(solution)/shard_map/reduce_scatter | solution.py:534
  516.6 565.9 %reduce-scatter.14.cloned.1.call-start = ((), (), s32[]{:S(2)}) async-start(), calls=%async_computation.13 | async-start | bytes 4325376 | tf_op jit(solution)/shard_map/reduce_scatter | solution.py:534
  522.7 1.2 copy-start.21
  522.7 809.9 %reduce-scatter.16.cloned.1.call-start = ((), (), s32[]{:S(2)}) async-start(), calls=%async_computation.14 | async-start | bytes 11894784 | tf_op jit(solution)/shard_map/reduce_scatter | solution.py:534
  531.7 1051.7 %reduce-scatter.18.cloned.1.call-start = ((), (), s32[]{:S(2)}) async-start(), calls=%async_computation.15 | async-start | bytes 11894784 | tf_op jit(solution)/shard_map/reduce_scatter | solution.py:534
  539.4 1.2 copy-start.24
  539.5 1295.3 %reduce-scatter.20.cloned.1.call-start = ((), (), s32[]{:S(2)}) async-start(), calls=%async_computation.16 | async-start | bytes 11894784 | tf_op jit(solution)/shard_map/reduce_scatter | solution.py:534
  548.5 1.2 copy-start.8
  549.7 3.0 copy-start.6
  552.7 3.0 copy-start.4
  552.7 3.0 copy-start.25
  600.4 4.2 copy-start.18
  600.4 4.2 copy-start.29
  (12 other events, 12.5 us)
Sparse Core Ops, SparseCore 0:
  11.0 69.9 all-gather.8
  84.4 68.5 all-gather.4
  156.5 168.3 all-gather.6
  507.4 142.3 reduce-scatter.9
  652.5 141.2 reduce-scatter.11
  796.5 141.2 reduce-scatter.7
  940.6 141.8 reduce-scatter.13
  1085.4 247.2 reduce-scatter.15
  1335.5 247.7 reduce-scatter.17
  1586.1 248.6 reduce-scatter.19

commit v2 on v1

--- a/solution.py
+++ b/solution.py
@@ -142,7 +142,7 @@
         pl.semaphore_signal(
             barrier, 1, device_id={"seq": lax.rem(me + step, parts)}, device_id_type=MESH
         )
-    pl.semaphore_wait(barrier, parts - 1)
+    return parts - 1
 
 
 def send(source, target, send_sem, recv_sem, peer):
@@ -174,92 +174,165 @@
 
 
 def forward_kernel(
-    parts, heads,
-    q_in, k_in, v_in, start,
-    q_all, k_all, v_all, o_all, lse_all, attended,
-    v_turn, q_own, best, total, accum, o_send,
-    in_send, in_recv, o_out, o_in,
+    parts, heads, plan, count,
+    q_in, k_in, v_in, start, *refs,
 ):
+    late, ready = refs[:1], refs[1:count]
+    q_all, k_all, v_all, o_all, lse_all, attended = refs[count : count + 6]
+    fulls = refs[count + 6 : 2 * count + 6]
+    late_held = refs[2 * count + 6]
+    v_turn, total, o_send, in_send, in_recv, o_out, o_in, *sems = refs[2 * count + 7 :]
+    place = Place()
     _, tokens, width = q_in.shape
+    half = parts // 2
     me = lax.axis_index("seq")
-    greet(parts, me)
+    own = me // half
+    place.greet(greet(parts, me))
+    spread = WeightSpread(place, plan, late, late_held, ready, fulls, sems)
     pairs = ((q_in, q_all), (k_in, k_all), (v_in, v_all))
+
+    def moved(index, peer):
+        source, target = pairs[index]
+        return send(
+            source.at[peer], target.at[me], in_send.at[index, peer], in_recv.at[index, me], peer
+        )
+
+    def over(first, action):
+        def body(step, _):
+            action(first + lax.rem(me + step, half))
+            return 0
+
+        lax.fori_loop(0, half, body, 0)
+
+    def start_cross(indices):
+        over((1 - own) * half, lambda peer: [moved(index, peer).start() for index in indices])
+
+    def sent_cross(indices):
+        over((1 - own) * half, lambda peer: [moved(index, peer).wait_send() for index in indices])
+
     for index, (source, target) in enumerate(pairs):
         pltpu.make_async_copy(source.at[me], target.at[me], in_recv.at[index, me]).start()
-
-    def start_step(step, _):
-        peer = lax.rem(me + step, parts)
-        for index, (source, target) in enumerate(pairs):
-            send(
-                source.at[peer], target.at[me],
-                in_send.at[index, peer], in_recv.at[index, me], peer,
-            ).start()
-        return 0
-
-    lax.fori_loop(1, parts, start_step, 0)
+    pl.when(own == 0)(lambda: start_cross((1, 2)))
+    pl.when(own == 1)(lambda: start_cross((0,)))
+
+    def start_near(peer):
+        @pl.when(peer != me)
+        def _():
+            for index in range(3):
+                moved(index, peer).start()
+
+    over(own * half, start_near)
+
+    def got(index, block):
+        arrive(pairs[index][1].at[block], in_recv.at[index, block])
+
+    def got_keys(block):
+        got(1, block)
+        got(2, block)
+        v_turn[block] = v_all[block].T
 
     def tile(i, j, masked):
         if masked:
             allowed = allowed_tile(i, j, tokens, start)
+        queries, keys = q_all[i], k_all[j]
         for head in range(heads):
             rows = slice(head * HEAD_DIM, (head + 1) * HEAD_DIM)
-            scores = against(k_all[j], q_own[head])
+            scores = against(keys, own_head(queries, head, width))
             if masked:
                 scores = jnp.where(allowed, scores, NEG)
-            old = best[head]
+            old = lse_all[i, head]
             new = jnp.maximum(old, jnp.max(scores, axis=0, keepdims=True))
             weights = jnp.exp(scores - new)
             factor = jnp.exp(old - new)
-            best[head] = new
-            total[head] = total[head] * factor + jnp.sum(weights, axis=0, keepdims=True)
-            accum[rows] = accum[rows] * factor + dot(v_turn[j, rows], weights.astype(BF16))
-
-    def query_block(i, _):
-        for index, (_, target) in enumerate(pairs):
-            arrive(target.at[i], in_recv.at[index, i])
-        v_turn[i] = v_all[i].T
-        for head in range(heads):
-            q_own[head] = own_head(q_all[i], head, width)
-        best[...] = jnp.full(best.shape, NEG, F32)
-        total[...] = jnp.zeros(total.shape, F32)
-        accum[...] = jnp.zeros(accum.shape, F32)
+            lse_all[i, head] = new
+            total[i, head] = total[i, head] * factor + jnp.sum(weights, axis=0, keepdims=True)
+            o_all[i, rows] = o_all[i, rows] * factor + dot(
+                v_turn[j, rows], weights.astype(BF16)
+            )
+
+    def tile_row(row, _):
+        phase, place_in = row // half, lax.rem(row, half)
+        lower = jnp.where(phase == 0, own, 1 - own) * half
+        i = jnp.where(phase == 1, half, lower) + place_in
+        first = jnp.where(phase == 1, 0, lower)
+        last = jnp.where(phase == 1, half, i + 1)
+        spread.at_row(row, 3 * half)
+
+        @pl.when(phase == 0)
+        def _():
+            got(0, i)
+            got_keys(i)
+
+        @pl.when((row == half) & (own == 0))
+        def _():
+            lax.fori_loop(half, parts, lambda block, _: got(0, block) or 0, 0)
+
+        @pl.when((row == half) & (own == 1))
+        def _():
+            sent_cross((0,))
+            start_cross((1, 2))
+            lax.fori_loop(0, half, lambda block, _: got_keys(block) or 0, 0)
+
+        @pl.when((row == 2 * half) & (own == 0))
+        def _():
+            sent_cross((1, 2))
+            start_cross((0,))
+
+        @pl.when((phase == 2) & (own == 0))
+        def _():
+            got_keys(i)
+
+        @pl.when((phase == 2) & (own == 1))
+        def _():
+            got(0, i)
+
+        @pl.when((phase == 0) | ((phase == 1) & (own == 0)) | ((phase == 2) & (own == 1)))
+        def _():
+            lse_all[i] = jnp.full(lse_all.shape[1:], NEG, F32)
+            total[i] = jnp.zeros(total.shape[1:], F32)
+            o_all[i] = jnp.zeros(o_all.shape[1:], F32)
 
         def key_block(j, _):
             masked = (j == 0) | (j == i) | (i == parts - 1)
-
-            @pl.when(masked)
+            pl.when(masked)(lambda: tile(i, j, True))
+            pl.when(jnp.logical_not(masked))(lambda: tile(i, j, False))
+            return 0
+
+        lax.fori_loop(first, last, key_block, 0)
+
+        @pl.when(((phase == 0) & (own == 0)) | ((phase == 1) & (own == 1)) | (phase == 2))
+        def _():
+            for head in range(heads):
+                rows = slice(head * HEAD_DIM, (head + 1) * HEAD_DIM)
+                o_all[i, rows] = o_all[i, rows] / total[i, head]
+                lse_all[i, head] = lse_all[i, head] + jnp.log(total[i, head])
+            o_send[i] = o_all[i].T.astype(BF16)
+
+            @pl.when(i == me)
             def _():
-                tile(i, j, True)
-
-            @pl.when(jnp.logical_not(masked))
+                pltpu.make_async_copy(o_send.at[i], attended.at[me], o_in.at[me]).start()
+
+            @pl.when(i != me)
             def _():
-                tile(i, j, False)
-
-            return 0
-
-        lax.fori_loop(0, i + 1, key_block, 0)
-        for head in range(heads):
-            rows = slice(head * HEAD_DIM, (head + 1) * HEAD_DIM)
-            o_all[i, rows] = accum[rows] / total[head]
-            lse_all[i, head] = best[head] + jnp.log(total[head])
-        o_send[i] = o_all[i].T.astype(BF16)
-
-        @pl.when(i == me)
+                send(o_send.at[i], attended.at[me], o_out.at[i], o_in.at[me], i).start()
+
+        return 0
+
+    lax.fori_loop(0, 3 * half, tile_row, 0)
+    spread.finish()
+    pl.when(own == 0)(lambda: sent_cross((0,)))
+    pl.when(own == 1)(lambda: sent_cross((1, 2)))
+
+    def sent_near(peer):
+        @pl.when(peer != me)
         def _():
-            pltpu.make_async_copy(o_send.at[i], attended.at[me], o_in.at[me]).start()
-
-        @pl.when(i != me)
-        def _():
-            send(o_send.at[i], attended.at[me], o_out.at[i], o_in.at[me], i).start()
-
-        return 0
-
-    lax.fori_loop(0, parts, query_block, 0)
+            for index in range(3):
+                moved(index, peer).wait_send()
+
+    over(own * half, sent_near)
 
     def finish(step, _):
         peer = lax.rem(me + step, parts)
-        for index, (source, _) in enumerate(pairs):
-            arrive(source.at[peer], in_send.at[index, peer])
         arrive(o_send.at[peer], o_out.at[peer])
         arrive(attended.at[peer], o_in.at[peer])
         return 0
@@ -268,16 +341,24 @@
     arrive(attended.at[me], o_in.at[me])
 
 
-def attend(q, k, v, start):
+def attend(q, k, v, start, late, ready):
     parts, tokens, width = q.shape
     heads = width // HEAD_DIM
+    place = Place()
     whole = pl.BlockSpec(memory_space=VMEM)
+    far = pl.BlockSpec(memory_space=pl.ANY)
     split = jax.ShapeDtypeStruct(q.shape, BF16)
     flops = 4 * parts * parts * tokens * tokens * width // 2
-    return pl.pallas_call(
-        functools.partial(forward_kernel, parts, heads),
-        in_specs=[whole] * 4,
-        out_specs=[whole] * 6,
+    held = jax.ShapeDtypeStruct((place.as_, *late.shape), late.dtype)
+    shapes = [late.shape] + [value.shape[1:] for value in ready]
+    fulls = [
+        jax.ShapeDtypeStruct((place.xs, 2, place.as_, place.bs, *shape), BF16) for shape in shapes
+    ]
+    plan = WeightSpread.plan(shapes)
+    results = pl.pallas_call(
+        functools.partial(forward_kernel, parts, heads, plan, len(shapes)),
+        in_specs=[whole] * 4 + [far] * len(shapes),
+        out_specs=[whole] * 6 + [far] * (len(shapes) + 1),
         out_shape=[
             split,
             split,
@@ -285,18 +366,18 @@
             jax.ShapeDtypeStruct((parts, width, tokens), F32),
             jax.ShapeDtypeStruct((parts, heads, 1, tokens), F32),
             split,
+            *fulls,
+            held,
         ],
         scratch_shapes=[
             VMEM((parts, width, tokens), BF16),
-            VMEM((heads, tokens, width), BF16),
-            VMEM((heads, 1, tokens), F32),
-            VMEM((heads, 1, tokens), F32),
-            VMEM((width, tokens), F32),
+            VMEM((parts, heads, 1, tokens), F32),
             VMEM((parts, tokens, width), BF16),
             pltpu.SemaphoreType.DMA((3, parts)),
             pltpu.SemaphoreType.DMA((3, parts)),
             pltpu.SemaphoreType.DMA((parts,)),
             pltpu.SemaphoreType.DMA((parts,)),
+            *WeightSpread.semaphores(place, plan),
         ],
         compiler_params=pltpu.CompilerParams(
             collective_id=1, has_side_effects=True, vmem_limit_bytes=48 * MIB
@@ -305,27 +386,47 @@
             flops=4 * flops, bytes_accessed=16 * q.size, transcendentals=flops // 256
         ),
         name="attend",
-    )(q, k, v, start)
+    )(q, k, v, start, late, *ready)
+    devices = place.xs * 2 * place.as_ * place.bs
+    weights = [value.reshape(devices, *value.shape[4:]) for value in results[6:-1]]
+    return results[:6], weights
 
 
 def backward_kernel(
-    parts, heads,
-    d_in, q_all, k_all, v_all, o_all, lse_all, start,
-    dq_got, dk_got, dv_got,
-    d_all, q_own, d_own, k_turn, delta, dq_turn, dk_sum, dv_sum, dq_send, dk_send, dv_send,
-    in_send, in_recv, out_send, out_recv,
+    parts, heads, plan, count,
+    d_in, q_all, k_all, v_all, o_all, lse_all, start, *refs,
 ):
+    grads = refs[:count]
+    dq_got, dk_got, dv_got = refs[count : count + 3]
+    results = refs[count + 3 : 2 * count + 3]
+    refs = refs[2 * count + 3 :]
+    d_all, k_turn, delta, dq_turn, dk_sum, dv_sum, dq_send, dk_send, dv_send = refs[:9]
+    in_send, in_recv, out_send, out_recv, *buffers = refs[9:]
+    place = Place()
     _, tokens, width = d_in.shape
+    half = parts // 2
     me = lax.axis_index("seq")
-    greet(parts, me)
+    own = me // half
+    place.greet(greet(parts, me))
+    adding = GradSums(place, plan, grads, results, buffers)
+
+    def over(first, action):
+        def body(step, _):
+            action(first + lax.rem(me + step, half))
+            return 0
+
+        lax.fori_loop(0, half, body, 0)
+
+    def moved(peer):
+        return send(d_in.at[peer], d_all.at[me], in_send.at[peer], in_recv.at[me], peer)
+
+    over((1 - own) * half, lambda peer: moved(peer).start())
     pltpu.make_async_copy(d_in.at[me], d_all.at[me], in_recv.at[me]).start()
 
-    def start_step(step, _):
-        peer = lax.rem(me + step, parts)
-        send(d_in.at[peer], d_all.at[me], in_send.at[peer], in_recv.at[me], peer).start()
-        return 0
-
-    lax.fori_loop(1, parts, start_step, 0)
+    def start_near(peer):
+        pl.when(peer != me)(lambda: moved(peer).start())
+
+    over(own * half, start_near)
     sends = ((dq_send, dq_got), (dk_send, dk_got), (dv_send, dv_got))
 
     def give(index, block):
@@ -344,68 +445,88 @@
                 out_send.at[index, block], out_recv.at[index, me], block,
             ).start()
 
+    def give_query(i):
+        dq_send[i] = (dq_turn[i] * HEAD_DIM**-0.5).T.astype(BF16)
+        give(0, i)
+
+    def give_keys(j):
+        dk_send[j] = dk_sum[j].astype(BF16)
+        dv_send[j] = dv_sum[j].astype(BF16)
+        give(1, j)
+        give(2, j)
+
     def tile(i, j, masked):
         if masked:
             allowed = allowed_tile(i, j, tokens, start)
+        queries, grads_out, keys, mixed = q_all[i], d_all[i], k_all[j], v_all[j]
         for head in range(heads):
             rows = slice(head * HEAD_DIM, (head + 1) * HEAD_DIM)
-            query, grad = q_own[head, i], d_own[head, i]
-            scores = against(k_all[j], query)
+            query, grad = own_head(queries, head, width), own_head(grads_out, head, width)
+            scores = against(keys, query)
             if masked:
                 scores = jnp.where(allowed, scores, NEG)
             weights = jnp.exp(scores - lse_all[i, head])
-            dv_sum[...] += dot(weights.astype(BF16), grad)
-            slope = against(v_all[j], grad) - delta[i, head]
+            dv_sum[j] += dot(weights.astype(BF16), grad)
+            slope = against(mixed, grad) - delta[i, head]
             d_scores = (weights * slope).astype(BF16)
-            dk_sum[...] += dot(d_scores, query)
+            dk_sum[j] += dot(d_scores, query)
             dq_turn[i, rows] += dot(k_turn[j, rows], d_scores)
 
-    dq_turn[...] = jnp.zeros(dq_turn.shape, F32)
-
-    def key_block(step, _):
-        j = parts - 1 - step
-        arrive(d_all.at[j], in_recv.at[j])
-        got = d_all[j]
-        product = got.astype(F32).T * o_all[j]
+    def prepare(block):
+        arrive(d_all.at[block], in_recv.at[block])
+        product = d_all[block].astype(F32).T * o_all[block]
         for head in range(heads):
             rows = slice(head * HEAD_DIM, (head + 1) * HEAD_DIM)
-            delta[j, head] = jnp.sum(product[rows], axis=0, keepdims=True)
-            q_own[head, j] = own_head(q_all[j], head, width)
-            d_own[head, j] = own_head(got, head, width)
-        k_turn[j] = k_all[j].T
-        dk_sum[...] = jnp.zeros(dk_sum.shape, F32)
-        dv_sum[...] = jnp.zeros(dv_sum.shape, F32)
-
-        def query_block(i, _):
+            delta[block, head] = jnp.sum(product[rows], axis=0, keepdims=True)
+        k_turn[block] = k_all[block].T
+        dq_turn[block] = jnp.zeros(dq_turn.shape[1:], F32)
+        dk_sum[block] = jnp.zeros(dk_sum.shape[1:], F32)
+        dv_sum[block] = jnp.zeros(dv_sum.shape[1:], F32)
+
+    def tile_row(row, _):
+        phase, place_in = row // half, lax.rem(row, half)
+        adding.at_row(row, 3 * half)
+
+        @pl.when(row == 0)
+        def _():
+            lax.fori_loop(0, half, lambda n, _: prepare(own * half + n) or 0, 0)
+
+        @pl.when(row == half)
+        def _():
+            lax.fori_loop(0, half, lambda n, _: prepare((1 - own) * half + n) or 0, 0)
+
+        by_query = jnp.where(phase == 1, own == 1, own == 0)
+        lower = jnp.where(phase == 0, own, 1 - own) * half
+        outer = jnp.where(
+            phase == 2, jnp.where(by_query, half, 0), lower
+        ) + place_in
+        first = jnp.where(phase == 2, jnp.where(by_query, 0, half), jnp.where(by_query, lower, outer))
+        last = jnp.where(
+            phase == 2,
+            jnp.where(by_query, half, parts),
+            jnp.where(by_query, outer + 1, lower + half),
+        )
+
+        def inner_block(inner, _):
+            i, j = jnp.where(by_query, outer, inner), jnp.where(by_query, inner, outer)
             masked = (j == 0) | (j == i) | (i == parts - 1)
-
-            @pl.when(masked)
-            def _():
-                tile(i, j, True)
-
-            @pl.when(jnp.logical_not(masked))
-            def _():
-                tile(i, j, False)
-
-            @pl.when(j == 0)
-            def _():
-                dq_send[i] = (dq_turn[i] * HEAD_DIM**-0.5).T.astype(BF16)
-                give(0, i)
-
+            pl.when(masked)(lambda: tile(i, j, True))
+            pl.when(jnp.logical_not(masked))(lambda: tile(i, j, False))
             return 0
 
-        lax.fori_loop(j, parts, query_block, 0)
-        dk_send[j] = dk_sum[...].astype(BF16)
-        dv_send[j] = dv_sum[...].astype(BF16)
-        give(1, j)
-        give(2, j)
+        lax.fori_loop(first, last, inner_block, 0)
+        pl.when(by_query)(lambda: give_query(outer))
+        pl.when(jnp.logical_not(by_query))(lambda: give_keys(outer))
         return 0
 
-    lax.fori_loop(0, parts, key_block, 0)
+    lax.fori_loop(0, 3 * half, tile_row, 0)
+    pl.when(own == 0)(lambda: over(0, give_keys))
+    pl.when(own == 1)(lambda: over(half, give_query))
+    adding.finish()
 
     def finish(step, _):
         peer = lax.rem(me + step, parts)
-        arrive(d_in.at[peer], in_send.at[peer])
+        moved(peer).wait_send()
         for index, (source, target) in enumerate(sends):
             arrive(source.at[peer], out_send.at[index, peer])
             arrive(target.at[peer], out_recv.at[index, peer])
@@ -416,26 +537,28 @@
         arrive(target.at[me], out_recv.at[index, me])
 
 
-def attend_back(d_att, q, k, v, o, lse, start):
+def attend_back(d_att, q, k, v, o, lse, start, grads):
     parts, tokens, width = q.shape
     heads = width // HEAD_DIM
+    place = Place()
     whole = pl.BlockSpec(memory_space=VMEM)
+    far = pl.BlockSpec(memory_space=pl.ANY)
     split = jax.ShapeDtypeStruct(q.shape, BF16)
     flops = 10 * parts * parts * tokens * tokens * width // 2
-    return pl.pallas_call(
-        functools.partial(backward_kernel, parts, heads),
-        in_specs=[whole] * 7,
-        out_specs=[whole] * 3,
-        out_shape=[split] * 3,
+    plan, sum_shapes, sum_scratch = GradSums.plan(place, grads)
+    grads = [placed(place, grad) for grad in grads]
+    results = pl.pallas_call(
+        functools.partial(backward_kernel, parts, heads, plan, len(grads)),
+        in_specs=[far] + [whole] * 6 + [far] * len(grads),
+        out_specs=[far] * 3 + [whole] * len(grads),
+        out_shape=[split] * 3 + sum_shapes,
         scratch_shapes=[
             VMEM((parts, tokens, width), BF16),
-            VMEM((heads, parts, tokens, width), BF16),
-            VMEM((heads, parts, tokens, width), BF16),
             VMEM((parts, width, tokens), BF16),
             VMEM((parts, heads, 1, tokens), F32),
             VMEM((parts, width, tokens), F32),
-            VMEM((tokens, width), F32),
-            VMEM((tokens, width), F32),
+            VMEM((parts, tokens, width), F32),
+            VMEM((parts, tokens, width), F32),
             VMEM((parts, tokens, width), BF16),
             VMEM((parts, tokens, width), BF16),
             VMEM((parts, tokens, width), BF16),
@@ -443,15 +566,667 @@
             pltpu.SemaphoreType.DMA((parts,)),
             pltpu.SemaphoreType.DMA((3, parts)),
             pltpu.SemaphoreType.DMA((3, parts)),
+            *sum_scratch,
         ],
         compiler_params=pltpu.CompilerParams(
-            collective_id=2, has_side_effects=True, vmem_limit_bytes=48 * MIB
+            collective_id=2, has_side_effects=True, vmem_limit_bytes=60 * MIB
         ),
         cost_estimate=pl.CostEstimate(
             flops=4 * flops, bytes_accessed=20 * q.size, transcendentals=flops // 640
         ),
         name="attend_back",
-    )(d_att, q, k, v, o, lse, start)
+    )(d_att, q, k, v, o, lse, start, *grads)
+    return results[:3], results[3:]
+
+
+class Place:
+    def __init__(self):
+        self.xs = lax.axis_size("dp") // 2
+        seq = lax.axis_size("seq")
+        self.bs = 2 if seq <= 8 else 4
+        self.as_ = seq // self.bs
+        dp, rank = lax.axis_index("dp"), lax.axis_index("seq")
+        self.x, self.core = dp // 2, lax.rem(dp, 2)
+        self.a, self.b = rank // self.bs, lax.rem(rank, self.bs)
+
+    def device(self, x=None, core=None, a=None, b=None):
+        x, core = (self.x if x is None else x), (self.core if core is None else core)
+        a, b = (self.a if a is None else a), (self.b if b is None else b)
+        return (x * 2 + core, a * self.bs + b)
+
+    def peers(self, axis):
+        size = {"x": self.xs, "a": self.as_, "b": self.bs}[axis]
+        own = getattr(self, axis)
+        return [(step - 1, lax.rem(own + step, size)) for step in range(1, size)]
+
+    def greet(self, greeted=0):
+        barrier = pltpu.get_barrier_semaphore()
+        others = [self.device(core=1 - self.core)]
+        for axis in "x" if greeted else "xab":
+            others += [self.device(**{axis: index}) for _, index in self.peers(axis)]
+        for other in others:
+            pl.semaphore_signal(barrier, 1, device_id=other, device_id_type=MESH)
+        pl.semaphore_wait(barrier, len(others) + greeted)
+
+    @property
+    def inner(self):
+        return (self.a == 1) | (self.a == 2)
+
+    @property
+    def beside(self):
+        return self.a + 1 - 2 * lax.rem(self.a, 2)
+
+
+def column_pieces(columns, wanted):
+    tiles = columns // 128
+    wanted = min(wanted, tiles)
+    edges = [tiles * n // wanted * 128 for n in range(wanted)] + [columns]
+    return [(edges[n], edges[n + 1] - edges[n]) for n in range(wanted)]
+
+
+def placed(place, value):
+    return value.reshape(place.xs, 2, place.as_, place.bs, *value.shape[1:])
+
+
+def remote(source, target, send_sem, recv_sem, device):
+    return pltpu.make_async_remote_copy(
+        src_ref=source,
+        dst_ref=target,
+        send_sem=send_sem,
+        recv_sem=recv_sem,
+        device_id=device,
+        device_id_type=MESH,
+    )
+
+
+def flat(ref):
+    rows, columns = ref.shape[-2:]
+    return ref.reshape(ref.size // (rows * columns), rows, columns)
+
+
+class Relay:
+    def __init__(self, place, source, target, sems):
+        self.p, self.source, self.target, self.sems = place, source, target, sems
+        assert place.as_ == 4
+
+    def near(self):
+        p = self.p
+        return remote(
+            self.source, self.target.at[p.a],
+            self.sems.at[0, 0], self.sems.at[1, 0], p.device(a=p.beside),
+        )
+
+    def middle(self):
+        p = self.p
+        held = self.target.at[pl.ds(p.a // 2 * 2, 2)]
+        return remote(
+            held, held, self.sems.at[0, 1], self.sems.at[1, 1], p.device(a=3 - p.a)
+        )
+
+    def outward(self):
+        p = self.p
+        held = self.target.at[pl.ds((1 - p.a // 2) * 2, 2)]
+        return remote(
+            held, held, self.sems.at[0, 2], self.sems.at[1, 1], p.device(a=p.beside)
+        )
+
+    def local(self):
+        return pltpu.make_async_copy(self.source, self.target.at[self.p.a], self.sems.at[1, 2])
+
+    def step(self, number):
+        if number == 0:
+            self.local().start()
+            self.near().start()
+        elif number == 1:
+            self.local().wait()
+            self.near().wait_recv()
+            pl.when(self.p.inner)(lambda: self.middle().start())
+        elif number == 2:
+
+            @pl.when(self.p.inner)
+            def _():
+                self.middle().wait_recv()
+                self.outward().start()
+        else:
+
+            @pl.when(jnp.logical_not(self.p.inner))
+            def _():
+                self.middle().wait_recv()
+
+            @pl.when(self.p.inner)
+            def _():
+                self.middle().wait_send()
+                self.outward().wait_send()
+
+            self.near().wait_send()
+
+
+class Spread:
+    def __init__(self, place, source, full, order, sems, copied):
+        self.place, self.order, self.sems, self.copied = place, order, sems, copied
+        self.source, self.full = source, full
+
+    def moves(self, number):
+        p, full = self.place, self.full
+        if number == 2:
+            held = full.at[:, p.core]
+            return [(held, held, 0, p.device(core=1 - p.core))]
+        held = full.at[p.x, p.core, :, p.b]
+        source = self.source if number == 0 and self.copied else held
+        if number == 1:
+            source = held = full.at[:, p.core, :, p.b] if self.order == "xb" else full.at[p.x, p.core]
+        axis = self.order[number]
+        return [(source, held, s, p.device(**{axis: index})) for s, index in p.peers(axis)]
+
+    def copies(self, number):
+        base = sum([len(self.place.peers(axis)) for axis in self.order][:number])
+        return [
+            remote(source, target, self.sems.at[0, base + s], self.sems.at[1, base + s], device)
+            for source, target, s, device in self.moves(number)
+        ]
+
+    def local(self):
+        p = self.place
+        return pltpu.make_async_copy(
+            self.source, self.full.at[p.x, p.core, :, p.b], self.sems.at[2, 0]
+        )
+
+    def start(self, number):
+        if number == 0 and self.copied:
+            self.local().start()
+        for copy in self.copies(number):
+            copy.start()
+
+    def finish(self, number):
+        if number == 0 and self.copied:
+            self.local().wait()
+        for copy in self.copies(number):
+            copy.wait_recv()
+            copy.wait_send()
+
+
+def spread_semaphores(place):
+    return pltpu.SemaphoreType.DMA((3, place.xs + place.bs - 1))
+
+
+RELAY_SEMAPHORES = (2, 3)
+
+
+class WeightSpread:
+    def __init__(self, place, plan, late, late_held, ready, fulls, sems):
+        self.relays = []
+        self.units = []
+        for number, (array, start, size, order) in enumerate(plan):
+            columns = (slice(None),) * 4 + (slice(None), pl.ds(start, size))
+            full = fulls[array].at[columns]
+            if array == 0:
+                held = late_held.at[:, :, pl.ds(start, size)]
+                relay = Relay(place, late[0].at[:, pl.ds(start, size)], held, sems[0].at[number])
+                self.relays.append(relay)
+            else:
+                held = ready[array - 1].at[:, :, pl.ds(start, size)]
+            self.units.append(Spread(place, held, full, order, sems[1 + number], True))
+
+    @staticmethod
+    def plan(shapes):
+        plan = []
+        for array, shape in enumerate(shapes):
+            small = array == 1
+            for start, size in column_pieces(shape[1], 1 if small else 2):
+                plan.append((array, start, size, "xb" if small else "bx"))
+        return plan
+
+    @staticmethod
+    def semaphores(place, plan):
+        return [pltpu.SemaphoreType.DMA((len(plan), *RELAY_SEMAPHORES))] + [
+            spread_semaphores(place) for _ in plan
+        ]
+
+    def actions(self):
+        late, ready = self.units[: len(self.relays)], self.units[len(self.relays) :]
+        ready = sorted(ready, key=lambda unit: unit.order != "xb")
+        done = [(0, functools.partial(unit.start, 0)) for unit in ready]
+        relay = lambda number: [functools.partial(r.step, number) for r in self.relays]
+        next_step = lambda unit, number: (
+            lambda: (unit.finish(number), unit.start(number + 1)) if number < 2 else unit.finish(2)
+        )
+        done += [(0, action) for action in relay(0)]
+        done += [(1, action) for action in relay(1)]
+        done += [(2, next_step(ready[0], 0))]
+        done += [(3, action) for action in relay(2)]
+        done += [(4, next_step(unit, 0)) for unit in ready[1:3]]
+        done += [(5, action) for action in relay(3)]
+        done += [(5, functools.partial(unit.start, 0)) for unit in late]
+        done += [(6, next_step(unit, 0)) for unit in ready[3:]]
+        done += [(8, next_step(unit, 0)) for unit in late]
+        done += [(9, next_step(unit, 1)) for unit in ready[:2]]
+        done += [(10, next_step(unit, 1)) for unit in ready[2:3]]
+        done += [(12, next_step(unit, 1)) for unit in ready[3:] + late]
+        done += [(12, next_step(unit, 2)) for unit in ready + late]
+        return done
+
+    def at_row(self, row, count):
+        rows = sorted({at for at, _ in self.actions() if at < 12})
+        for at in rows:
+
+            @pl.when(row == at * count // 12)
+            def _():
+                for own_row, action in self.actions():
+                    if own_row == at:
+                        action()
+
+    def finish(self):
+        for at, action in self.actions():
+            if at >= 12:
+                action()
+
+
+def gather_kernel(plan, count, halves, *refs):
+    place = Place()
+    total = count + halves
+    sources, results = refs[:total], refs[total : 2 * total]
+    relay_sems, *sems = refs[2 * total :]
+    place.greet()
+    units, relays = [], []
+    for number, (array, start, size, order) in enumerate(plan):
+        source = sources[array].at[:, pl.ds(start, size)]
+        if array < count:
+            full = results[array].at[:, :, :, :, :, pl.ds(start, size)]
+            held = full.at[place.x, place.core, :, place.b]
+            units.append(Spread(place, None, full, order, sems[number], False))
+        else:
+            held = results[array].at[:, :, pl.ds(start, size)]
+        relays.append(Relay(place, source, held, relay_sems.at[number]))
+    first = len(units)
+
+    def act(index, number):
+        if number < 4:
+            relays[index].step(number)
+            if number == 3:
+                units[index].start(0)
+        else:
+            units[index].finish(number - 4)
+            if number < 6:
+                units[index].start(number - 3)
+
+    for relay in relays[:first]:
+        relay.step(0)
+    for number in (1, 2, 3):
+        for index in range(first):
+            act(index, number)
+        for relay in relays[first:] if number == 3 else []:
+            relay.step(0)
+    for index in range(first):
+        act(index, 4)
+    for relay in relays[first:]:
+        relay.step(1)
+    for index in range(first):
+        act(index, 5)
+    for relay in relays[first:]:
+        relay.step(2)
+    for index in range(first):
+        act(index, 6)
+    for relay in relays[first:]:
+        relay.step(3)
+
+
+def gathered(arrays, partly, collective_id):
+    place = Place()
+    xs, as_, bs = place.xs, place.as_, place.bs
+    both = [*arrays, *partly]
+    plan = []
+    for number, array in enumerate(both):
+        pieces = column_pieces(array.shape[1], 2)
+        for place_in, (start, size) in enumerate(pieces):
+            plan.append((number, start, size, "xb" if place_in == 0 else "bx"))
+    full = [jax.ShapeDtypeStruct((xs, 2, as_, bs, *array.shape), array.dtype) for array in arrays]
+    full += [jax.ShapeDtypeStruct((as_, *array.shape), array.dtype) for array in partly]
+    count = len([piece for piece in plan if piece[0] < len(arrays)])
+    results = pl.pallas_call(
+        functools.partial(gather_kernel, plan, len(arrays), len(partly)),
+        in_specs=[pl.BlockSpec(memory_space=pl.ANY)] * len(both),
+        out_specs=[pl.BlockSpec(memory_space=pl.ANY)] * len(both),
+        out_shape=full,
+        scratch_shapes=[
+            pltpu.SemaphoreType.DMA((len(plan), *RELAY_SEMAPHORES)),
+            *[spread_semaphores(place)] * count,
+        ],
+        compiler_params=pltpu.CompilerParams(collective_id=collective_id, has_side_effects=True),
+        cost_estimate=pl.CostEstimate(
+            flops=0, bytes_accessed=sum(array.size for array in arrays) * 64, transcendentals=0
+        ),
+        name="gathered",
+    )(*both)
+    devices = xs * 2 * as_ * bs
+    return [
+        result.reshape(devices, *result.shape[4:]) for result in results[: len(arrays)]
+    ] + list(results[len(arrays) :])
+
+
+def add_up(mine, others):
+    lead = mine.shape[:-2]
+
+    def at(ref, step):
+        index = []
+        for size in reversed(lead):
+            index.insert(0, lax.rem(step, size))
+            step = step // size
+        return ref.at[tuple(index)]
+
+    def body(step, _):
+        total = at(mine, step)[...].astype(F32)
+        for other in others:
+            total += at(other, step)[...].astype(F32)
+        at(mine, step)[...] = total.astype(mine.dtype)
+        return 0
+
+    count = 1
+    for size in lead:
+        count *= size
+    lax.fori_loop(0, count, body, 0)
+
+
+class RelaySum:
+    def __init__(self, place, own, inward, middle, last, sems, result):
+        self.p, self.own, self.sems, self.result = place, own, sems, result
+        self.inward, self.middle, self.last = inward, middle, last
+        assert place.as_ == 4
+
+    def move(self, number):
+        p = self.p
+        far = self.own.at[pl.ds((1 - p.a // 2) * 2, 2)]
+        if number == 0:
+            source, target, device = far, self.inward, p.beside
+        elif number == 1:
+            source, target, device = far, self.middle, 3 - p.a
+        else:
+            source, target, device = self.own.at[p.beside], self.last, p.beside
+        return remote(
+            source, target, self.sems.at[0, number], self.sems.at[1, number], p.device(a=device)
+        )
+
+    def step(self, number):
+        p, inner = self.p, self.p.inner
+        outer = jnp.logical_not(inner)
+        if number == 0:
+            pl.when(outer)(lambda: self.move(0).start())
+            pl.when(outer)(lambda: self.move(2).start())
+        elif number == 1:
+
+            @pl.when(inner)
+            def _():
+                self.move(0).wait_recv()
+                add_up(self.own.at[pl.ds((1 - p.a // 2) * 2, 2)], [self.inward])
+                self.move(1).start()
+        elif number == 2:
+
+            @pl.when(inner)
+            def _():
+                self.move(1).wait_recv()
+                add_up(self.own.at[pl.ds(p.a // 2 * 2, 2)], [self.middle])
+                self.move(2).start()
+        else:
+            self.move(2).wait_recv()
+            self.result[...] = self.own[p.a].astype(F32) + self.last[...].astype(F32)
+            pl.when(outer)(lambda: self.move(0).wait_send())
+            pl.when(inner)(lambda: self.move(1).wait_send())
+            self.move(2).wait_send()
+
+    @staticmethod
+    def scratch(rows, columns, dtype):
+        return [
+            VMEM((2, rows, columns), dtype),
+            VMEM((2, rows, columns), dtype),
+            VMEM((rows, columns), dtype),
+            pltpu.SemaphoreType.DMA((2, 3)),
+        ]
+
+
+class Sum:
+    def __init__(self, place, source, order, buffers):
+        self.place, self.order, self.source = place, order, source
+        self.own, self.got0, self.got1, self.got2, self.sems = buffers
+
+    @property
+    def held(self):
+        return self.own.at[self.place.x, :, self.place.b]
+
+    def moves(self, number):
+        p = self.place
+        if number == 0:
+            return [(self.source.at[:, 1 - p.core], self.got0, 0, p.device(core=1 - p.core))]
+        axis = self.order[number - 1]
+        got = self.got1 if number == 1 else self.got2
+        moves = []
+        for slot, index in p.peers(axis):
+            if axis == "x":
+                piece = self.own.at[index] if number == 1 else self.own.at[index, :, p.b]
+            else:
+                piece = self.own.at[:, :, index] if number == 1 else self.own.at[p.x, :, index]
+            moves.append((piece, got.at[slot], slot, p.device(**{axis: index})))
+        return moves
+
+    def copies(self, number):
+        base = sum(([1] + [len(self.place.peers(axis)) for axis in self.order])[:number])
+        return [
+            remote(source, target, self.sems.at[0, base + s], self.sems.at[1, base + s], device)
+            for source, target, s, device in self.moves(number)
+        ]
+
+    def local(self):
+        return pltpu.make_async_copy(
+            self.source.at[:, self.place.core], self.own, self.sems.at[2, 0]
+        )
+
+    def start(self, number):
+        for copy in self.copies(number):
+            copy.start()
+        if number == 0:
+            self.local().start()
+
+    def finish(self, number):
+        p = self.place
+        if number == 0:
+            self.local().wait()
+        for copy in self.copies(number):
+            copy.wait_recv()
+            copy.wait_send()
+        if number == 0:
+            add_up(self.own, [self.got0])
+        else:
+            if number == 2:
+                mine = self.held
+            else:
+                mine = self.own.at[p.x] if self.order[0] == "x" else self.own.at[:, :, p.b]
+            got = self.got1 if number == 1 else self.got2
+            add_up(mine, [got.at[slot] for slot in range(len(p.peers(self.order[number - 1])))])
+
+    @staticmethod
+    def scratch(place, rows, size, order, dtype):
+        xs, as_, bs = place.xs, place.as_, place.bs
+        shapes = {
+            "x": ((xs - 1, as_, bs, rows, size), (xs - 1, as_, rows, size)),
+            "b": ((bs - 1, xs, as_, rows, size), (bs - 1, as_, rows, size)),
+        }
+        return [
+            VMEM((xs, as_, bs, rows, size), dtype),
+            VMEM((xs, as_, bs, rows, size), dtype),
+            VMEM(shapes[order[0]][0], dtype),
+            VMEM(shapes[order[1]][1], dtype),
+            pltpu.SemaphoreType.DMA((3, xs + bs - 1)),
+        ]
+
+
+class GradSums:
+    WHOLE = 2
+
+    def __init__(self, place, plan, grads, results, buffers):
+        self.place = place
+        self.units, self.relays, self.results = [], [], []
+        for array, start, size, order in plan:
+            source = grads[array].at[:, :, :, :, :, pl.ds(start, size)]
+            unit, buffers = Sum(place, source, order, buffers[:5]), buffers[5:]
+            self.units.append(unit)
+            if array < self.WHOLE:
+                result = results[array].at[:, pl.ds(start, size)]
+                self.relays.append(RelaySum(place, unit.held, *buffers[:4], result))
+                buffers = buffers[4:]
+            else:
+                self.relays.append(None)
+                self.results.append((unit, results[array], start, size))
+
+    @classmethod
+    def plan(cls, place, grads):
+        plan, scratch, shapes = [], [], []
+        for array, grad in enumerate(grads):
+            rows, columns = grad.shape[1:]
+            small = array == len(grads) - 1
+            order = "bx" if small else "xb"
+            for start, size in column_pieces(columns, 1 if small else 2):
+                plan.append((array, start, size, order))
+                scratch += Sum.scratch(place, rows, size, order, grad.dtype)
+                if array < cls.WHOLE:
+                    scratch += RelaySum.scratch(rows, size, grad.dtype)
+            whole = array < cls.WHOLE
+            shape = (rows, columns) if whole else (place.as_, rows, columns)
+            shapes.append(jax.ShapeDtypeStruct(shape, F32 if whole else grad.dtype))
+        return plan, shapes, scratch
+
+    def actions(self):
+        units = self.units
+        count = len(units)
+
+        def step(index, number):
+            def action():
+                units[index].finish(number)
+                if number < 2:
+                    units[index].start(number + 1)
+                elif self.relays[index]:
+                    self.relays[index].step(0)
+
+            return action
+
+        def relay(index, number):
+            return lambda: self.relays[index].step(number)
+
+        done = [(0, functools.partial(unit.start, 0)) for unit in units]
+        first = [(0, 0), (1, 1), (1, 2), (2, 3), (2, 4), (3, 5), (3, 6)]
+        done += [(row, step(index, 0)) for row, index in first]
+        done += [(4, step(count - 1, 1)), (5, step(0, 1)), (7, step(1, 1)), (8, step(0, 2))]
+        done += [(9, step(2, 1)), (9, relay(0, 1)), (9, step(1, 2)), (10, relay(0, 2))]
+        done += [(10, relay(1, 1)), (11, step(3, 1)), (11, step(2, 2)), (11, relay(0, 3))]
+        done += [(11, relay(1, 2)), (11, step(count - 1, 2))]
+        done += [(12, step(3, 2)), (12, relay(2, 1)), (12, relay(3, 1)), (12, relay(1, 3))]
+        done += [(12, relay(2, 2)), (12, relay(3, 2))]
+        done += [(12, step(index, 1)) for index in range(4, count - 1)]
+        done += [(12, relay(2, 3)), (12, relay(3, 3))]
+        done += [(12, step(index, 2)) for index in range(4, count - 1)]
+        return done
+
+    def at_row(self, row, count):
+        rows = sorted({at for at, _ in self.actions() if at < 12})
+        for at in rows:
+
+            @pl.when(row == at * count // 12)
+            def _():
+                for own_row, action in self.actions():
+                    if own_row == at:
+                        action()
+
+    def finish(self):
+        for at, action in self.actions():
+            if at >= 12:
+                action()
+        for unit, result, start, size in self.results:
+            result[:, :, pl.ds(start, size)] = unit.held[...]
+
+
+def sums_kernel(plan, count, relayed, *refs):
+    place = Place()
+    total = count + relayed
+    sources, results, buffers = refs[:total], refs[total : 2 * total], refs[2 * total :]
+    place.greet()
+    units, relays = [], []
+    for array, start, size, order in plan:
+        result = results[array].at[:, pl.ds(start, size)]
+        if array < count:
+            source = sources[array].at[:, :, :, :, :, pl.ds(start, size)]
+            unit, buffers = Sum(place, source, order, buffers[:5]), buffers[5:]
+            units.append(unit)
+            own = unit.held
+        else:
+            own, buffers = buffers[0], buffers[1:]
+            own[...] = sources[array][:, :, pl.ds(start, size)]
+        relays.append(RelaySum(place, own, *buffers[:4], result))
+        buffers = buffers[4:]
+    first = len(units)
+    for unit in units:
+        unit.start(0)
+    for relay in relays[first:]:
+        relay.step(0)
+    for unit in units:
+        unit.finish(0)
+        unit.start(1)
+    for relay in relays[first:]:
+        relay.step(1)
+    for number in (1, 2):
+        for unit, relay in zip(units, relays):
+            unit.finish(number)
+            if number == 1:
+                unit.start(2)
+            else:
+                relay.step(0)
+        for relay in relays[first:]:
+            relay.step(number + 1)
+    for number in (1, 2, 3):
+        for relay in relays[:first]:
+            relay.step(number)
+
+
+def sums(arrays, partly, collective_id):
+    place = Place()
+    plan, scratch = [], []
+    for number, array in enumerate([*arrays, *partly]):
+        rows, columns = array.shape[1:]
+        for place_in, (start, size) in enumerate(column_pieces(columns, 2)):
+            order = "xb" if place_in == 0 else "bx"
+            plan.append((number, start, size, order))
+            if number < len(arrays):
+                scratch += Sum.scratch(place, rows, size, order, array.dtype)
+            else:
+                scratch.append(VMEM((place.as_, rows, size), array.dtype))
+            scratch += RelaySum.scratch(rows, size, array.dtype)
+    both = [placed(place, array) for array in arrays] + list(partly)
+    far, whole = pl.BlockSpec(memory_space=pl.ANY), pl.BlockSpec(memory_space=VMEM)
+    return pl.pallas_call(
+        functools.partial(sums_kernel, plan, len(arrays), len(partly)),
+        in_specs=[far] * len(arrays) + [whole] * len(partly),
+        out_specs=[whole] * len(both),
+        out_shape=[jax.ShapeDtypeStruct(array.shape[-2:], F32) for array in both],
+        scratch_shapes=scratch,
+        compiler_params=pltpu.CompilerParams(
+            collective_id=collective_id, has_side_effects=True, vmem_limit_bytes=48 * MIB
+        ),
+        cost_estimate=pl.CostEstimate(
+            flops=0, bytes_accessed=sum(array.size for array in arrays) * 4, transcendentals=0
+        ),
+        name="sums",
+    )(*both)
+
+
+def stacked(value, devices):
+    rows, columns = value.shape[0] // devices, value.shape[1]
+    fold = 1
+    while rows * fold % 16:
+        fold *= 2
+    value = value.reshape(devices, rows, fold, columns // fold)
+    return value.transpose(0, 2, 1, 3).reshape(devices, rows * fold, columns // fold)
+
+
+def unstacked(value, rows):
+    devices, high, columns = value.shape
+    value = value.reshape(devices, high // rows, rows, columns).transpose(0, 2, 1, 3)
+    return value.reshape(devices * rows, high // rows * columns)
 
 
 def shards(
@@ -462,19 +1237,27 @@
     assert row_count == 1
     parts = lax.axis_size("seq")
     rank = lax.axis_index("seq")
-    both = ("dp", "seq")
-    gather = lambda value: lax.all_gather(value, both, axis=0, tiled=True)
-
-    qkv = gather(jnp.concatenate([w_query, w_key, w_value], axis=1))
-    gains = gather(jnp.stack([gain_attn, gain_mlp], axis=1)).astype(F32)
-    gain_one, gain_two = gains[:, 0], gains[:, 1]
-    rest = gather(jnp.concatenate([w_out, w_gate, w_up], axis=1))
-    down_full = gather(w_down)
-    hidden_size = w_gate.shape[1]
-    query_full, key_full, value_full = (qkv[:, n * width : (n + 1) * width] for n in range(3))
-    out_full = rest[:, :width]
-    gate_full = rest[:, width : width + hidden_size]
-    up_full = rest[:, width + hidden_size :]
+    devices = lax.axis_size("dp") * parts
+    rows, down_rows = w_query.shape[0], w_down.shape[0]
+    multiple = 16 if down_rows >= 64 else 8
+    down_padded = -(-down_rows // multiple) * multiple
+
+    def spaced(value):
+        value = value.reshape(rows, devices, down_rows)
+        value = jnp.pad(value, ((0, 0), (0, 0), (0, down_padded - down_rows)))
+        return value.reshape(rows, devices * down_padded)
+
+    gains = jnp.pad(jnp.stack([gain_attn, gain_mlp]), ((0, 14), (0, 128 - rows)))
+    wide = lambda value: stacked(value, 1)[0]
+    query_full, key_full, value_full, gains, *ready = gathered(
+        [wide(w_query), wide(w_key), wide(w_value), gains],
+        [wide(w_out), wide(spaced(w_gate)), wide(spaced(w_up))],
+        3,
+    )
+    late = wide(jnp.pad(w_down, ((0, down_padded - down_rows), (0, 0))))
+    tall = lambda value: unstacked(value, rows)
+    query_full, key_full, value_full = tall(query_full), tall(key_full), tall(value_full)
+    gain_one, gain_two = (gains[:, n, :rows].reshape(width).astype(F32) for n in range(2))
 
     ends = jnp.cumsum(lengths[0])
     begins = ends - lengths[0]
@@ -495,7 +1278,11 @@
         x_low, gain_one[None], query_full, key_full, value_full,
         first_values.reshape(tokens, width), cosine, sine, parts,
     )
-    q_all, k_all, v_all, o_all, lse_all, attended = attend(q, k, v, start)
+    (q_all, k_all, v_all, o_all, lse_all, attended), (down_full, *weights) = attend(
+        q, k, v, start, late, ready
+    )
+    out_full, gate_full, up_full = (tall(value) for value in weights)
+    down_full = unstacked(down_full, down_padded)
     attended = attended.transpose(1, 0, 2).reshape(tokens, width)
 
     x_in = x_low.astype(F32)
@@ -523,7 +1310,11 @@
     d_att = against(grad_branch, out_full).astype(BF16)
     d_att = d_att.reshape(tokens, parts, width // parts).transpose(1, 0, 2)
 
-    dq, dk, dv = attend_back(d_att, q_all, k_all, v_all, o_all, lse_all, start)
+    share = lambda grad: stacked(grad.astype(BF16), devices)
+    (dq, dk, dv), (total_gate, total_up, part_down, part_out) = attend_back(
+        d_att, q_all, k_all, v_all, o_all, lse_all, start,
+        [share(grad_gate), share(grad_up), share(grad_down), share(grad_out)],
+    )
     dq, dk, dv, grad_first = unproject(dq, dk, dv, cosine, sine)
     grad_query_w = across(hidden_in, dq)
     grad_key_w = across(hidden_in, dk)
@@ -531,20 +1322,32 @@
     grad_hidden_in = against(dq, query_full) + against(dk, key_full) + against(dv, value_full)
     grad_x, grad_gain_one = norm_back(grad_hidden_in, x_in, gain_one)
     grad_x = grad_x + grad_middle
-    scatter = lambda value: lax.psum_scatter(value, both, scatter_dimension=0, tiled=True)
+    gains_grad = jnp.stack([grad_gain_one, grad_gain_two]).reshape(2, devices, rows)
+    gains_grad = jnp.pad(gains_grad.transpose(1, 0, 2), ((0, 0), (0, 6), (0, 128 - rows)))
+    total_query, total_key, total_value, gains_total, total_down, total_out = sums(
+        [share(grad_query_w), share(grad_key_w), share(grad_value_w), gains_grad],
+        [part_down, part_out],
+        4,
+    )
+    low = lambda total: unstacked(total[None], rows)
+
+    def close(total):
+        total = low(total).reshape(rows, devices, down_padded)
+        return total[:, :, :down_rows].reshape(rows, devices * down_rows)
+
     return (
         output,
         grad_x.reshape(inputs.shape),
         grad_first.reshape(inputs.shape),
-        scatter(grad_query_w),
-        scatter(grad_key_w),
-        scatter(grad_value_w),
-        scatter(grad_out),
-        scatter(grad_gain_one),
-        scatter(grad_gate),
-        scatter(grad_up),
-        scatter(grad_down),
-        scatter(grad_gain_two),
+        low(total_query),
+        low(total_key),
+        low(total_value),
+        low(total_out),
+        gains_total[0, :rows],
+        close(total_gate),
+        close(total_up),
+        unstacked(total_down[None], down_padded)[:down_rows],
+        gains_total[1, :rows],
     )
 
 

time: 1850 us -> 602 us (0.33)
  waiting for transfers between devices: 1320 us -> 0 us
  Pallas kernels: 253 us -> 469 us
  blocking collectives: 109 us -> 0 us
  matrix products: 101 us -> 78.5 us
    reduce_scatter x7 -> x0, waiting for transfers between devices: 1220 us -> none  [shards(): lax.psum_scatter(value, both, scatter_dimension=0, tiled=True)]
    pallas_call x2 -> x4, Pallas kernels: 243 us -> 459 us  [the longest x1 171 us: attend_back(): pl.pallas_call(functools.partial(backward_kernel, parts, heads, plan, len...]
    all_gather x3 -> x0, waiting for transfers between devices: 99.5 us -> none  [shards(): gather = lambda value: lax.all_gather(value, both, axis=0, tiled=True)]
    all_gather x1 -> x0, blocking collectives: 69.7 us -> none  [shards(): gather = lambda value: lax.all_gather(value, both, axis=0, tiled=True)]
    unnamed x1 -> x0, blocking collectives: 38.8 us -> none
    dot_general x18, matrix products: 101 us -> 78.5 us  [dot(): lax.dot_general(left, right, (((left_dim,), (right_dim,)), ((), ())), pre...]
  transfers between devices with their start and end apart: 10 -> 0, of which waited for: 9 -> 0; matrix products, arithmetic and copies ran while one was open for 4% -> 0% of each run, Pallas kernels for 7% -> 0%
where the time goes in v2:
time: 602 us; the launch traced here: 595 us
  Pallas kernels  469 us (78%)
  matrix products  78.5 us (13%)
  local copies, waits for them, and re-layouts  37.2 us (6%)
  other arithmetic  9.17 us (2%)
    pallas_call x1, Pallas kernels, attend_back(): pl.pallas_call(functools.partial(backward_kernel, parts, heads, plan, len...  171 us
    pallas_call x1, Pallas kernels, attend(): pl.pallas_call(functools.partial(forward_kernel, parts, heads, plan, len(...  159 us
    dot_general x18, matrix products, dot(): lax.dot_general(left, right, (((left_dim,), (right_dim,)), ((), ())), pre...  78.5 us
    pallas_call x1, Pallas kernels, gathered(): pl.pallas_call(functools.partial(gather_kernel, plan, len(arrays), len(pa...  64.9 us
    pallas_call x1, Pallas kernels, sums(): pl.pallas_call(functools.partial(sums_kernel, plan, len(arrays), len(part...  63.4 us
    unnamed x106, local copies, waits for them, and re-layouts  20.6 us

profile of v2, /device:TPU:0, one launch (start us, length us, event | category | flops | bytes accessed | tf_op | source)
XLA Modules:
  0.0 595.3 jit_solution(9299538284935940948)
XLA Ops:
  2.2 1.5 fusion.14
  8.2 1.5 reshape.172
  10.8 64.9 %gathered.1 = (bf16[2,2,4,2,32,1024]{5,4,3,2,1,0:T(8,128)(2,1)}, bf16[2,2,4,2,32,1024]{5,4,3,2,1,0:T(8,128)(2,1)}, bf16[2,2,4,2,32,1024]{5,4,3,2,1,0:T(8,128)(2,...) custom-call(bf16[32,1024]{1,0:T(8,128)(2,1)} %refs_0_.1, ...), custom_call_target="tpu_custom_call" | custom-call | bytes 6422528 | tf_op jit(solution)/shard_map/gathered/pallas_call | solution.py:885
  78.3 1.6 copy-done.1
  79.9 1.6 copy-done.11
  81.5 1.6 copy-done.13
  83.1 6.2 %project.1 = (bf16[8,512,128]{2,1,0:T(8,128)(2,1)S(1)}, bf16[8,512,128]{2,1,0:T(8,128)(2,1)S(1)}, bf16[8,512,128]{2,1,0:T(8,128)(2,1)S(1)}, bf16[512,1024]{1,0:T(8,128)(2,1)S(1)}) custom-call(bf16[512,1024]{1,0:T(8,128)(2,1)S(1)} %bitcast.108, f32[1,1024]{1,0:T(1,128)S(1)} %reshape.187.gain, bf16[1024,1024]{1,0:T(8,128)(2,1)S(1)} %bitcast.117, ...), custom_call_target="tpu_custom_call" | custom-call | flops 3221225472 | bytes 8388608 | tf_op jit(solution)/shard_map/project/pallas_call | solution.py:85
  93.2 159.5 %attend.1 = (bf16[8,512,128]{2,1,0:T(8,128)(2,1)S(1)}, bf16[8,512,128]{2,1,0:T(8,128)(2,1)S(1)}, bf16[8,512,128]{2,1,0:T(8,128)(2,1)S(1)}, f32[8,128,512]{2,1,0:...) custom-call(bf16[8,512,128]{2,1,0:T(8,128)(2,1)} %copy-done.25, ...), custom_call_target="tpu_custom_call" | custom-call | flops 17179869184 | bytes 8388608 | tf_op jit(solution)/shard_map/attend/pallas_call | solution.py:358
  256.3 1.5 copy.39
  257.8 3.4 multiply_reduce_fusion.2
  261.6 5.3 fusion.32
  266.9 5.4 fusion.31
  272.3 12.7 %fusion.3 = (bf16[512,3072]{1,0:T(8,128)(2,1)}, bf16[512,3072]{1,0:T(8,128)(2,1)}, bf16[512,3072]{1,0:T(8,128)(2,1)}) fusion(f32[512,3072]{1,0:T(8,128)} %fusion.31, f32[512,3072]{1,0:T(8,128)} %fusion.32, bf16[3072,1024]{1,0:T(8,128)(2,1)} %bitcast.146, bf16[1,512,1024]{2,1,0:T(8,128)(2,1)S(1)} %copy-done.38), kind=kOutput, calls=%fused_computation.5 | convolution fusion | flops 3244818432 | bytes 29360128 | tf_op jit(solution)/shard_map/dot_general | solution.py:22
  285.0 8.3 %fusion.15 = bf16[1,512,1024]{2,1,0:T(8,128)(2,1)} fusion(f32[512,1024]{1,0:T(8,128)S(1)} %get-tuple-element.101, bf16[512,3072]{1,0:T(8,128)(2,1)} %get-tuple-element.94, bf16[3072,1024]{1,0:T(8,128)(2,1)} %bitcast.147), kind=kOutput, calls=%fused_computation.38 | convolution fusion | flops 3222274048 | bytes 12582912 | tf_op jit(solution)/shard_map/dot_general | solution.py:22
  293.2 3.5 fusion.33
  296.7 5.8 multiply_reduce_fusion
  303.1 1.3 copy-done.32
  304.4 2.3 convolution_convert_fusion.7
  306.7 1.5 copy.41
  308.2 1.3 copy.42
  309.6 4.6 convolution_convert_fusion.6
  314.3 5.6 convolution_convert_fusion
  319.9 5.4 convolution_convert_fusion.1
  325.3 5.4 convolution_convert_fusion.2
  330.7 171.3 %attend_back.1 = (bf16[8,512,128]{2,1,0:T(8,128)(2,1)}, bf16[8,512,128]{2,1,0:T(8,128)(2,1)}, bf16[8,512,128]{2,1,0:T(8,128)(2,1)}, f32[32,3072]{1,0:T(8,128)}, ...) custom-call(bf16[8,512,128]{2,1,0:T(8,128)(2,1)} %bitcast.130, ...), custom_call_target="tpu_custom_call" | custom-call | flops 42949672960 | bytes 10485760 | tf_op jit(solution)/shard_map/attend_back/pallas_call | solution.py:550
  509.1 3.5 unproject.1
  513.9 1.4 copy-done.12
  516.9 1.8 fusion.13
  518.8 1.9 fusion.12
  520.9 2.7 convolution_convert_fusion.3
  523.5 2.6 convolution_convert_fusion.4
  527.5 63.4 %sums.1 = (f32[32,1024]{1,0:T(8,128)S(1)}, f32[32,1024]{1,0:T(8,128)S(1)}, f32[32,1024]{1,0:T(8,128)S(1)}, f32[8,128]{1,0:T(8,128)S(1)}, f32[96,1024]{1,0:T(8,128)S(1)}, /*index=5*/f32[32,1024]{1,0:T(8,128)S(1)}) custom-call(bf16[2,2,4,2,32,1024]{5,4,3,2,1,0:T(8,128)(2,1)S(1)} %bitcast.109, bf16[2,2,4,2,32,1024]{5,4,3,2,1,0:T(8,128)(2,1)} %bitcast.124, ...), custom_call_target="tpu_custom_call" | custom-call | bytes 12713984 | tf_op jit(solution)/shard_map/sums/pallas_call | solution.py:1201
  (145 shorter events, 33.5 us)
Async XLA Ops:
  0.6 5.7 copy-start.41
  0.7 5.9 copy-start.40
  5.7 87.5 %copy-start.10 = (s32[4096]{0:T(1024)}, s32[4096]{0:T(1024)S(1)}, u32[]{:S(2)}) copy-start(s32[4096]{0:T(1024)S(1)} %select_reduce_fusion) | copy-start | bytes 49156
  6.4 71.9 %copy-start = (bf16[1,512,1024]{2,1,0:T(8,128)(2,1)S(1)}, bf16[1,512,1024]{2,1,0:T(8,128)(2,1)}, u32[]{:S(2)}) copy-start(bf16[1,512,1024]{2,1,0:T(8,128)(2,1)} %param.13) | copy-start | bytes 3145732
  6.4 71.9 %copy-start.15 = (bf16[1,512,1024]{2,1,0:T(8,128)(2,1)S(1)}, bf16[1,512,1024]{2,1,0:T(8,128)(2,1)}, u32[]{:S(2)}) copy-start(bf16[1,512,1024]{2,1,0:T(8,128)(2,1)} %param.14) | copy-start | bytes 3145732
  78.3 1.6 copy-start.1
  83.1 10.1 %copy-start.20 = (bf16[4,32,3072]{2,1,0:T(8,128)(2,1)S(1)}, bf16[4,32,3072]{2,1,0:T(8,128)(2,1)}, u32[]{:S(2)}) copy-start(bf16[4,32,3072]{2,1,0:T(8,128)(2,1)} %get-tuple-element.58.refs_2_) | copy-start | bytes 2359300
  83.1 10.1 %copy-start.21 = (bf16[4,32,3072]{2,1,0:T(8,128)(2,1)S(1)}, bf16[4,32,3072]{2,1,0:T(8,128)(2,1)}, u32[]{:S(2)}) copy-start(bf16[4,32,3072]{2,1,0:T(8,128)(2,1)} %get-tuple-element.59.refs_3_) | copy-start | bytes 2359300
  83.1 10.1 %copy-start.22 = (bf16[4,32,1024]{2,1,0:T(8,128)(2,1)S(1)}, bf16[4,32,1024]{2,1,0:T(8,128)(2,1)}, u32[]{:S(2)}) copy-start(bf16[4,32,1024]{2,1,0:T(8,128)(2,1)} %get-tuple-element.57.refs_1_) | copy-start | bytes 786436
  257.7 3.4 copy-start.34
  257.8 3.8 copy-start.44
  261.1 5.7 slice-start
  261.5 5.3 copy-start.36
  261.5 5.3 slice-start.1
  266.9 5.4 copy-start.38
  284.9 8.3 %copy-start.46 = (bf16[512,3072]{1,0:T(8,128)(2,1)S(1)}, bf16[512,3072]{1,0:T(8,128)(2,1)}, u32[]{:S(2)}) copy-start(bf16[512,3072]{1,0:T(8,128)(2,1)} %get-tuple-element.93) | copy-start | bytes 9437188
  302.5 1.9 copy-start.35
  309.6 4.7 copy-start.39
  309.6 4.6 copy-start.48
  314.3 5.6 copy-start.37
  314.3 5.6 copy-start.45
  319.9 5.4 copy-start.47
  502.0 4.6 copy-start.3
  509.1 3.5 copy-start.14
  512.6 4.0 copy-start.6
  512.6 2.7 copy-start.12
  515.3 1.6 copy-start.43
  516.9 1.8 copy-start.33
  518.7 2.1 copy-start.7
  518.7 2.1 copy-start.24
  520.9 2.7 copy-start.19
  523.5 2.6 copy-start.17
  (19 other events, 22.9 us)

commit v3 on v2

--- a/solution.py
+++ b/solution.py
@@ -174,21 +174,20 @@
 
 
 def forward_kernel(
-    parts, heads, plan, count,
+    parts, heads, pieces, count,
     q_in, k_in, v_in, start, *refs,
 ):
-    late, ready = refs[:1], refs[1:count]
-    q_all, k_all, v_all, o_all, lse_all, attended = refs[count : count + 6]
-    fulls = refs[count + 6 : 2 * count + 6]
-    late_held = refs[2 * count + 6]
-    v_turn, total, o_send, in_send, in_recv, o_out, o_in, *sems = refs[2 * count + 7 :]
+    helds, refs = refs[: len(pieces)], refs[len(pieces) :]
+    q_all, k_all, v_all, o_all, lse_all, attended = refs[:6]
+    fulls, refs = refs[6 : 6 + count], refs[6 + count :]
+    v_turn, total, o_send, in_send, in_recv, o_out, o_in, *sems = refs
     place = Place()
     _, tokens, width = q_in.shape
     half = parts // 2
     me = lax.axis_index("seq")
     own = me // half
     place.greet(greet(parts, me))
-    spread = WeightSpread(place, plan, late, late_held, ready, fulls, sems)
+    spread = WeightSpread(place, pieces, helds, fulls, sems)
     pairs = ((q_in, q_all), (k_in, k_all), (v_in, v_all))
 
     def moved(index, peer):
@@ -341,7 +340,7 @@
     arrive(attended.at[me], o_in.at[me])
 
 
-def attend(q, k, v, start, late, ready):
+def attend(q, k, v, start, helds, pieces, shapes):
     parts, tokens, width = q.shape
     heads = width // HEAD_DIM
     place = Place()
@@ -349,16 +348,13 @@
     far = pl.BlockSpec(memory_space=pl.ANY)
     split = jax.ShapeDtypeStruct(q.shape, BF16)
     flops = 4 * parts * parts * tokens * tokens * width // 2
-    held = jax.ShapeDtypeStruct((place.as_, *late.shape), late.dtype)
-    shapes = [late.shape] + [value.shape[1:] for value in ready]
     fulls = [
         jax.ShapeDtypeStruct((place.xs, 2, place.as_, place.bs, *shape), BF16) for shape in shapes
     ]
-    plan = WeightSpread.plan(shapes)
     results = pl.pallas_call(
-        functools.partial(forward_kernel, parts, heads, plan, len(shapes)),
-        in_specs=[whole] * 4 + [far] * len(shapes),
-        out_specs=[whole] * 6 + [far] * (len(shapes) + 1),
+        functools.partial(forward_kernel, parts, heads, pieces, len(shapes)),
+        in_specs=[whole] * 4 + [far] * len(pieces),
+        out_specs=[whole] * 6 + [far] * len(shapes),
         out_shape=[
             split,
             split,
@@ -367,7 +363,6 @@
             jax.ShapeDtypeStruct((parts, heads, 1, tokens), F32),
             split,
             *fulls,
-            held,
         ],
         scratch_shapes=[
             VMEM((parts, width, tokens), BF16),
@@ -377,7 +372,7 @@
             pltpu.SemaphoreType.DMA((3, parts)),
             pltpu.SemaphoreType.DMA((parts,)),
             pltpu.SemaphoreType.DMA((parts,)),
-            *WeightSpread.semaphores(place, plan),
+            *[spread_semaphores(place)] * len(pieces),
         ],
         compiler_params=pltpu.CompilerParams(
             collective_id=1, has_side_effects=True, vmem_limit_bytes=48 * MIB
@@ -386,20 +381,19 @@
             flops=4 * flops, bytes_accessed=16 * q.size, transcendentals=flops // 256
         ),
         name="attend",
-    )(q, k, v, start, late, *ready)
+    )(q, k, v, start, *helds)
     devices = place.xs * 2 * place.as_ * place.bs
-    weights = [value.reshape(devices, *value.shape[4:]) for value in results[6:-1]]
+    weights = [value.reshape(devices, *value.shape[4:]) for value in results[6:]]
     return results[:6], weights
 
 
 def backward_kernel(
-    parts, heads, plan, count,
+    parts, heads, pieces, count,
     d_in, q_all, k_all, v_all, o_all, lse_all, start, *refs,
 ):
-    grads = refs[:count]
-    dq_got, dk_got, dv_got = refs[count : count + 3]
-    results = refs[count + 3 : 2 * count + 3]
-    refs = refs[2 * count + 3 :]
+    grads, refs = refs[:count], refs[count:]
+    (dq_got, dk_got, dv_got), refs = refs[:3], refs[3:]
+    results, refs = refs[: len(pieces)], refs[len(pieces) :]
     d_all, k_turn, delta, dq_turn, dk_sum, dv_sum, dq_send, dk_send, dv_send = refs[:9]
     in_send, in_recv, out_send, out_recv, *buffers = refs[9:]
     place = Place()
@@ -408,7 +402,7 @@
     me = lax.axis_index("seq")
     own = me // half
     place.greet(greet(parts, me))
-    adding = GradSums(place, plan, grads, results, buffers)
+    adding = GradSums(place, pieces, grads, results, buffers)
 
     def over(first, action):
         def body(step, _):
@@ -537,7 +531,7 @@
         arrive(target.at[me], out_recv.at[index, me])
 
 
-def attend_back(d_att, q, k, v, o, lse, start, grads):
+def attend_back(d_att, q, k, v, o, lse, start, grads, pieces):
     parts, tokens, width = q.shape
     heads = width // HEAD_DIM
     place = Place()
@@ -545,12 +539,13 @@
     far = pl.BlockSpec(memory_space=pl.ANY)
     split = jax.ShapeDtypeStruct(q.shape, BF16)
     flops = 10 * parts * parts * tokens * tokens * width // 2
-    plan, sum_shapes, sum_scratch = GradSums.plan(place, grads)
+    sum_shapes = [piece.held(place, grads[piece.array].shape[1]) for piece in pieces]
+    sum_scratch = GradSums.scratch(place, pieces, grads)
     grads = [placed(place, grad) for grad in grads]
     results = pl.pallas_call(
-        functools.partial(backward_kernel, parts, heads, plan, len(grads)),
+        functools.partial(backward_kernel, parts, heads, pieces, len(grads)),
         in_specs=[far] + [whole] * 6 + [far] * len(grads),
-        out_specs=[far] * 3 + [whole] * len(grads),
+        out_specs=[far] * 3 + [far] * len(pieces),
         out_shape=[split] * 3 + sum_shapes,
         scratch_shapes=[
             VMEM((parts, tokens, width), BF16),
@@ -701,49 +696,80 @@
             self.near().wait_send()
 
 
+class Piece:
+    def __init__(self, array, start, size, order, deep):
+        self.array, self.start, self.size, self.order, self.deep = array, start, size, order, deep
+
+    @staticmethod
+    def all(shapes):
+        pieces = []
+        for array, kinds in enumerate(
+            ([("bx", 0)], [("bx", 1)] * 2, [("xb", 1), ("bx", 1)], [("bx", 0)] * 2)
+        ):
+            for (start, size), kind in zip(column_pieces(shapes[array][1], len(kinds)), kinds):
+                pieces.append(Piece(array, start, size, *kind))
+        return pieces
+
+    def held(self, place, rows):
+        lead = {"": (), "b": (place.bs,), "x": (place.xs,)}[self.order[0] if self.deep else ""]
+        lead = (*lead, place.as_) if self.order[0] == "x" else (place.as_, *lead)
+        return jax.ShapeDtypeStruct((*lead, rows, self.size), BF16)
+
+    def along_a(self, place, held):
+        if not self.deep:
+            return held
+        return held.at[place.x] if self.order[0] == "x" else held.at[:, place.b]
+
+    def columns(self, ref):
+        return ref.at[(slice(None),) * (len(ref.shape) - 1) + (pl.ds(self.start, self.size),)]
+
+
 class Spread:
-    def __init__(self, place, source, full, order, sems, copied):
-        self.place, self.order, self.sems, self.copied = place, order, sems, copied
-        self.source, self.full = source, full
-
-    def moves(self, number):
-        p, full = self.place, self.full
+    def __init__(self, place, views, order, sems, source=None, first=0):
+        self.place, self.views, self.order, self.sems = place, views, order, sems
+        self.source, self.first = source, first
+
+    @staticmethod
+    def views_of(place, full, order):
+        p = place
+        middle = full.at[:, p.core, :, p.b] if order == "xb" else full.at[p.x, p.core]
+        return full.at[p.x, p.core, :, p.b], middle, full.at[:, p.core]
+
+    def copies(self, number):
+        p, view = self.place, self.views[number]
+        source = self.source if self.source is not None and number == self.first else view
+        base = sum([len(p.peers(axis)) for axis in self.order][:number])
         if number == 2:
-            held = full.at[:, p.core]
-            return [(held, held, 0, p.device(core=1 - p.core))]
-        held = full.at[p.x, p.core, :, p.b]
-        source = self.source if number == 0 and self.copied else held
-        if number == 1:
-            source = held = full.at[:, p.core, :, p.b] if self.order == "xb" else full.at[p.x, p.core]
-        axis = self.order[number]
-        return [(source, held, s, p.device(**{axis: index})) for s, index in p.peers(axis)]
-
-    def copies(self, number):
-        base = sum([len(self.place.peers(axis)) for axis in self.order][:number])
+            devices = [(0, p.device(core=1 - p.core))]
+        else:
+            axis = self.order[number]
+            devices = [(s, p.device(**{axis: index})) for s, index in p.peers(axis)]
         return [
-            remote(source, target, self.sems.at[0, base + s], self.sems.at[1, base + s], device)
-            for source, target, s, device in self.moves(number)
+            remote(source, view, self.sems.at[0, base + s], self.sems.at[1, base + s], device)
+            for s, device in devices
         ]
 
     def local(self):
-        p = self.place
-        return pltpu.make_async_copy(
-            self.source, self.full.at[p.x, p.core, :, p.b], self.sems.at[2, 0]
-        )
+        return pltpu.make_async_copy(self.source, self.views[self.first], self.sems.at[2, 0])
 
     def start(self, number):
-        if number == 0 and self.copied:
+        if self.source is not None and number == self.first:
             self.local().start()
         for copy in self.copies(number):
             copy.start()
 
     def finish(self, number):
-        if number == 0 and self.copied:
+        if self.source is not None and number == self.first:
             self.local().wait()
         for copy in self.copies(number):
             copy.wait_recv()
             copy.wait_send()
 
+    def then(self, number):
+        self.finish(number)
+        if number < 2:
+            self.start(number + 1)
+
 
 def spread_semaphores(place):
     return pltpu.SemaphoreType.DMA((3, place.xs + place.bs - 1))
@@ -752,62 +778,9 @@
 RELAY_SEMAPHORES = (2, 3)
 
 
-class WeightSpread:
-    def __init__(self, place, plan, late, late_held, ready, fulls, sems):
-        self.relays = []
-        self.units = []
-        for number, (array, start, size, order) in enumerate(plan):
-            columns = (slice(None),) * 4 + (slice(None), pl.ds(start, size))
-            full = fulls[array].at[columns]
-            if array == 0:
-                held = late_held.at[:, :, pl.ds(start, size)]
-                relay = Relay(place, late[0].at[:, pl.ds(start, size)], held, sems[0].at[number])
-                self.relays.append(relay)
-            else:
-                held = ready[array - 1].at[:, :, pl.ds(start, size)]
-            self.units.append(Spread(place, held, full, order, sems[1 + number], True))
-
-    @staticmethod
-    def plan(shapes):
-        plan = []
-        for array, shape in enumerate(shapes):
-            small = array == 1
-            for start, size in column_pieces(shape[1], 1 if small else 2):
-                plan.append((array, start, size, "xb" if small else "bx"))
-        return plan
-
-    @staticmethod
-    def semaphores(place, plan):
-        return [pltpu.SemaphoreType.DMA((len(plan), *RELAY_SEMAPHORES))] + [
-            spread_semaphores(place) for _ in plan
-        ]
-
-    def actions(self):
-        late, ready = self.units[: len(self.relays)], self.units[len(self.relays) :]
-        ready = sorted(ready, key=lambda unit: unit.order != "xb")
-        done = [(0, functools.partial(unit.start, 0)) for unit in ready]
-        relay = lambda number: [functools.partial(r.step, number) for r in self.relays]
-        next_step = lambda unit, number: (
-            lambda: (unit.finish(number), unit.start(number + 1)) if number < 2 else unit.finish(2)
-        )
-        done += [(0, action) for action in relay(0)]
-        done += [(1, action) for action in relay(1)]
-        done += [(2, next_step(ready[0], 0))]
-        done += [(3, action) for action in relay(2)]
-        done += [(4, next_step(unit, 0)) for unit in ready[1:3]]
-        done += [(5, action) for action in relay(3)]
-        done += [(5, functools.partial(unit.start, 0)) for unit in late]
-        done += [(6, next_step(unit, 0)) for unit in ready[3:]]
-        done += [(8, next_step(unit, 0)) for unit in late]
-        done += [(9, next_step(unit, 1)) for unit in ready[:2]]
-        done += [(10, next_step(unit, 1)) for unit in ready[2:3]]
-        done += [(12, next_step(unit, 1)) for unit in ready[3:] + late]
-        done += [(12, next_step(unit, 2)) for unit in ready + late]
-        return done
-
+class InRows:
     def at_row(self, row, count):
-        rows = sorted({at for at, _ in self.actions() if at < 12})
-        for at in rows:
+        for at in sorted({at for at, _ in self.actions() if at < 12}):
 
             @pl.when(row == at * count // 12)
             def _():
@@ -821,74 +794,99 @@
                 action()
 
 
-def gather_kernel(plan, count, halves, *refs):
+class WeightSpread(InRows):
+    def __init__(self, place, pieces, sources, fulls, sems):
+        self.units = []
+        for piece, source, own_sems in zip(pieces, sources, sems):
+            full = piece.columns(fulls[piece.array])
+            views = Spread.views_of(place, full, piece.order)
+            self.units.append(Spread(place, views, piece.order, own_sems, source, piece.deep))
+
+    def actions(self):
+        out, gate0, gate1, up0, up1, down0, down1 = self.units
+        start = lambda unit: functools.partial(unit.start, unit.first)
+        then = lambda unit, number: functools.partial(unit.then, number)
+        done = [(0, start(unit)) for unit in (gate0, down0, gate1, down1, up1, out, up0)]
+        done += [(4, then(down0, 0)), (5, then(down1, 0)), (6, then(out, 0))]
+        done += [(7, then(gate0, 1)), (8, then(gate1, 1)), (9, then(up0, 1)), (10, then(up1, 1))]
+        done += [(12, then(unit, 1)) for unit in (down0, down1, out)]
+        done += [(12, then(unit, 2)) for unit in (gate0, gate1, up0, up1, down0, down1, out)]
+        return done
+
+
+def gather_kernel(plan, pieces, arrays, parted, *refs):
     place = Place()
-    total = count + halves
-    sources, results = refs[:total], refs[total : 2 * total]
-    relay_sems, *sems = refs[2 * total :]
+    total = arrays + parted
+    sources, refs = refs[:total], refs[total:]
+    fulls, helds, (relay_sems, *sems) = (
+        refs[:arrays], refs[arrays : arrays + len(pieces)], refs[arrays + len(pieces) :]
+    )
     place.greet()
-    units, relays = [], []
+    whole, relays = [], []
     for number, (array, start, size, order) in enumerate(plan):
-        source = sources[array].at[:, pl.ds(start, size)]
-        if array < count:
-            full = results[array].at[:, :, :, :, :, pl.ds(start, size)]
-            held = full.at[place.x, place.core, :, place.b]
-            units.append(Spread(place, None, full, order, sems[number], False))
-        else:
-            held = results[array].at[:, :, pl.ds(start, size)]
-        relays.append(Relay(place, source, held, relay_sems.at[number]))
-    first = len(units)
-
-    def act(index, number):
-        if number < 4:
-            relays[index].step(number)
-            if number == 3:
-                units[index].start(0)
-        else:
-            units[index].finish(number - 4)
-            if number < 6:
-                units[index].start(number - 3)
-
-    for relay in relays[:first]:
-        relay.step(0)
-    for number in (1, 2, 3):
-        for index in range(first):
-            act(index, number)
-        for relay in relays[first:] if number == 3 else []:
-            relay.step(0)
-    for index in range(first):
-        act(index, 4)
-    for relay in relays[first:]:
-        relay.step(1)
-    for index in range(first):
-        act(index, 5)
-    for relay in relays[first:]:
-        relay.step(2)
-    for index in range(first):
-        act(index, 6)
-    for relay in relays[first:]:
+        views = Spread.views_of(place, fulls[array].at[:, :, :, :, :, pl.ds(start, size)], order)
+        relays.append(
+            Relay(place, sources[array].at[:, pl.ds(start, size)], views[0], relay_sems.at[number])
+        )
+        whole.append(Spread(place, views, order, sems[number]))
+    deep, flat_relays, deep_relays = [], [], []
+    for number, (piece, held) in enumerate(zip(pieces, helds)):
+        view = piece.along_a(place, held)
+        index = len(plan) + number
+        source = piece.columns(sources[arrays + piece.array])
+        relay = Relay(place, source, view, relay_sems.at[index])
+        (deep_relays if piece.deep else flat_relays).append(relay)
+        if piece.deep:
+            deep.append(Spread(place, [view], piece.order, sems[index]))
+
+    def step(group, number):
+        for relay in group:
+            relay.step(number)
+
+    step(relays, 0)
+    step(relays, 1)
+    step(deep_relays, 0)
+    step(relays, 2)
+    for relay, unit in zip(relays, whole):
         relay.step(3)
-
-
-def gathered(arrays, partly, collective_id):
+        unit.start(0)
+    step(deep_relays, 1)
+    step(flat_relays, 0)
+    for unit in whole:
+        unit.then(0)
+    step(deep_relays, 2)
+    for relay, unit in zip(deep_relays, deep):
+        relay.step(3)
+        unit.start(0)
+    step(flat_relays, 1)
+    for unit in whole:
+        unit.then(1)
+    step(flat_relays, 2)
+    for unit in whole:
+        unit.then(2)
+    step(flat_relays, 3)
+    for unit in deep:
+        unit.finish(0)
+
+
+def gathered(arrays, parted, pieces, collective_id):
     place = Place()
     xs, as_, bs = place.xs, place.as_, place.bs
-    both = [*arrays, *partly]
     plan = []
-    for number, array in enumerate(both):
-        pieces = column_pieces(array.shape[1], 2)
-        for place_in, (start, size) in enumerate(pieces):
+    for number, array in enumerate(arrays):
+        for place_in, (start, size) in enumerate(column_pieces(array.shape[1], 2)):
             plan.append((number, start, size, "xb" if place_in == 0 else "bx"))
     full = [jax.ShapeDtypeStruct((xs, 2, as_, bs, *array.shape), array.dtype) for array in arrays]
-    full += [jax.ShapeDtypeStruct((as_, *array.shape), array.dtype) for array in partly]
-    count = len([piece for piece in plan if piece[0] < len(arrays)])
+    full += [piece.held(place, parted[piece.array].shape[0]) for piece in pieces]
+    far = pl.BlockSpec(memory_space=pl.ANY)
+    count = len(plan) + len(pieces)
     results = pl.pallas_call(
-        functools.partial(gather_kernel, plan, len(arrays), len(partly)),
-        in_specs=[pl.BlockSpec(memory_space=pl.ANY)] * len(both),
-        out_specs=[pl.BlockSpec(memory_space=pl.ANY)] * len(both),
+        functools.partial(gather_kernel, plan, pieces, len(arrays), len(parted)),
+        in_specs=[far] * (len(arrays) + len(parted)),
+        out_specs=[far] * len(full),
         out_shape=full,
         scratch_shapes=[
-            pltpu.SemaphoreType.DMA((len(plan), *RELAY_SEMAPHORES)),
+            pltpu.SemaphoreType.DMA((count, *RELAY_SEMAPHORES)),
             *[spread_semaphores(place)] * count,
         ],
         compiler_params=pltpu.CompilerParams(collective_id=collective_id, has_side_effects=True),
@@ -896,11 +894,10 @@
             flops=0, bytes_accessed=sum(array.size for array in arrays) * 64, transcendentals=0
         ),
         name="gathered",
-    )(*both)
+    )(*arrays, *parted)
     devices = xs * 2 * as_ * bs
-    return [
-        result.reshape(devices, *result.shape[4:]) for result in results[: len(arrays)]
-    ] + list(results[len(arrays) :])
+    gives = [result.reshape(devices, *result.shape[4:]) for result in results[: len(arrays)]]
+    return gives, results[len(arrays) :]
 
 
 def add_up(mine, others):
@@ -990,6 +987,11 @@
     @property
     def held(self):
         return self.own.at[self.place.x, :, self.place.b]
+
+    @property
+    def part(self):
+        p = self.place
+        return self.own.at[p.x] if self.order[0] == "x" else self.own.at[:, :, p.b]
 
     def moves(self, number):
         p = self.place
@@ -1034,10 +1036,7 @@
         if number == 0:
             add_up(self.own, [self.got0])
         else:
-            if number == 2:
-                mine = self.held
-            else:
-                mine = self.own.at[p.x] if self.order[0] == "x" else self.own.at[:, :, p.b]
+            mine = self.held if number == 2 else self.part
             got = self.got1 if number == 1 else self.got2
             add_up(mine, [got.at[slot] for slot in range(len(p.peers(self.order[number - 1])))])
 
@@ -1057,152 +1056,174 @@
         ]
 
 
-class GradSums:
-    WHOLE = 2
-
-    def __init__(self, place, plan, grads, results, buffers):
-        self.place = place
-        self.units, self.relays, self.results = [], [], []
-        for array, start, size, order in plan:
-            source = grads[array].at[:, :, :, :, :, pl.ds(start, size)]
-            unit, buffers = Sum(place, source, order, buffers[:5]), buffers[5:]
+class GradSums(InRows):
+    def __init__(self, place, pieces, grads, results, buffers):
+        self.units, self.outs = [], []
+        for piece, result in zip(pieces, results):
+            source = piece.columns(grads[piece.array])
+            unit, buffers = Sum(place, source, piece.order[::-1], buffers[:5]), buffers[5:]
             self.units.append(unit)
-            if array < self.WHOLE:
-                result = results[array].at[:, pl.ds(start, size)]
-                self.relays.append(RelaySum(place, unit.held, *buffers[:4], result))
-                buffers = buffers[4:]
-            else:
-                self.relays.append(None)
-                self.results.append((unit, results[array], start, size))
-
-    @classmethod
-    def plan(cls, place, grads):
-        plan, scratch, shapes = [], [], []
-        for array, grad in enumerate(grads):
-            rows, columns = grad.shape[1:]
-            small = array == len(grads) - 1
-            order = "bx" if small else "xb"
-            for start, size in column_pieces(columns, 1 if small else 2):
-                plan.append((array, start, size, order))
-                scratch += Sum.scratch(place, rows, size, order, grad.dtype)
-                if array < cls.WHOLE:
-                    scratch += RelaySum.scratch(rows, size, grad.dtype)
-            whole = array < cls.WHOLE
-            shape = (rows, columns) if whole else (place.as_, rows, columns)
-            shapes.append(jax.ShapeDtypeStruct(shape, F32 if whole else grad.dtype))
-        return plan, shapes, scratch
+            self.outs.append((unit.part if piece.deep else unit.held, result))
+
+    @staticmethod
+    def scratch(place, pieces, grads):
+        return [
+            item
+            for piece in pieces
+            for item in Sum.scratch(
+                place, grads[piece.array].shape[1], piece.size, piece.order[::-1], BF16
+            )
+        ]
 
     def actions(self):
-        units = self.units
-        count = len(units)
-
-        def step(index, number):
+        out, gate0, gate1, up0, up1, down0, down1 = self.units
+
+        def copy_of(unit):
+            source, result = self.outs[self.units.index(unit)]
+            return pltpu.make_async_copy(source, result, unit.sems.at[2, 1])
+
+        def then(unit, number):
             def action():
-                units[index].finish(number)
-                if number < 2:
-                    units[index].start(number + 1)
-                elif self.relays[index]:
-                    self.relays[index].step(0)
+                unit.finish(number)
+                if number < (1 if unit in (gate0, gate1, up0, up1) else 2):
+                    unit.start(number + 1)
+                else:
+                    copy_of(unit).start()
 
             return action
 
-        def relay(index, number):
-            return lambda: self.relays[index].step(number)
-
-        done = [(0, functools.partial(unit.start, 0)) for unit in units]
-        first = [(0, 0), (1, 1), (1, 2), (2, 3), (2, 4), (3, 5), (3, 6)]
-        done += [(row, step(index, 0)) for row, index in first]
-        done += [(4, step(count - 1, 1)), (5, step(0, 1)), (7, step(1, 1)), (8, step(0, 2))]
-        done += [(9, step(2, 1)), (9, relay(0, 1)), (9, step(1, 2)), (10, relay(0, 2))]
-        done += [(10, relay(1, 1)), (11, step(3, 1)), (11, step(2, 2)), (11, relay(0, 3))]
-        done += [(11, relay(1, 2)), (11, step(count - 1, 2))]
-        done += [(12, step(3, 2)), (12, relay(2, 1)), (12, relay(3, 1)), (12, relay(1, 3))]
-        done += [(12, relay(2, 2)), (12, relay(3, 2))]
-        done += [(12, step(index, 1)) for index in range(4, count - 1)]
-        done += [(12, relay(2, 3)), (12, relay(3, 3))]
-        done += [(12, step(index, 2)) for index in range(4, count - 1)]
+        order = (down0, down1, out, up0, gate0, gate1, up1)
+        done = [(0, functools.partial(unit.start, 0)) for unit in order]
+        done += [(row, then(unit, 0)) for row, unit in zip((0, 1, 1, 2, 2, 3, 3), order)]
+        done += [(6, then(down0, 1)), (7, then(down1, 1)), (8, then(out, 1)), (9, then(up0, 1))]
+        done += [(10, then(gate0, 1)), (11, then(down0, 2))]
+        done += [(12, then(down1, 2)), (12, then(out, 2)), (12, then(gate1, 1)), (12, then(up1, 1))]
+        done += [(12, lambda unit=unit: copy_of(unit).wait()) for unit in order]
         return done
 
-    def at_row(self, row, count):
-        rows = sorted({at for at, _ in self.actions() if at < 12})
-        for at in rows:
-
-            @pl.when(row == at * count // 12)
-            def _():
-                for own_row, action in self.actions():
-                    if own_row == at:
-                        action()
+
+class HeldSum:
+    def __init__(self, place, piece, source, buffers, result):
+        self.place, self.piece, self.source = place, piece, source
+        self.own, self.got, self.sems, *relay = buffers
+        self.relay = RelaySum(place, self.own, *relay, result)
+        self.axis = piece.order[0]
+
+    def copies(self):
+        if not self.piece.deep:
+            return []
+        p = self.place
+        at = lambda index: self.source.at[index] if self.axis == "x" else self.source.at[:, index]
+        return [
+            remote(
+                at(index), self.got.at[s], self.sems.at[0, s], self.sems.at[1, s],
+                p.device(**{self.axis: index}),
+            )
+            for s, index in p.peers(self.axis)
+        ]
+
+    def local(self):
+        mine = self.piece.along_a(self.place, self.source)
+        return pltpu.make_async_copy(mine, self.own, self.sems.at[2, 0])
+
+    def start(self):
+        self.local().start()
+        for copy in self.copies():
+            copy.start()
 
     def finish(self):
-        for at, action in self.actions():
-            if at >= 12:
-                action()
-        for unit, result, start, size in self.results:
-            result[:, :, pl.ds(start, size)] = unit.held[...]
-
-
-def sums_kernel(plan, count, relayed, *refs):
+        self.local().wait()
+        copies = self.copies()
+        for copy in copies:
+            copy.wait_recv()
+            copy.wait_send()
+        if copies:
+            add_up(self.own, [self.got.at[slot] for slot in range(len(copies))])
+        self.relay.step(0)
+
+    @staticmethod
+    def scratch(place, piece, rows):
+        count = len(place.peers(piece.order[0])) if piece.deep else 1
+        got = (count, place.as_, rows, piece.size) if piece.deep else (1, 1, 16, 128)
+        return [
+            VMEM((place.as_, rows, piece.size), BF16),
+            VMEM(got, BF16),
+            pltpu.SemaphoreType.DMA((3, count)),
+            *RelaySum.scratch(rows, piece.size, BF16),
+        ]
+
+
+def sums_kernel(plan, pieces, arrays, parted, *refs):
     place = Place()
-    total = count + relayed
-    sources, results, buffers = refs[:total], refs[total : 2 * total], refs[2 * total :]
+    sources, helds, refs = refs[:arrays], refs[arrays : arrays + len(pieces)], refs[arrays + len(pieces) :]
+    results, buffers = refs[: arrays + parted], refs[arrays + parted :]
     place.greet()
-    units, relays = [], []
+    units, relays, rest = [], [], []
     for array, start, size, order in plan:
+        source = sources[array].at[:, :, :, :, :, pl.ds(start, size)]
+        unit = Sum(place, source, order, buffers[:5])
         result = results[array].at[:, pl.ds(start, size)]
-        if array < count:
-            source = sources[array].at[:, :, :, :, :, pl.ds(start, size)]
-            unit, buffers = Sum(place, source, order, buffers[:5]), buffers[5:]
-            units.append(unit)
-            own = unit.held
-        else:
-            own, buffers = buffers[0], buffers[1:]
-            own[...] = sources[array][:, :, pl.ds(start, size)]
-        relays.append(RelaySum(place, own, *buffers[:4], result))
-        buffers = buffers[4:]
-    first = len(units)
-    for unit in units:
-        unit.start(0)
-    for relay in relays[first:]:
-        relay.step(0)
+        relays.append(RelaySum(place, unit.held, *buffers[5:9], result))
+        units.append(unit)
+        buffers = buffers[9:]
+    for piece, held in zip(pieces, helds):
+        result = piece.columns(results[arrays + piece.array])
+        rest.append(HeldSum(place, piece, held, buffers[:7], result))
+        buffers = buffers[7:]
+    deep = [unit for unit in rest if unit.piece.deep]
+    simple = [unit for unit in rest if not unit.piece.deep]
+
+    def step(group, number):
+        for item in group:
+            (item if isinstance(item, RelaySum) else item.relay).step(number)
+
+    for unit in units + simple + deep:
+        unit.start(*((0,) if isinstance(unit, Sum) else ()))
+    for unit in simple:
+        unit.finish()
     for unit in units:
         unit.finish(0)
         unit.start(1)
-    for relay in relays[first:]:
-        relay.step(1)
-    for number in (1, 2):
-        for unit, relay in zip(units, relays):
-            unit.finish(number)
-            if number == 1:
-                unit.start(2)
-            else:
-                relay.step(0)
-        for relay in relays[first:]:
-            relay.step(number + 1)
-    for number in (1, 2, 3):
-        for relay in relays[:first]:
-            relay.step(number)
-
-
-def sums(arrays, partly, collective_id):
+    step(simple, 1)
+    for unit in deep:
+        unit.finish()
+    step(simple, 2)
+    for unit in units:
+        unit.finish(1)
+        unit.start(2)
+    step(deep, 1)
+    step(simple, 3)
+    for unit, relay in zip(units, relays):
+        unit.finish(2)
+        relay.step(0)
+    step(deep, 2)
+    step(relays, 1)
+    step(deep, 3)
+    step(relays, 2)
+    step(relays, 3)
+
+
+def sums(arrays, helds, pieces, shapes, collective_id):
     place = Place()
     plan, scratch = [], []
-    for number, array in enumerate([*arrays, *partly]):
+    for number, array in enumerate(arrays):
         rows, columns = array.shape[1:]
         for place_in, (start, size) in enumerate(column_pieces(columns, 2)):
             order = "xb" if place_in == 0 else "bx"
             plan.append((number, start, size, order))
-            if number < len(arrays):
-                scratch += Sum.scratch(place, rows, size, order, array.dtype)
-            else:
-                scratch.append(VMEM((place.as_, rows, size), array.dtype))
+            scratch += Sum.scratch(place, rows, size, order, array.dtype)
             scratch += RelaySum.scratch(rows, size, array.dtype)
-    both = [placed(place, array) for array in arrays] + list(partly)
+    for piece in pieces:
+        scratch += HeldSum.scratch(place, piece, shapes[piece.array][0])
+    both = [placed(place, array) for array in arrays] + list(helds)
     far, whole = pl.BlockSpec(memory_space=pl.ANY), pl.BlockSpec(memory_space=VMEM)
+    out = [jax.ShapeDtypeStruct(array.shape[1:], F32) for array in arrays]
+    out += [jax.ShapeDtypeStruct(shape, F32) for shape in shapes]
     return pl.pallas_call(
-        functools.partial(sums_kernel, plan, len(arrays), len(partly)),
-        in_specs=[far] * len(arrays) + [whole] * len(partly),
-        out_specs=[whole] * len(both),
-        out_shape=[jax.ShapeDtypeStruct(array.shape[-2:], F32) for array in both],
+        functools.partial(sums_kernel, plan, pieces, len(arrays), len(shapes)),
+        in_specs=[far] * len(both),
+        out_specs=[whole] * len(out),
+        out_shape=out,
         scratch_shapes=scratch,
         compiler_params=pltpu.CompilerParams(
             collective_id=collective_id, has_side_effects=True, vmem_limit_bytes=48 * MIB
@@ -1227,6 +1248,96 @@
     devices, high, columns = value.shape
     value = value.reshape(devices, high // rows, rows, columns).transpose(0, 2, 1, 3)
     return value.reshape(devices * rows, high // rows * columns)
+
+
+def middle_kernel(
+    steps, x, att, dy, w_out, gain, w_gate, w_up, w_down,
+    out, d_middle, d_att, g_out, g_gate, g_up, g_down, g_gain,
+    attended, middle, hidden, hidden_turn, result, d_hidden,
+):
+    step = pl.program_id(0)
+    parts, _, width = att.shape
+
+    @pl.when(step == 0)
+    def _():
+        for part in range(parts):
+            attended[:, part * width : (part + 1) * width] = att[part]
+        total = x[...].astype(F32) + dot(attended[...], w_out[...])
+        scale = lax.rsqrt(jnp.mean(total * total, axis=-1, keepdims=True) + EPS)
+        normed = (total * scale * gain[...]).astype(BF16)
+        middle[...] = total
+        result[...] = total
+        hidden[...] = normed
+        hidden_turn[...] = normed.T
+        d_hidden[...] = jnp.zeros_like(d_hidden)
+
+    grad = dy[...]
+    gate = dot(hidden[...], w_gate[...])
+    up = dot(hidden[...], w_up[...])
+    d_inner = against(grad, w_down[...])
+    sigma = jax.nn.sigmoid(gate)
+    silu = gate * sigma
+    inner = (silu * up).astype(BF16)
+    d_gate = (d_inner * up * sigma * (1.0 + gate * (1.0 - sigma))).astype(BF16)
+    d_up = (d_inner * silu).astype(BF16)
+    result[...] += dot(inner, w_down[...])
+    g_down[...] = across(inner, grad).astype(BF16)
+    g_gate[...] = dot(hidden_turn[...], d_gate).astype(BF16)
+    g_up[...] = dot(hidden_turn[...], d_up).astype(BF16)
+    d_hidden[...] += against(d_gate, w_gate[...]) + against(d_up, w_up[...])
+
+    @pl.when(step == steps - 1)
+    def _():
+        out[...] = result[...].astype(BF16)
+        grad_values, grad_gain = norm_back(d_hidden[...], middle[...], gain[...])
+        total = grad_values + dy[...].astype(F32)
+        d_middle[...] = total
+        g_gain[...] = grad_gain[None]
+        d_branch = total.astype(BF16)
+        g_out[...] = across(attended[...], d_branch).astype(BF16)
+        back = against(d_branch, w_out[...]).astype(BF16)
+        for part in range(parts):
+            d_att[part] = back[:, part * width : (part + 1) * width]
+
+
+def between(x, att, dy, w_out, gain, w_gate, w_up, w_down):
+    tokens, dim = x.shape
+    units = w_gate.shape[1]
+    chunk = 512 if units % 512 == 0 else 128
+    whole = lambda value: pl.BlockSpec(value.shape, lambda g: (0,) * len(value.shape))
+    wide = pl.BlockSpec((dim, chunk), lambda g: (0, g))
+    tall = pl.BlockSpec((chunk, dim), lambda g: (g, 0))
+    shape = jax.ShapeDtypeStruct
+    outs = [
+        shape((tokens, dim), BF16),
+        shape((tokens, dim), F32),
+        shape(att.shape, BF16),
+        shape(w_out.shape, BF16),
+        shape(w_gate.shape, BF16),
+        shape(w_up.shape, BF16),
+        shape(w_down.shape, BF16),
+        shape((1, dim), F32),
+    ]
+    return pl.pallas_call(
+        functools.partial(middle_kernel, units // chunk),
+        grid=(units // chunk,),
+        in_specs=[whole(v) for v in (x, att, dy, w_out, gain)] + [wide, wide, tall],
+        out_specs=[whole(v) for v in outs[:4]] + [wide, wide, tall, whole(outs[7])],
+        out_shape=outs,
+        scratch_shapes=[
+            VMEM((tokens, dim), BF16),
+            VMEM((tokens, dim), F32),
+            VMEM((tokens, dim), BF16),
+            VMEM((dim, tokens), BF16),
+            VMEM((tokens, dim), F32),
+            VMEM((tokens, dim), F32),
+        ],
+        compiler_params=pltpu.CompilerParams(vmem_limit_bytes=56 * MIB),
+        cost_estimate=pl.CostEstimate(
+            flops=18 * tokens * dim * units, bytes_accessed=12 * dim * units, transcendentals=0
+        ),
+        name="between",
+    )(x, att, dy, w_out, gain, w_gate, w_up, w_down)
 
 
 def shards(
@@ -1249,12 +1360,13 @@
 
     gains = jnp.pad(jnp.stack([gain_attn, gain_mlp]), ((0, 14), (0, 128 - rows)))
     wide = lambda value: stacked(value, 1)[0]
-    query_full, key_full, value_full, gains, *ready = gathered(
-        [wide(w_query), wide(w_key), wide(w_value), gains],
-        [wide(w_out), wide(spaced(w_gate)), wide(spaced(w_up))],
-        3,
+    padded_down = jnp.pad(w_down, ((0, down_padded - down_rows), (0, 0)))
+    parted = [wide(w_out), wide(spaced(w_gate)), wide(spaced(w_up)), wide(padded_down)]
+    shapes = [value.shape for value in parted]
+    pieces = Piece.all(shapes)
+    (query_full, key_full, value_full, gains), helds = gathered(
+        [wide(w_query), wide(w_key), wide(w_value), gains], parted, pieces, 3
     )
-    late = wide(jnp.pad(w_down, ((0, down_padded - down_rows), (0, 0))))
     tall = lambda value: unstacked(value, rows)
     query_full, key_full, value_full = tall(query_full), tall(key_full), tall(value_full)
     gain_one, gain_two = (gains[:, n, :rows].reshape(width).astype(F32) for n in range(2))
@@ -1278,42 +1390,22 @@
         x_low, gain_one[None], query_full, key_full, value_full,
         first_values.reshape(tokens, width), cosine, sine, parts,
     )
-    (q_all, k_all, v_all, o_all, lse_all, attended), (down_full, *weights) = attend(
-        q, k, v, start, late, ready
+    (q_all, k_all, v_all, o_all, lse_all, attended), (*weights, down_full) = attend(
+        q, k, v, start, helds, pieces, shapes
     )
     out_full, gate_full, up_full = (tall(value) for value in weights)
     down_full = unstacked(down_full, down_padded)
-    attended = attended.transpose(1, 0, 2).reshape(tokens, width)
-
+    output, grad_middle, d_att, grad_out, grad_gate, grad_up, grad_down, grad_gain_two = between(
+        x_low, attended, cotangent.reshape(tokens, width), out_full, gain_two[None],
+        gate_full, up_full, down_full,
+    )
+    grad_gain_two = grad_gain_two[0]
     x_in = x_low.astype(F32)
-    middle = x_in + dot(attended, out_full)
-    scale = lax.rsqrt(jnp.mean(middle * middle, axis=-1, keepdims=True) + EPS)
-    hidden_mlp = (middle * scale * gain_two).astype(BF16)
-    gate = dot(hidden_mlp, gate_full)
-    upward = dot(hidden_mlp, up_full)
-    sigma = jax.nn.sigmoid(gate)
-    silu_gate = gate * sigma
-    inner = (silu_gate * upward).astype(BF16)
-    output = (middle + dot(inner, down_full)).astype(BF16).reshape(inputs.shape)
-    grad_y = cotangent.reshape(tokens, width)
-    grad_down = across(inner, grad_y)
-    grad_inner = against(grad_y, down_full)
-    grad_gate_low = (grad_inner * upward * sigma * (1.0 + gate * (1.0 - sigma))).astype(BF16)
-    grad_up_low = (grad_inner * silu_gate).astype(BF16)
-    grad_gate = across(hidden_mlp, grad_gate_low)
-    grad_up = across(hidden_mlp, grad_up_low)
-    grad_hidden_mlp = against(grad_gate_low, gate_full) + against(grad_up_low, up_full)
-    grad_middle, grad_gain_two = norm_back(grad_hidden_mlp, middle, gain_two)
-    grad_middle = grad_middle + grad_y.astype(F32)
-    grad_branch = grad_middle.astype(BF16)
-    grad_out = across(attended, grad_branch)
-    d_att = against(grad_branch, out_full).astype(BF16)
-    d_att = d_att.reshape(tokens, parts, width // parts).transpose(1, 0, 2)
 
     share = lambda grad: stacked(grad.astype(BF16), devices)
-    (dq, dk, dv), (total_gate, total_up, part_down, part_out) = attend_back(
+    (dq, dk, dv), helds = attend_back(
         d_att, q_all, k_all, v_all, o_all, lse_all, start,
-        [share(grad_gate), share(grad_up), share(grad_down), share(grad_out)],
+        [share(grad_out), share(grad_gate), share(grad_up), share(grad_down)], pieces,
     )
     dq, dk, dv, grad_first = unproject(dq, dk, dv, cosine, sine)
     grad_query_w = across(hidden_in, dq)
@@ -1324,10 +1416,12 @@
     grad_x = grad_x + grad_middle
     gains_grad = jnp.stack([grad_gain_one, grad_gain_two]).reshape(2, devices, rows)
     gains_grad = jnp.pad(gains_grad.transpose(1, 0, 2), ((0, 0), (0, 6), (0, 128 - rows)))
-    total_query, total_key, total_value, gains_total, total_down, total_out = sums(
+    (
+        total_query, total_key, total_value, gains_total,
+        total_out, total_gate, total_up, total_down,
+    ) = sums(
         [share(grad_query_w), share(grad_key_w), share(grad_value_w), gains_grad],
-        [part_down, part_out],
-        4,
+        helds, pieces, shapes, 4,
     )
     low = lambda total: unstacked(total[None], rows)
 
@@ -1336,7 +1430,7 @@
         return total[:, :, :down_rows].reshape(rows, devices * down_rows)
 
     return (
-        output,
+        output.reshape(inputs.shape),
         grad_x.reshape(inputs.shape),
         grad_first.reshape(inputs.shape),
         low(total_query),

time: 602 us -> 508 us (0.84); the launches traced: 595 us -> 507 us
  matrix products: 78.5 us -> 15.7 us
  Pallas kernels: 469 us -> 455 us
  local copies, waits for them, and re-layouts: 37.2 us -> 27.7 us
    dot_general x18 -> x6, matrix products: 78.5 us -> 15.7 us  [dot(): lax.dot_general(left, right, (((left_dim,), (right_dim,)), ((), ())), pre...]
    pallas_call x4 -> x5, Pallas kernels: 459 us -> 445 us  [the longest x1 125 us: attend(): pl.pallas_call(functools.partial(forward_kernel, parts, heads, pieces, le...]
    unnamed x106 -> x82, local copies, waits for them, and re-layouts: 20.6 us -> 17.2 us
where the time goes in v3:
time: 508 us; the launch traced here: 507 us
  Pallas kernels  455 us (90%)
  local copies, waits for them, and re-layouts  27.7 us (5%)
  matrix products  15.7 us (3%)
  other arithmetic  8.16 us (2%)
    pallas_call x1, Pallas kernels, attend(): pl.pallas_call(functools.partial(forward_kernel, parts, heads, pieces, le...  125 us
    pallas_call x1, Pallas kernels, attend_back(): pl.pallas_call(functools.partial(backward_kernel, parts, heads, pieces, l...  108 us
    pallas_call x1, Pallas kernels, sums(): pl.pallas_call(functools.partial(sums_kernel, plan, pieces, len(arrays),...  86.6 us
    pallas_call x1, Pallas kernels, gathered(): pl.pallas_call(functools.partial(gather_kernel, plan, pieces, len(arrays)...  80.9 us
    pallas_call x1, Pallas kernels, between(): pl.pallas_call(functools.partial(middle_kernel, units // chunk), grid=(un...  45.1 us
    unnamed x82, local copies, waits for them, and re-layouts  17.2 us
    dot_general x6, matrix products, dot(): lax.dot_general(left, right, (((left_dim,), (right_dim,)), ((), ())), pre...  15.7 us

profile of v3, /device:TPU:0, one launch (start us, length us, event | category | flops | bytes accessed | tf_op | source)
XLA Modules:
  0.0 507.3 jit_solution(1851572201175952112)
XLA Ops:
  2.2 1.5 fusion.9
  3.7 1.3 fusion.17.refs_3_
  7.3 1.0 squeeze_reshape_transpose_reshape_reshape.6.refs_5_
  9.0 1.0 squeeze_reshape_transpose_reshape_reshape.7.refs_6_
  10.0 80.9 %gathered.1 = (bf16[2,2,4,2,32,1024]{5,4,3,2,1,0:T(8,128)(2,1)}, bf16[2,2,4,2,32,1024]{5,4,3,2,1,0:T(8,128)(2,1)}, bf16[2,2,4,2,32,1024]{5,4,3,2,1,0:T(8,128)(2,...) custom-call(bf16[32,1024]{1,0:T(8,128)(2,1)} %refs_0_.1, ...), custom_call_target="tpu_custom_call" | custom-call | bytes 6422528 | tf_op jit(solution)/shard_map/gathered/pallas_call | solution.py:883
  92.8 1.6 copy-done.2
  94.4 1.6 copy-done.15
  95.9 1.6 copy-done.17
  97.6 6.2 %project.1 = (bf16[8,512,128]{2,1,0:T(8,128)(2,1)S(1)}, bf16[8,512,128]{2,1,0:T(8,128)(2,1)S(1)}, bf16[8,512,128]{2,1,0:T(8,128)(2,1)S(1)}, bf16[512,1024]{1,0:T(8,128)(2,1)S(1)}) custom-call(bf16[512,1024]{1,0:T(8,128)(2,1)S(1)} %bitcast.68, f32[1,1024]{1,0:T(1,128)S(1)} %reshape.171.gain, bf16[1024,1024]{1,0:T(8,128)(2,1)S(1)} %bitcast.77, ...), custom_call_target="tpu_custom_call" | custom-call | flops 3221225472 | bytes 8388608 | tf_op jit(solution)/shard_map/project/pallas_call | solution.py:85
  103.8 1.0 copy-done.28
  104.8 1.0 copy-done.30
  105.8 1.0 copy-done.31
  106.7 1.0 copy-done.32
  107.8 124.6 %attend.1 = (bf16[8,512,128]{2,1,0:T(8,128)(2,1)S(1)}, bf16[8,512,128]{2,1,0:T(8,128)(2,1)}, bf16[8,512,128]{2,1,0:T(8,128)(2,1)}, f32[8,128,512]{2,1,0:T(8,128)...) custom-call(bf16[8,512,128]{2,1,0:T(8,128)(2,1)} %copy-done.30, ...), custom_call_target="tpu_custom_call" | custom-call | flops 17179869184 | bytes 8388608 | tf_op jit(solution)/shard_map/attend/pallas_call | solution.py:354
  232.4 1.0 copy-done.33
  234.0 45.1 %between.1 = (bf16[512,1024]{1,0:T(8,128)(2,1)}, f32[512,1024]{1,0:T(8,128)}, bf16[8,512,128]{2,1,0:T(8,128)(2,1)}, bf16[1024,1024]{1,0:T(8,128)(2,1)}, bf16[102...) custom-call(bf16[512,1024]{1,0:T(8,128)(2,1)} %bitcast.67, ...), custom_call_target="tpu_custom_call" | custom-call | flops 28991029248 | bytes 37748736 | tf_op jit(solution)/shard_map/between/pallas_call | solution.py:1321
  279.6 1.3 reduce.3
  281.0 107.6 %attend_back.1 = (bf16[8,512,128]{2,1,0:T(8,128)(2,1)}, bf16[8,512,128]{2,1,0:T(8,128)(2,1)}, bf16[8,512,128]{2,1,0:T(8,128)(2,1)}, bf16[4,32,1024]{2,1,0:T(8,12...) custom-call(bf16[8,512,128]{2,1,0:T(8,128)(2,1)} %get-tuple-element., ...), custom_call_target="tpu_custom_call" | custom-call | flops 42949672960 | bytes 10485760 | tf_op jit(solution)/shard_map/attend_back/pallas_call | solution.py:545
  388.7 1.2 copy-done.4
  389.9 1.2 copy-done.5
  391.1 1.2 copy-done.6
  392.3 3.5 unproject.1
  395.8 3.3 fusion.20
  399.2 1.3 fusion.21
  401.1 1.8 fusion.8
  402.9 1.9 fusion.7
  405.0 4.0 convolution_convert_fusion
  409.0 2.7 convolution_convert_fusion.1
  411.7 2.6 convolution_convert_fusion.2
  414.4 86.6 %sums.1 = (f32[32,1024]{1,0:T(8,128)S(1)}, f32[32,1024]{1,0:T(8,128)S(1)}, f32[32,1024]{1,0:T(8,128)S(1)}, f32[8,128]{1,0:T(8,128)S(1)}, f32[32,1024]{1,0:T(8,12...) custom-call(bf16[2,2,4,2,32,1024]{5,4,3,2,1,0:T(8,128)(2,1)} %bitcast.83, ...), custom_call_target="tpu_custom_call" | custom-call | bytes 12713984 | tf_op jit(solution)/shard_map/sums/pallas_call | solution.py:1222
  502.4 1.0 reshape.169
  503.7 1.0 reshape.170
  (103 shorter events, 12.5 us)
Async XLA Ops:
  0.6 5.1 %copy-start.38 = (bf16[88,1024]{1,0:T(8,128)(2,1)S(1)}, bf16[88,1024]{1,0:T(8,128)(2,1)}, u32[]{:S(2)}) copy-start(bf16[88,1024]{1,0:T(8,128)(2,1)} %param.23) | copy-start | bytes 540676
  0.7 6.0 %copy-start.36 = (bf16[32,2816]{1,0:T(8,128)(2,1)S(1)}, bf16[32,2816]{1,0:T(8,128)(2,1)}, u32[]{:S(2)}) copy-start(bf16[32,2816]{1,0:T(8,128)(2,1)} %param.21) | copy-start | bytes 540676
  3.7 4.6 copy-start.37
  5.2 102.5 %copy-start.14 = (s32[4096]{0:T(1024)}, s32[4096]{0:T(1024)S(1)}, u32[]{:S(2)}) copy-start(s32[4096]{0:T(1024)S(1)} %select_reduce_fusion) | copy-start | bytes 49156
  6.6 86.1 %copy-start = (bf16[1,512,1024]{2,1,0:T(8,128)(2,1)S(1)}, bf16[1,512,1024]{2,1,0:T(8,128)(2,1)}, u32[]{:S(2)}) copy-start(bf16[1,512,1024]{2,1,0:T(8,128)(2,1)} %param.13) | copy-start | bytes 3145732
  6.6 86.1 %copy-start.18 = (bf16[1,512,1024]{2,1,0:T(8,128)(2,1)S(1)}, bf16[1,512,1024]{2,1,0:T(8,128)(2,1)}, u32[]{:S(2)}) copy-start(bf16[1,512,1024]{2,1,0:T(8,128)(2,1)} %param.14) | copy-start | bytes 3145732
  92.8 1.6 copy-start.2
  94.4 1.6 copy-start.15
  95.9 1.6 copy-start.17
  97.5 10.2 %copy-start.21 = (bf16[4,2,32,1536]{3,2,1,0:T(8,128)(2,1)S(1)}, bf16[4,2,32,1536]{3,2,1,0:T(8,128)(2,1)}, u32[]{:S(2)}) copy-start(bf16[4,2,32,1536]{3,2,1,0:T(8,128)(2,1)} %get-tuple-element.75.refs_1_) | copy-start | bytes 2359300
  97.5 10.2 %copy-start.22 = (bf16[4,2,32,1536]{3,2,1,0:T(8,128)(2,1)S(1)}, bf16[4,2,32,1536]{3,2,1,0:T(8,128)(2,1)}, u32[]{:S(2)}) copy-start(bf16[4,2,32,1536]{3,2,1,0:T(8,128)(2,1)} %get-tuple-element.76.refs_2_) | copy-start | bytes 2359300
  97.5 10.2 %copy-start.23 = (bf16[2,4,32,1536]{3,2,1,0:T(8,128)(2,1)S(1)}, bf16[2,4,32,1536]{3,2,1,0:T(8,128)(2,1)}, u32[]{:S(2)}) copy-start(bf16[2,4,32,1536]{3,2,1,0:T(8,128)(2,1)} %get-tuple-element.77.refs_3_) | copy-start | bytes 2359300
  97.5 10.2 %copy-start.24 = (bf16[4,2,32,1536]{3,2,1,0:T(8,128)(2,1)S(1)}, bf16[4,2,32,1536]{3,2,1,0:T(8,128)(2,1)}, u32[]{:S(2)}) copy-start(bf16[4,2,32,1536]{3,2,1,0:T(8,128)(2,1)} %get-tuple-element.78.refs_4_) | copy-start | bytes 2359300
  97.5 10.2 %copy-start.25 = (bf16[4,96,512]{2,1,0:T(8,128)(2,1)S(1)}, bf16[4,96,512]{2,1,0:T(8,128)(2,1)}, u32[]{:S(2)}) copy-start(bf16[4,96,512]{2,1,0:T(8,128)(2,1)} %get-tuple-element.79.refs_5_) | copy-start | bytes 1179652
  97.6 10.2 %copy-start.26 = (bf16[4,96,512]{2,1,0:T(8,128)(2,1)S(1)}, bf16[4,96,512]{2,1,0:T(8,128)(2,1)}, u32[]{:S(2)}) copy-start(bf16[4,96,512]{2,1,0:T(8,128)(2,1)} %get-tuple-element.80.refs_6_) | copy-start | bytes 1179652
  97.6 10.2 %copy-start.27 = (bf16[4,32,1024]{2,1,0:T(8,128)(2,1)S(1)}, bf16[4,32,1024]{2,1,0:T(8,128)(2,1)}, u32[]{:S(2)}) copy-start(bf16[4,32,1024]{2,1,0:T(8,128)(2,1)} %get-tuple-element.74.refs_0_) | copy-start | bytes 786436
  388.7 1.2 copy-start.4
  389.9 1.2 copy-start.5
  395.8 3.3 copy-start.19
  395.8 3.3 copy-start.16
  399.2 1.3 copy-start.1
  399.2 1.9 copy-start.3
  401.1 1.8 copy-start.35
  404.9 4.0 copy-start.20
  405.0 4.0 copy-start.29
  411.7 2.7 copy-start.7
  411.7 2.7 copy-start.8
  411.7 2.7 copy-start.9
  411.7 2.7 copy-start.10
  411.7 2.7 copy-start.11
  411.7 2.7 copy-start.12
  411.7 2.7 copy-start.13
  (7 other events, 6.7 us)

commit v4 on v3

--- a/solution.py
+++ b/solution.py
@@ -51,89 +51,6 @@
         pltpu.roll(values, HEAD_DIM // 2, 1),
     )
     return values * cosine + other * sine
-
-
-def project_kernel(width, x, gain, wq, wk, wv, first, cosine, sine, q_out, k_out, v_out, h_out):
-    @pl.when(pl.program_id(0) == 0)
-    def _():
-        values = x[...].astype(F32)
-        scale = lax.rsqrt(jnp.mean(values * values, axis=-1, keepdims=True) + EPS)
-        h_out[...] = (values * scale * gain[...]).astype(BF16)
-
-    hidden = h_out[...]
-    cos, sin = cosine[...], sine[...]
-    for weight, out, scale in ((wq, q_out, HEAD_DIM**-0.5), (wk, k_out, 1.0)):
-        raw = dot(hidden, weight[...])
-        for part in range(2):
-            done = turned(raw[:, part * 128 : part * 128 + 128], cos, sin) * scale
-            for piece in range(128 // width):
-                out[part * (128 // width) + piece] = done[
-                    :, piece * width : (piece + 1) * width
-                ].astype(BF16)
-    mixed = (0.5 * dot(hidden, wv[...]) + 0.5 * first[...].astype(F32)).astype(BF16)
-    for piece in range(256 // width):
-        v_out[piece] = mixed[:, piece * width : (piece + 1) * width]
-
-
-def project(x, gain, wq, wk, wv, first, cosine, sine, parts):
-    tokens, dim = x.shape
-    width = dim // parts
-    whole = lambda shape: pl.BlockSpec(shape, lambda g: (0,) * len(shape))
-    cols = lambda rows: pl.BlockSpec((rows, 256), lambda g: (0, g))
-    out = pl.BlockSpec((256 // width, tokens, width), lambda g: (g, 0, 0))
-    split = jax.ShapeDtypeStruct((parts, tokens, width), BF16)
-    return pl.pallas_call(
-        functools.partial(project_kernel, width),
-        grid=(dim // 256,),
-        in_specs=[
-            whole((tokens, dim)),
-            whole((1, dim)),
-            cols(dim),
-            cols(dim),
-            cols(dim),
-            cols(tokens),
-            whole((tokens, 128)),
-            whole((tokens, 128)),
-        ],
-        out_specs=[out, out, out, whole((tokens, dim))],
-        out_shape=[split, split, split, jax.ShapeDtypeStruct((tokens, dim), BF16)],
-        compiler_params=pltpu.CompilerParams(vmem_limit_bytes=40 * MIB),
-        cost_estimate=pl.CostEstimate(
-            flops=6 * tokens * dim * dim, bytes_accessed=16 * tokens * dim, transcendentals=0
-        ),
-        name="project",
-    )(x, gain, wq, wk, wv, first, cosine, sine)
-
-
-def unproject_kernel(width, dq, dk, dv, cosine, sine, q_out, k_out, v_out, first_out):
-    cos, sin = cosine[...], sine[...]
-    for part in range(2):
-        lanes = slice(part * 128, part * 128 + 128)
-        picks = range(part * (128 // width), (part + 1) * (128 // width))
-        join = lambda ref: jnp.concatenate([ref[p] for p in picks], axis=1).astype(F32)
-        q_out[:, lanes] = turned(join(dq), cos, -sin).astype(BF16)
-        k_out[:, lanes] = turned(join(dk), cos, -sin).astype(BF16)
-        value = 0.5 * join(dv)
-        first_out[:, lanes] = value
-        v_out[:, lanes] = value.astype(BF16)
-
-
-def unproject(dq, dk, dv, cosine, sine):
-    parts, tokens, width = dq.shape
-    dim = parts * width
-    split = pl.BlockSpec((256 // width, tokens, width), lambda g: (g, 0, 0))
-    table = pl.BlockSpec((tokens, 128), lambda g: (0, 0))
-    cols = pl.BlockSpec((tokens, 256), lambda g: (0, g))
-    low = jax.ShapeDtypeStruct((tokens, dim), BF16)
-    return pl.pallas_call(
-        functools.partial(unproject_kernel, width),
-        grid=(dim // 256,),
-        in_specs=[split, split, split, table, table],
-        out_specs=[cols, cols, cols, cols],
-        out_shape=[low, low, low, jax.ShapeDtypeStruct((tokens, dim), F32)],
-        compiler_params=pltpu.CompilerParams(vmem_limit_bytes=40 * MIB),
-        name="unproject",
-    )(dq, dk, dv, cosine, sine)
 
 
 def greet(parts, me):
@@ -211,9 +128,6 @@
 
     for index, (source, target) in enumerate(pairs):
         pltpu.make_async_copy(source.at[me], target.at[me], in_recv.at[index, me]).start()
-    pl.when(own == 0)(lambda: start_cross((1, 2)))
-    pl.when(own == 1)(lambda: start_cross((0,)))
-
     def start_near(peer):
         @pl.when(peer != me)
         def _():
@@ -221,6 +135,8 @@
                 moved(index, peer).start()
 
     over(own * half, start_near)
+    pl.when(own == 0)(lambda: start_cross((1, 2)))
+    pl.when(own == 1)(lambda: start_cross((0,)))
 
     def got(index, block):
         arrive(pairs[index][1].at[block], in_recv.at[index, block])
@@ -268,11 +184,14 @@
 
         @pl.when((row == half) & (own == 1))
         def _():
+            lax.fori_loop(0, half, lambda block, _: got_keys(block) or 0, 0)
+
+        @pl.when((row == half * 3 // 4) & (own == 1))
+        def _():
             sent_cross((0,))
             start_cross((1, 2))
-            lax.fori_loop(0, half, lambda block, _: got_keys(block) or 0, 0)
-
-        @pl.when((row == 2 * half) & (own == 0))
+
+        @pl.when((row == half + half // 2) & (own == 0))
         def _():
             sent_cross((1, 2))
             start_cross((0,))
@@ -414,13 +333,13 @@
     def moved(peer):
         return send(d_in.at[peer], d_all.at[me], in_send.at[peer], in_recv.at[me], peer)
 
-    over((1 - own) * half, lambda peer: moved(peer).start())
     pltpu.make_async_copy(d_in.at[me], d_all.at[me], in_recv.at[me]).start()
 
     def start_near(peer):
         pl.when(peer != me)(lambda: moved(peer).start())
 
     over(own * half, start_near)
+    over((1 - own) * half, lambda peer: moved(peer).start())
     sends = ((dq_send, dq_got), (dk_send, dk_got), (dv_send, dv_got))
 
     def give(index, block):
@@ -696,6 +615,34 @@
             self.near().wait_send()
 
 
+class Direct:
+    def __init__(self, place, source, target, sems):
+        self.p, self.source, self.target, self.sems = place, source, target, sems
+
+    def copies(self):
+        p = self.p
+        return [
+            remote(
+                self.source, self.target.at[p.a],
+                self.sems.at[0, s], self.sems.at[1, s], p.device(a=index),
+            )
+            for s, index in p.peers("a")
+        ]
+
+    def local(self):
+        return pltpu.make_async_copy(self.source, self.target.at[self.p.a], self.sems.at[0, 3])
+
+    def step(self, number):
+        if number == 0:
+            self.local().start()
+            for copy in self.copies():
+                copy.start()
+        elif number == 3:
+            self.local().wait()
+            for copy in self.copies():
+                copy.wait()
+
+
 class Piece:
     def __init__(self, array, start, size, order, deep):
         self.array, self.start, self.size, self.order, self.deep = array, start, size, order, deep
@@ -775,7 +722,7 @@
     return pltpu.SemaphoreType.DMA((3, place.xs + place.bs - 1))
 
 
-RELAY_SEMAPHORES = (2, 3)
+RELAY_SEMAPHORES = (2, 4)
 
 
 class InRows:
@@ -814,27 +761,67 @@
         return done
 
 
-def gather_kernel(plan, pieces, arrays, parted, *refs):
+class TotalSum:
+    def __init__(self, place, mine, got, sems):
+        self.place, self.mine, self.got, self.sems = place, mine, got, sems
+
+    def slots(self, number):
+        p = self.place
+        devices = [[p.device(core=1 - p.core)]]
+        devices += [[p.device(**{axis: index}) for _, index in p.peers(axis)] for axis in "xba"]
+        return sum(len(some) for some in devices[:number]), devices[number]
+
+    def copies(self, number):
+        base, devices = self.slots(number)
+        return [
+            remote(
+                self.mine, self.got.at[base + n],
+                self.sems.at[0, base + n], self.sems.at[1, base + n], device,
+            )
+            for n, device in enumerate(devices)
+        ]
+
+    def start(self, number):
+        for copy in self.copies(number):
+            copy.start()
+
+    def then(self, number):
+        for copy in self.copies(number):
+            copy.wait()
+        base, devices = self.slots(number)
+        for slot in range(len(devices)):
+            self.mine[...] += self.got[base + slot]
+        if number < 3:
+            self.start(number + 1)
+
+
+def opening_kernel(
+    plan, pieces, parted,
+    x, first, cosine, sine, gains, w_query, w_key, w_value, *refs,
+):
+    shares, refs = refs[:parted], refs[parted:]
+    q_out, k_out, v_out, hidden, gains_total, *fulls = refs[:8]
+    helds, refs = refs[8 : 8 + len(pieces)], refs[8 + len(pieces) :]
+    got_gains, gain_sems, relay_sems, *sems = refs
     place = Place()
-    total = arrays + parted
-    sources, refs = refs[:total], refs[total:]
-    fulls, helds, (relay_sems, *sems) = (
-        refs[:arrays], refs[arrays : arrays + len(pieces)], refs[arrays + len(pieces) :]
-    )
+    parts, tokens, width = q_out.shape
+    dim = parts * width
     place.greet()
-    whole, relays = [], []
+    gains_total[...] = gains[...]
+    total = TotalSum(place, gains_total, got_gains, gain_sems)
+    units, relays = [], []
+    sources = (w_query, w_key, w_value)
     for number, (array, start, size, order) in enumerate(plan):
         views = Spread.views_of(place, fulls[array].at[:, :, :, :, :, pl.ds(start, size)], order)
         relays.append(
-            Relay(place, sources[array].at[:, pl.ds(start, size)], views[0], relay_sems.at[number])
+            Direct(place, sources[array].at[:, pl.ds(start, size)], views[0], relay_sems.at[number])
         )
-        whole.append(Spread(place, views, order, sems[number]))
+        units.append(Spread(place, views, order, sems[number]))
     deep, flat_relays, deep_relays = [], [], []
     for number, (piece, held) in enumerate(zip(pieces, helds)):
         view = piece.along_a(place, held)
         index = len(plan) + number
-        source = piece.columns(sources[arrays + piece.array])
-        relay = Relay(place, source, view, relay_sems.at[index])
+        relay = Relay(place, piece.columns(shares[piece.array]), view, relay_sems.at[index])
         (deep_relays if piece.deep else flat_relays).append(relay)
         if piece.deep:
             deep.append(Spread(place, [view], piece.order, sems[index]))
@@ -843,61 +830,119 @@
         for relay in group:
             relay.step(number)
 
+    def then(some, number):
+        for unit in some:
+            unit.then(number)
+
+    def weight(array, start, size):
+        full = fulls[array]
+        rows, columns = full.shape[-2:]
+        fold = dim // columns
+        value = full[:, :, :, :, :, start % columns : start % columns + size]
+        if fold > 1:
+            share = rows // fold
+            part = start // columns * share
+            value = value.astype(F32)[:, :, :, :, part : part + share]
+        return value.reshape(dim, size).astype(BF16)
+
+    def project(array):
+        for start in range(0, dim, 256):
+            raw = dot(hidden[...], weight(array, start, 256))
+            if array == 2:
+                raw = 0.5 * raw + 0.5 * first[:, start : start + 256].astype(F32)
+            for begin in range(0, 256, 128):
+                value = raw[:, begin : begin + 128]
+                if array < 2:
+                    value = turned(value, cosine[...], sine[...])
+                if array == 0:
+                    value = value * HEAD_DIM**-0.5
+                for lane in range(0, 128, width):
+                    out = (q_out, k_out, v_out)[array]
+                    out[(start + begin + lane) // width] = value[:, lane : lane + width].astype(BF16)
+
+    half = len(units) // 2
+    line = deep_relays + flat_relays
+
+    def tick(number):
+        for back in (3, 2, 1, 0):
+            index = number - back
+            if 0 <= index < len(line):
+                line[index].step(back)
+                if back == 3 and index < len(deep):
+                    deep[index].start(0)
+
     step(relays, 0)
+    total.start(0)
     step(relays, 1)
-    step(deep_relays, 0)
+    tick(0)
     step(relays, 2)
-    for relay, unit in zip(relays, whole):
+    total.then(0)
+    for relay, unit in zip(relays, units):
         relay.step(3)
         unit.start(0)
-    step(deep_relays, 1)
-    step(flat_relays, 0)
-    for unit in whole:
-        unit.then(0)
-    step(deep_relays, 2)
-    for relay, unit in zip(deep_relays, deep):
-        relay.step(3)
-        unit.start(0)
-    step(flat_relays, 1)
-    for unit in whole:
-        unit.then(1)
-    step(flat_relays, 2)
-    for unit in whole:
-        unit.then(2)
-    step(flat_relays, 3)
+    tick(1)
+    total.then(1)
+    then(units[:half], 0)
+    tick(2)
+    then(units[half:], 0)
+    total.then(2)
+    tick(3)
+    total.then(3)
+    values = x[...].astype(F32)
+    scale = lax.rsqrt(jnp.mean(values * values, axis=-1, keepdims=True) + EPS)
+    hidden[...] = (values * scale * gains_total[0:1]).astype(BF16)
+    tick(4)
+    then(units[:half], 1)
+    tick(5)
+    then(units[half:], 1)
+    for array in range(3):
+        then([unit for unit, piece in zip(units, plan) if piece[0] == array], 2)
+        project(array)
+        tick(6 + array)
+    for number in range(9, len(line) + 3):
+        tick(number)
     for unit in deep:
         unit.finish(0)
 
 
-def gathered(arrays, parted, pieces, collective_id):
+def opening(x, first, cosine, sine, gains, weights, parted, pieces, parts, collective_id):
     place = Place()
     xs, as_, bs = place.xs, place.as_, place.bs
+    tokens, dim = x.shape
     plan = []
-    for number, array in enumerate(arrays):
-        for place_in, (start, size) in enumerate(column_pieces(array.shape[1], 2)):
-            plan.append((number, start, size, "xb" if place_in == 0 else "bx"))
-    full = [jax.ShapeDtypeStruct((xs, 2, as_, bs, *array.shape), array.dtype) for array in arrays]
-    full += [piece.held(place, parted[piece.array].shape[0]) for piece in pieces]
-    far = pl.BlockSpec(memory_space=pl.ANY)
+    for number, array in enumerate(weights):
+        for start, size in column_pieces(array.shape[1], 2):
+            plan.append((number, start, size, "xb" if len(plan) % 2 == 1 else "bx"))
+    shape = jax.ShapeDtypeStruct
+    near = [shape((parts, tokens, dim // parts), BF16)] * 3
+    near += [shape((tokens, dim), BF16), shape(gains.shape, F32)]
+    near += [shape((xs, 2, as_, bs, *array.shape), array.dtype) for array in weights]
+    held = [piece.held(place, parted[piece.array].shape[0]) for piece in pieces]
+    far, whole = pl.BlockSpec(memory_space=pl.ANY), pl.BlockSpec(memory_space=VMEM)
     count = len(plan) + len(pieces)
+    peers = 1 + (xs - 1) + (bs - 1) + (as_ - 1)
     results = pl.pallas_call(
-        functools.partial(gather_kernel, plan, pieces, len(arrays), len(parted)),
-        in_specs=[far] * (len(arrays) + len(parted)),
-        out_specs=[far] * len(full),
-        out_shape=full,
+        functools.partial(opening_kernel, plan, pieces, len(parted)),
+        in_specs=[whole] * 5 + [far] * (3 + len(parted)),
+        out_specs=[whole] * len(near) + [far] * len(held),
+        out_shape=near + held,
         scratch_shapes=[
+            VMEM((peers, *gains.shape), F32),
+            pltpu.SemaphoreType.DMA((2, peers)),
             pltpu.SemaphoreType.DMA((count, *RELAY_SEMAPHORES)),
             *[spread_semaphores(place)] * count,
         ],
-        compiler_params=pltpu.CompilerParams(collective_id=collective_id, has_side_effects=True),
+        compiler_params=pltpu.CompilerParams(
+            collective_id=collective_id, has_side_effects=True, vmem_limit_bytes=48 * MIB
+        ),
         cost_estimate=pl.CostEstimate(
-            flops=0, bytes_accessed=sum(array.size for array in arrays) * 64, transcendentals=0
+            flops=6 * tokens * dim * dim, bytes_accessed=20 * dim * dim, transcendentals=0
         ),
-        name="gathered",
-    )(*arrays, *parted)
+        name="opening",
+    )(x, first, cosine, sine, gains, *weights, *parted)
     devices = xs * 2 * as_ * bs
-    gives = [result.reshape(devices, *result.shape[4:]) for result in results[: len(arrays)]]
-    return gives, results[len(arrays) :]
+    fulls = [value.reshape(devices, *value.shape[4:]) for value in results[5:8]]
+    return results[:4], results[4], fulls, results[8:]
 
 
 def add_up(mine, others):
@@ -979,10 +1024,46 @@
         ]
 
 
+class DirectSum:
+    def __init__(self, place, own, got, sems, result):
+        self.p, self.own, self.got, self.sems, self.result = place, own, got, sems, result
+
+    def copies(self):
+        p = self.p
+        return [
+            remote(
+                self.own.at[index], self.got.at[s],
+                self.sems.at[0, s], self.sems.at[1, s], p.device(a=index),
+            )
+            for s, index in p.peers("a")
+        ]
+
+    def step(self, number):
+        if number == 0:
+            for copy in self.copies():
+                copy.start()
+        elif number == 3:
+            total = self.own[self.p.a].astype(F32)
+            for slot, copy in enumerate(self.copies()):
+                copy.wait()
+                total += self.got[slot].astype(F32)
+            self.result[...] = total
+
+    @staticmethod
+    def scratch(place, rows, columns, dtype):
+        return [
+            VMEM((place.as_ - 1, rows, columns), dtype),
+            pltpu.SemaphoreType.DMA((2, place.as_ - 1)),
+        ]
+
+
 class Sum:
     def __init__(self, place, source, order, buffers):
         self.place, self.order, self.source = place, order, source
         self.own, self.got0, self.got1, self.got2, self.sems = buffers
+        self.copied = self.own is not None
+        if not self.copied:
+            self.own = source.at[:, place.core]
 
     @property
     def held(self):
@@ -1023,12 +1104,12 @@
     def start(self, number):
         for copy in self.copies(number):
             copy.start()
-        if number == 0:
+        if number == 0 and self.copied:
             self.local().start()
 
     def finish(self, number):
         p = self.place
-        if number == 0:
+        if number == 0 and self.copied:
             self.local().wait()
         for copy in self.copies(number):
             copy.wait_recv()
@@ -1041,14 +1122,13 @@
             add_up(mine, [got.at[slot] for slot in range(len(p.peers(self.order[number - 1])))])
 
     @staticmethod
-    def scratch(place, rows, size, order, dtype):
+    def scratch(place, rows, size, order, dtype, copied=True):
         xs, as_, bs = place.xs, place.as_, place.bs
         shapes = {
             "x": ((xs - 1, as_, bs, rows, size), (xs - 1, as_, rows, size)),
             "b": ((bs - 1, xs, as_, rows, size), (bs - 1, as_, rows, size)),
         }
-        return [
-            VMEM((xs, as_, bs, rows, size), dtype),
+        return [VMEM((xs, as_, bs, rows, size), dtype)] * copied + [
             VMEM((xs, as_, bs, rows, size), dtype),
             VMEM(shapes[order[0]][0], dtype),
             VMEM(shapes[order[1]][1], dtype),
@@ -1137,7 +1217,7 @@
         for copy in copies:
             copy.wait_recv()
             copy.wait_send()
-        if copies:
+        if len(copies):
             add_up(self.own, [self.got.at[slot] for slot in range(len(copies))])
         self.relay.step(0)
 
@@ -1153,86 +1233,196 @@
         ]
 
 
-def sums_kernel(plan, pieces, arrays, parted, *refs):
+def closing_kernel(
+    plan, pieces, rows, fold, parted,
+    dq, dk, dv, w_query, w_key, w_value, hidden, x, d_middle, gains, cosine, sine, gain, *refs,
+):
+    helds, refs = refs[: len(pieces)], refs[len(pieces) :]
+    grad_first, grad_x, gains_total, *refs = refs
+    results, buffers = refs[: 3 + parted], refs[3 + parted :]
+    slopes, weights, hidden_in, x_in, middle, hidden_turn, d_hidden, got_gains, gain_sems = buffers[:9]
+    loads, buffers = buffers[9], buffers[10:]
     place = Place()
-    sources, helds, refs = refs[:arrays], refs[arrays : arrays + len(pieces)], refs[arrays + len(pieces) :]
-    results, buffers = refs[: arrays + parted], refs[arrays + parted :]
+    parts, tokens, width = dq.shape
+    dim = parts * width
+    devices = dim // rows
     place.greet()
-    units, relays, rest = [], [], []
+    copies = [
+        pltpu.make_async_copy(source, target, loads.at[n])
+        for n, (source, target) in enumerate(
+            (
+                (hidden, hidden_in), (dq, slopes.at[0]), (w_query, weights.at[0]),
+                (dk, slopes.at[1]), (w_key, weights.at[1]), (dv, slopes.at[2]),
+                (w_value, weights.at[2]), (x, x_in), (d_middle, middle),
+            )
+        )
+    ]
+    for copy in copies:
+        copy.start()
+    units, relays, grads, rest = [], [], [], []
     for array, start, size, order in plan:
-        source = sources[array].at[:, :, :, :, :, pl.ds(start, size)]
-        unit = Sum(place, source, order, buffers[:5])
+        source = buffers[0]
+        unit = Sum(place, source, order, (None, *buffers[1:5]))
         result = results[array].at[:, pl.ds(start, size)]
-        relays.append(RelaySum(place, unit.held, *buffers[5:9], result))
+        relays.append(DirectSum(place, unit.held, *buffers[5:7], result))
         units.append(unit)
-        buffers = buffers[9:]
+        grads.append(source)
+        buffers = buffers[7:]
     for piece, held in zip(pieces, helds):
-        result = piece.columns(results[arrays + piece.array])
+        result = piece.columns(results[3 + piece.array])
         rest.append(HeldSum(place, piece, held, buffers[:7], result))
         buffers = buffers[7:]
     deep = [unit for unit in rest if unit.piece.deep]
     simple = [unit for unit in rest if not unit.piece.deep]
+    total = TotalSum(place, gains_total, got_gains, gain_sems)
+    for unit in simple + deep:
+        unit.start()
+
+    def low(array, first, size):
+        done = []
+        for start in range(first, first + size, 128):
+            picks = range(start // width, (start + 128) // width)
+            value = jnp.concatenate([slopes[array, n] for n in picks], axis=1).astype(F32)
+            if array < 2:
+                value = turned(value, cosine[...], -sine[...])
+            else:
+                value = 0.5 * value
+                grad_first[:, start : start + 128] = value
+            done.append(value.astype(BF16))
+        return jnp.concatenate(done, axis=1)
+
+    def compute(index):
+        array, start, size, _ = plan[index]
+        blocks = []
+        for part in range(fold):
+            first = part * (dim // fold) + start
+            slope = low(array, first, size)
+            blocks.append(dot(hidden_turn[...], slope).reshape(devices, rows, size))
+            d_hidden[...] += against(slope, weights[array, :, first : first + size])
+        block = (blocks[0] if fold == 1 else jnp.concatenate(blocks, axis=1)).astype(BF16)
+        grads[index][...] = block.reshape(grads[index].shape)
 
     def step(group, number):
-        for item in group:
-            (item if isinstance(item, RelaySum) else item.relay).step(number)
-
-    for unit in units + simple + deep:
-        unit.start(*((0,) if isinstance(unit, Sum) else ()))
-    for unit in simple:
-        unit.finish()
-    for unit in units:
-        unit.finish(0)
-        unit.start(1)
-    step(simple, 1)
+        for unit in group:
+            unit.relay.step(number)
+
+    def then(index, number):
+        units[index].finish(number)
+        if number < 2:
+            units[index].start(number + 1)
+        else:
+            relays[index].step(0)
+
+    copies[0].wait()
+    hidden_turn[...] = hidden_in[...].T
+    d_hidden[...] = jnp.zeros_like(d_hidden)
+    count = len(units)
+    for index in range(count):
+        array = plan[index][0]
+        if index == 0 or plan[index - 1][0] != array:
+            copies[1 + 2 * array].wait()
+            copies[2 + 2 * array].wait()
+        compute(index)
+        units[index].start(0)
+        if index == 0:
+            for unit in simple:
+                unit.finish()
+        else:
+            then(index - 1, 0)
+        if index == 2:
+            step(simple, 1)
+        if index == 4:
+            step(simple, 2)
+    copies[7].wait()
+    copies[8].wait()
+    grad_values, grad_gain = norm_back(d_hidden[...], x_in[...].astype(F32), gain[...])
+    grad_x[...] = grad_values + middle[...]
+    gains_total[...] = gains[...]
+    gains_total[0:1] = grad_gain[None]
+    total.start(0)
+    then(count - 1, 0)
     for unit in deep:
         unit.finish()
-    step(simple, 2)
-    for unit in units:
-        unit.finish(1)
-        unit.start(2)
+    step(simple, 3)
+    for index in range(count // 2):
+        then(index, 1)
     step(deep, 1)
-    step(simple, 3)
-    for unit, relay in zip(units, relays):
-        unit.finish(2)
-        relay.step(0)
+    total.then(0)
+    for index in range(count // 2, count):
+        then(index, 1)
     step(deep, 2)
-    step(relays, 1)
+    total.then(1)
+    for index in range(count // 2):
+        then(index, 2)
+    total.then(2)
+    for relay in relays[: count // 2]:
+        relay.step(1)
+    for index in range(count // 2, count):
+        then(index, 2)
     step(deep, 3)
-    step(relays, 2)
-    step(relays, 3)
-
-
-def sums(arrays, helds, pieces, shapes, collective_id):
+    for relay in relays[count // 2 :]:
+        relay.step(1)
+    total.then(3)
+    for relay in relays:
+        relay.step(2)
+    for relay in relays:
+        relay.step(3)
+
+
+def closing(
+    slopes, weights, hidden, x, d_middle, grad_gain, cosine, sine, gain, rows, helds, pieces,
+    shapes, collective_id,
+):
     place = Place()
+    parts, tokens, width = slopes[0].shape
+    dim = parts * width
+    fold = 1
+    while rows * fold % 16:
+        fold *= 2
     plan, scratch = [], []
-    for number, array in enumerate(arrays):
-        rows, columns = array.shape[1:]
-        for place_in, (start, size) in enumerate(column_pieces(columns, 2)):
-            order = "xb" if place_in == 0 else "bx"
-            plan.append((number, start, size, order))
-            scratch += Sum.scratch(place, rows, size, order, array.dtype)
-            scratch += RelaySum.scratch(rows, size, array.dtype)
+    for array in range(3):
+        for start, size in column_pieces(dim // fold, 2):
+            order = "bx" if len(plan) % 2 == 1 else "xb"
+            plan.append((array, start, size, order))
+            lead = (place.xs, 2, place.as_, place.bs)
+            scratch.append(VMEM((*lead, rows * fold, size), BF16))
+            scratch += Sum.scratch(place, rows * fold, size, order, BF16, False)
+            scratch += DirectSum.scratch(place, rows * fold, size, BF16)
     for piece in pieces:
         scratch += HeldSum.scratch(place, piece, shapes[piece.array][0])
-    both = [placed(place, array) for array in arrays] + list(helds)
+    peers = 1 + (place.xs - 1) + (place.bs - 1) + (place.as_ - 1)
+    gains = jnp.pad(grad_gain[None], ((1, 6), (0, 0)))
     far, whole = pl.BlockSpec(memory_space=pl.ANY), pl.BlockSpec(memory_space=VMEM)
-    out = [jax.ShapeDtypeStruct(array.shape[1:], F32) for array in arrays]
-    out += [jax.ShapeDtypeStruct(shape, F32) for shape in shapes]
+    shape = jax.ShapeDtypeStruct
+    out = [shape((tokens, dim), F32), shape((tokens, dim), F32), shape((8, dim), F32)]
+    out += [shape((rows * fold, dim // fold), F32)] * 3
+    out += [shape(each, F32) for each in shapes]
     return pl.pallas_call(
-        functools.partial(sums_kernel, plan, pieces, len(arrays), len(shapes)),
-        in_specs=[far] * len(both),
+        functools.partial(closing_kernel, plan, pieces, rows, fold, len(shapes)),
+        in_specs=[far] * 9 + [whole] * 4 + [far] * len(helds),
         out_specs=[whole] * len(out),
         out_shape=out,
-        scratch_shapes=scratch,
+        scratch_shapes=[
+            VMEM((3, parts, tokens, width), BF16),
+            VMEM((3, dim, dim), BF16),
+            VMEM((tokens, dim), BF16),
+            VMEM((tokens, dim), BF16),
+            VMEM((tokens, dim), F32),
+            VMEM((dim, tokens), BF16),
+            VMEM((tokens, dim), F32),
+            VMEM((peers, 8, dim), F32),
+            pltpu.SemaphoreType.DMA((2, peers)),
+            pltpu.SemaphoreType.DMA((9,)),
+            *scratch,
+        ],
         compiler_params=pltpu.CompilerParams(
-            collective_id=collective_id, has_side_effects=True, vmem_limit_bytes=48 * MIB
+            collective_id=collective_id, has_side_effects=True, vmem_limit_bytes=60 * MIB
         ),
         cost_estimate=pl.CostEstimate(
-            flops=0, bytes_accessed=sum(array.size for array in arrays) * 4, transcendentals=0
+            flops=12 * tokens * dim * dim, bytes_accessed=20 * dim * dim, transcendentals=0
         ),
-        name="sums",
-    )(*both)
+        name="closing",
+    )(*slopes, *weights, hidden, x, d_middle, gains, cosine, sine, gain, *helds)
 
 
 def stacked(value, devices):
@@ -1358,19 +1548,14 @@
         value = jnp.pad(value, ((0, 0), (0, 0), (0, down_padded - down_rows)))
         return value.reshape(rows, devices * down_padded)
 
-    gains = jnp.pad(jnp.stack([gain_attn, gain_mlp]), ((0, 14), (0, 128 - rows)))
+    index = lax.axis_index("dp") * parts + rank
+    gains = jnp.pad(jnp.stack([gain_attn, gain_mlp]).astype(F32), ((0, 6), (0, width - rows)))
+    gains = jnp.roll(gains, index * rows, axis=1)
     wide = lambda value: stacked(value, 1)[0]
     padded_down = jnp.pad(w_down, ((0, down_padded - down_rows), (0, 0)))
     parted = [wide(w_out), wide(spaced(w_gate)), wide(spaced(w_up)), wide(padded_down)]
     shapes = [value.shape for value in parted]
     pieces = Piece.all(shapes)
-    (query_full, key_full, value_full, gains), helds = gathered(
-        [wide(w_query), wide(w_key), wide(w_value), gains], parted, pieces, 3
-    )
-    tall = lambda value: unstacked(value, rows)
-    query_full, key_full, value_full = tall(query_full), tall(key_full), tall(value_full)
-    gain_one, gain_two = (gains[:, n, :rows].reshape(width).astype(F32) for n in range(2))
-
     ends = jnp.cumsum(lengths[0])
     begins = ends - lengths[0]
     time = jnp.arange(tokens * parts, dtype=jnp.int32)
@@ -1386,10 +1571,13 @@
     start = start_all.reshape(parts, 1, tokens)
 
     x_low = inputs.reshape(tokens, width)
-    q, k, v, hidden_in = project(
-        x_low, gain_one[None], query_full, key_full, value_full,
-        first_values.reshape(tokens, width), cosine, sine, parts,
+    (q, k, v, hidden_in), gains, fulls, helds = opening(
+        x_low, first_values.reshape(tokens, width), cosine, sine, gains,
+        [wide(w_query), wide(w_key), wide(w_value)], parted, pieces, parts, 3,
     )
+    tall = lambda value: unstacked(value, rows)
+    query_full, key_full, value_full = (tall(value) for value in fulls)
+    gain_one, gain_two = gains[0], gains[1]
     (q_all, k_all, v_all, o_all, lse_all, attended), (*weights, down_full) = attend(
         q, k, v, start, helds, pieces, shapes
     )
@@ -1400,29 +1588,20 @@
         gate_full, up_full, down_full,
     )
     grad_gain_two = grad_gain_two[0]
-    x_in = x_low.astype(F32)
 
     share = lambda grad: stacked(grad.astype(BF16), devices)
     (dq, dk, dv), helds = attend_back(
         d_att, q_all, k_all, v_all, o_all, lse_all, start,
         [share(grad_out), share(grad_gate), share(grad_up), share(grad_down)], pieces,
     )
-    dq, dk, dv, grad_first = unproject(dq, dk, dv, cosine, sine)
-    grad_query_w = across(hidden_in, dq)
-    grad_key_w = across(hidden_in, dk)
-    grad_value_w = across(hidden_in, dv)
-    grad_hidden_in = against(dq, query_full) + against(dk, key_full) + against(dv, value_full)
-    grad_x, grad_gain_one = norm_back(grad_hidden_in, x_in, gain_one)
-    grad_x = grad_x + grad_middle
-    gains_grad = jnp.stack([grad_gain_one, grad_gain_two]).reshape(2, devices, rows)
-    gains_grad = jnp.pad(gains_grad.transpose(1, 0, 2), ((0, 0), (0, 6), (0, 128 - rows)))
     (
-        total_query, total_key, total_value, gains_total,
+        grad_first, grad_x, gains_total, total_query, total_key, total_value,
         total_out, total_gate, total_up, total_down,
-    ) = sums(
-        [share(grad_query_w), share(grad_key_w), share(grad_value_w), gains_grad],
-        helds, pieces, shapes, 4,
+    ) = closing(
+        (dq, dk, dv), (query_full, key_full, value_full), hidden_in, x_low, grad_middle,
+        grad_gain_two, cosine, sine, gain_one[None], rows, helds, pieces, shapes, 4,
     )
+    own_gain = lambda n: lax.dynamic_slice_in_dim(gains_total[n], index * rows, rows)
     low = lambda total: unstacked(total[None], rows)
 
     def close(total):
@@ -1437,11 +1616,11 @@
         low(total_key),
         low(total_value),
         low(total_out),
-        gains_total[0, :rows],
+        own_gain(0),
         close(total_gate),
         close(total_up),
         unstacked(total_down[None], down_padded)[:down_rows],
-        gains_total[1, :rows],
+        own_gain(1),
     )
 
 

time: 508 us -> 465 us (0.915); the launches traced: 507 us -> 457 us
  Pallas kernels: 455 us -> 432 us
  matrix products: 15.7 us -> 0 us
  local copies, waits for them, and re-layouts: 27.7 us -> 20 us
  other arithmetic: 8.16 us -> 2.91 us
    pallas_call x4 -> x2, Pallas kernels: 177 us -> 161 us  [the longest x1 82.6 us: closing(): pl.pallas_call(functools.partial(closing_kernel, plan, pieces, rows, fold...]
    dot_general x6 -> x0, matrix products: 15.7 us -> none  [dot(): lax.dot_general(left, right, (((left_dim,), (right_dim,)), ((), ())), pre...]
    unnamed x82 -> x42, local copies, waits for them, and re-layouts: 17.2 us -> 7.95 us
    pallas_call x1, Pallas kernels: 125 us -> 116 us  [attend(): pl.pallas_call(functools.partial(forward_kernel, parts, heads, pieces, le...]
where the time goes in v4:
time: 465 us; the launch traced here: 457 us
  Pallas kernels  432 us (93%)
  local copies, waits for them, and re-layouts  20 us (4%)
    pallas_call x1, Pallas kernels, attend(): pl.pallas_call(functools.partial(forward_kernel, parts, heads, pieces, le...  116 us
    pallas_call x1, Pallas kernels, attend_back(): pl.pallas_call(functools.partial(backward_kernel, parts, heads, pieces, l...  111 us
    pallas_call x1, Pallas kernels, closing(): pl.pallas_call(functools.partial(closing_kernel, plan, pieces, rows, fold...  82.6 us
    pallas_call x1, Pallas kernels, opening(): pl.pallas_call(functools.partial(opening_kernel, plan, pieces, len(parted...  78.1 us
    pallas_call x1, Pallas kernels, between(): pl.pallas_call(functools.partial(middle_kernel, units // chunk), grid=(un...  45 us

profile of v4, /device:TPU:0, one launch (start us, length us, event | category | flops | bytes accessed | tf_op | source)
XLA Modules:
  0.0 456.7 jit_solution(10476263025290402885)
XLA Ops:
  0.7 0.9 reduce-window.4
  1.6 0.7 fusion.12
  2.5 0.7 fusion.7
  3.3 0.3 fusion.6
  3.8 1.1 pad.23.refs_3_
  5.1 0.6 reshape.113
  5.8 0.3 squeeze_reshape_transpose_reshape_reshape.6.refs_1_
  6.1 0.6 reshape.114
  6.8 0.3 squeeze_reshape_transpose_reshape_reshape.7.refs_2_
  7.2 78.1 %opening.1 = (bf16[8,512,128]{2,1,0:T(8,128)(2,1)}, bf16[8,512,128]{2,1,0:T(8,128)(2,1)}, bf16[8,512,128]{2,1,0:T(8,128)(2,1)}, bf16[512,1024]{1,0:T(8,128)(2,1)...) custom-call(bf16[512,1024]{1,0:T(8,128)(2,1)} %bitcast.49, ...), custom_call_target="tpu_custom_call" | custom-call | flops 3221225472 | bytes 20971520 | tf_op jit(solution)/shard_map/opening/pallas_call | solution.py:924
  85.3 0.6 fusion.14
  85.9 116.1 %attend.1 = (bf16[8,512,128]{2,1,0:T(8,128)(2,1)S(1)}, bf16[8,512,128]{2,1,0:T(8,128)(2,1)}, bf16[8,512,128]{2,1,0:T(8,128)(2,1)}, f32[8,128,512]{2,1,0:T(8,128)...) custom-call(bf16[8,512,128]{2,1,0:T(8,128)(2,1)} %get-tuple-element., ...), custom_call_target="tpu_custom_call" | custom-call | flops 17179869184 | bytes 8388608 | tf_op jit(solution)/shard_map/attend/pallas_call | solution.py:273
  202.0 1.0 copy-done.7
  203.0 0.6 copy-done.8
  203.6 45.0 %between.1 = (bf16[512,1024]{1,0:T(8,128)(2,1)}, f32[512,1024]{1,0:T(8,128)}, bf16[8,512,128]{2,1,0:T(8,128)(2,1)}, bf16[1024,1024]{1,0:T(8,128)(2,1)}, bf16[102...) custom-call(bf16[512,1024]{1,0:T(8,128)(2,1)} %bitcast.50, ...), custom_call_target="tpu_custom_call" | custom-call | flops 28991029248 | bytes 37748736 | tf_op jit(solution)/shard_map/between/pallas_call | solution.py:1511
  248.6 1.3 pad.24.gains
  249.9 110.6 %attend_back.1 = (bf16[8,512,128]{2,1,0:T(8,128)(2,1)}, bf16[8,512,128]{2,1,0:T(8,128)(2,1)}, bf16[8,512,128]{2,1,0:T(8,128)(2,1)}, bf16[4,32,1024]{2,1,0:T(8,12...) custom-call(bf16[8,512,128]{2,1,0:T(8,128)(2,1)} %get-tuple-element., ...), custom_call_target="tpu_custom_call" | custom-call | flops 42949672960 | bytes 10485760 | tf_op jit(solution)/shard_map/attend_back/pallas_call | solution.py:464
  360.5 82.6 %closing.1 = (f32[512,1024]{1,0:T(8,128)}, f32[512,1024]{1,0:T(8,128)}, f32[8,1024]{1,0:T(8,128)}, f32[32,1024]{1,0:T(8,128)}, f32[32,1024]{1,0:T(8,128)}, /*ind...) custom-call(bf16[8,512,128]{2,1,0:T(8,128)(2,1)} %get-tuple-element.92., ...), custom_call_target="tpu_custom_call" | custom-call | flops 6442450944 | bytes 20971520 | tf_op jit(solution)/shard_map/closing/pallas_call | solution.py:1400
  443.1 0.8 fusion.13
  443.9 0.6 fusion.10
  444.5 1.9 slice.26
  446.4 1.2 reshape_reshape_transpose_reshape_broadcast_in_dim.6
  447.6 1.0 reshape.120
  448.7 0.2 reshape_reshape_transpose_reshape_broadcast_in_dim.7
  448.9 1.0 reshape.121
  449.9 1.3 copy.39
  451.2 1.0 copy-done.9
  452.3 1.3 copy.40
  453.6 0.7 copy.41
  454.3 0.7 copy.42
  454.9 0.7 copy.43
  455.6 0.7 copy.44
  (44 shorter events, 0.8 us)
Async XLA Ops:
  0.6 4.5 copy-start.12
  0.7 5.5 %copy-start.13 = (bf16[32,2816]{1,0:T(8,128)(2,1)S(1)}, bf16[32,2816]{1,0:T(8,128)(2,1)}, u32[]{:S(2)}) copy-start(bf16[32,2816]{1,0:T(8,128)(2,1)} %param.22) | copy-start | bytes 540676
  2.4 83.5 %copy-start.2 = (s32[4096]{0:T(1024)}, s32[4096]{0:T(1024)S(1)}, u32[]{:S(2)}) copy-start(s32[4096]{0:T(1024)S(1)} %select_reduce_fusion) | copy-start | bytes 49156
  3.8 81.5 %copy-start = (f32[512,128]{1,0:T(8,128)}, f32[512,128]{1,0:T(8,128)S(1)}, u32[]{:S(2)}) copy-start(f32[512,128]{1,0:T(8,128)S(1)} %copy.30.sine) | copy-start | bytes 786436
  3.8 3.3 copy-start.3
  3.8 3.3 copy-start.4
  3.8 3.3 copy-start.5
  3.8 3.3 copy-start.6
  5.1 80.1 %copy-start.1 = (f32[512,128]{1,0:T(8,128)}, f32[512,128]{1,0:T(8,128)S(1)}, u32[]{:S(2)}) copy-start(f32[512,128]{1,0:T(8,128)S(1)} %copy.29.cosine) | copy-start | bytes 786436
  202.0 1.0 copy-start.7
  203.0 0.6 copy-start.8
  443.1 5.6 %copy-start.11 = (f32[32,3072]{1,0:T(8,128)S(1)}, f32[32,3072]{1,0:T(8,128)}, u32[]{:S(2)}) copy-start(f32[32,3072]{1,0:T(8,128)} %get-tuple-element.116) | copy-start | bytes 1179652
  444.5 5.4 %copy-start.10 = (f32[512,1024]{1,0:T(8,128)S(1)}, f32[512,1024]{1,0:T(8,128)}, u32[]{:S(2)}) copy-start(f32[512,1024]{1,0:T(8,128)} %get-tuple-element.108) | copy-start | bytes 6291460
  449.9 2.3 copy-start.9
  452.3 1.3 copy-start.17
  452.3 2.0 copy-start.16
  452.3 2.6 copy-start.15
  452.3 3.3 copy-start.14

commit v5 on v4

--- a/solution.py
+++ b/solution.py
@@ -272,7 +272,7 @@
     ]
     results = pl.pallas_call(
         functools.partial(forward_kernel, parts, heads, pieces, len(shapes)),
-        in_specs=[whole] * 4 + [far] * len(pieces),
+        in_specs=[whole] * (4 + len(pieces)),
         out_specs=[whole] * 6 + [far] * len(shapes),
         out_shape=[
             split,
@@ -924,7 +924,7 @@
     results = pl.pallas_call(
         functools.partial(opening_kernel, plan, pieces, len(parted)),
         in_specs=[whole] * 5 + [far] * (3 + len(parted)),
-        out_specs=[whole] * len(near) + [far] * len(held),
+        out_specs=[whole] * (len(near) + len(held)),
         out_shape=near + held,
         scratch_shapes=[
             VMEM((peers, *gains.shape), F32),
@@ -1287,7 +1287,7 @@
                 value = turned(value, cosine[...], -sine[...])
             else:
                 value = 0.5 * value
-                grad_first[:, start : start + 128] = value
+                grad_first[:, start : start + 128] = value.astype(BF16)
             done.append(value.astype(BF16))
         return jnp.concatenate(done, axis=1)
 
@@ -1394,7 +1394,7 @@
     gains = jnp.pad(grad_gain[None], ((1, 6), (0, 0)))
     far, whole = pl.BlockSpec(memory_space=pl.ANY), pl.BlockSpec(memory_space=VMEM)
     shape = jax.ShapeDtypeStruct
-    out = [shape((tokens, dim), F32), shape((tokens, dim), F32), shape((8, dim), F32)]
+    out = [shape((tokens, dim), BF16), shape((tokens, dim), F32), shape((8, dim), F32)]
     out += [shape((rows * fold, dim // fold), F32)] * 3
     out += [shape(each, F32) for each in shapes]
     return pl.pallas_call(
@@ -1438,6 +1438,43 @@
     devices, high, columns = value.shape
     value = value.reshape(devices, high // rows, rows, columns).transpose(0, 2, 1, 3)
     return value.reshape(devices * rows, high // rows * columns)
+
+
+def settle_kernel(share, padded, first, grad_x, gate, up, down, *refs):
+    others, (first_out, x_out, gate_out, up_out, down_out, *others_out) = refs[:4], refs[4:]
+    first_out[...] = first[...].astype(F32)
+    x_out[...] = grad_x[...]
+
+    @pl.when(pl.program_id(0) == 0)
+    def _():
+        for source, target in ((gate, gate_out), (up, up_out)):
+            count = source.shape[1] // padded
+            target[...] = jnp.concatenate(
+                [source[:, n * padded : n * padded + share] for n in range(count)], axis=1
+            )
+        down_out[...] = down[:share]
+        for source, target in zip(others, others_out):
+            target[...] = source[...]
+
+
+def settle(first, grad_x, gate, up, down, others, share):
+    tokens, dim = grad_x.shape
+    padded = down.shape[0]
+    units = gate.shape[1] // padded * share
+    block = pl.BlockSpec((tokens // 4, dim), lambda g: (g, 0))
+    whole = lambda value: pl.BlockSpec(value.shape, lambda g: (0,) * len(value.shape))
+    shape = lambda *dims: jax.ShapeDtypeStruct(dims, F32)
+    outs = [shape(gate.shape[0], units)] * 2 + [shape(share, dim)]
+    outs += [shape(*value.shape) for value in others]
+    return pl.pallas_call(
+        functools.partial(settle_kernel, share, padded),
+        grid=(4,),
+        in_specs=[block, block] + [whole(value) for value in (gate, up, down, *others)],
+        out_specs=[block, block] + [whole(value) for value in outs],
+        out_shape=[shape(tokens, dim)] * 2 + outs,
+        compiler_params=pltpu.CompilerParams(vmem_limit_bytes=62 * MIB),
+        name="settle",
+    )(first, grad_x, gate, up, down, *others)
 
 
 def middle_kernel(
@@ -1522,7 +1559,7 @@
             VMEM((tokens, dim), F32),
             VMEM((tokens, dim), F32),
         ],
-        compiler_params=pltpu.CompilerParams(vmem_limit_bytes=56 * MIB),
+        compiler_params=pltpu.CompilerParams(vmem_limit_bytes=62 * MIB),
         cost_estimate=pl.CostEstimate(
             flops=18 * tokens * dim * units, bytes_accessed=12 * dim * units, transcendentals=0
         ),
@@ -1556,7 +1593,8 @@
     parted = [wide(w_out), wide(spaced(w_gate)), wide(spaced(w_up)), wide(padded_down)]
     shapes = [value.shape for value in parted]
     pieces = Piece.all(shapes)
-    ends = jnp.cumsum(lengths[0])
+    upto = jnp.arange(lengths.shape[1])
+    ends = jnp.sum(jnp.where(upto[:, None] >= upto[None, :], lengths, 0), axis=1)
     begins = ends - lengths[0]
     time = jnp.arange(tokens * parts, dtype=jnp.int32)
     inside = (time[:, None] >= begins[None, :]) & (time[:, None] < ends[None, :])
@@ -1602,24 +1640,29 @@
         grad_gain_two, cosine, sine, gain_one[None], rows, helds, pieces, shapes, 4,
     )
     own_gain = lambda n: lax.dynamic_slice_in_dim(gains_total[n], index * rows, rows)
-    low = lambda total: unstacked(total[None], rows)
-
-    def close(total):
-        total = low(total).reshape(rows, devices, down_padded)
-        return total[:, :, :down_rows].reshape(rows, devices * down_rows)
-
+    if rows % 16 == 0:
+        grad_first, grad_x, total_gate, total_up, total_down, *totals = settle(
+            grad_first, grad_x, total_gate, total_up, total_down,
+            (total_query, total_key, total_value, total_out), down_rows,
+        )
+    else:
+        low = lambda total: unstacked(total[None], rows)
+        close = lambda total: low(total).reshape(rows, devices, down_padded)[:, :, :down_rows]
+        total_gate, total_up = (
+            close(total).reshape(rows, devices * down_rows) for total in (total_gate, total_up)
+        )
+        total_down = unstacked(total_down[None], down_padded)[:down_rows]
+        totals = [low(total) for total in (total_query, total_key, total_value, total_out)]
+        grad_first = grad_first.astype(F32)
     return (
         output.reshape(inputs.shape),
         grad_x.reshape(inputs.shape),
         grad_first.reshape(inputs.shape),
-        low(total_query),
-        low(total_key),
-        low(total_value),
-        low(total_out),
+        *totals,
         own_gain(0),
-        close(total_gate),
-        close(total_up),
-        unstacked(total_down[None], down_padded)[:down_rows],
+        total_gate,
+        total_up,
+        total_down,
         own_gain(1),
     )
 

time: 465 us -> 459 us (0.987)
  local copies, waits for them, and re-layouts: 20 us -> 8.3 us
  Pallas kernels: 432 us -> 438 us
    unnamed x42 -> x22, local copies, waits for them, and re-layouts: 7.95 us -> 1.62 us
    pallas_call x0 -> x1, Pallas kernels: none -> 5.89 us  [settle(): pl.pallas_call(functools.partial(settle_kernel, share, padded), grid=(4,)...]
where the time goes in v5:
time: 459 us; the launch traced here: 450 us
  Pallas kernels  438 us (95%)
  local copies, waits for them, and re-layouts  8.3 us (2%)
    pallas_call x1, Pallas kernels, attend(): pl.pallas_call(functools.partial(forward_kernel, parts, heads, pieces, le...  116 us
    pallas_call x1, Pallas kernels, attend_back(): pl.pallas_call(functools.partial(backward_kernel, parts, heads, pieces, l...  111 us
    pallas_call x1, Pallas kernels, closing(): pl.pallas_call(functools.partial(closing_kernel, plan, pieces, rows, fold...  82.2 us
    pallas_call x1, Pallas kernels, opening(): pl.pallas_call(functools.partial(opening_kernel, plan, pieces, len(parted...  78 us
    pallas_call x1, Pallas kernels, between(): pl.pallas_call(functools.partial(middle_kernel, units // chunk), grid=(un...  45 us

profile of v5, /device:TPU:0, one launch (start us, length us, event | category | flops | bytes accessed | tf_op | source)
XLA Modules:
  0.0 450.4 jit_solution(2486723663628925484)
XLA Ops:
  0.7 0.8 select_reduce_fusion.1
  1.5 0.7 fusion.12
  2.2 0.1 select_reduce_fusion
  2.3 0.0 copy-start.2
  2.3 0.1 subtract_convert_fusion
  2.4 0.7 fusion.7
  3.1 0.1 fusion.9.gains
  3.2 0.3 fusion.6
  3.6 0.1 copy.30.sine
  3.7 0.0 copy-start
  3.7 0.0 copy-start.3
  3.8 0.0 copy-start.4
  3.8 1.1 pad.23.refs_3_
  4.9 0.1 copy.29.cosine
  5.1 0.6 reshape.97
  5.7 0.1 pad.21
  5.7 0.3 squeeze_reshape_transpose_reshape_reshape.6.refs_1_
  6.1 0.6 reshape.98
  6.7 0.1 pad.22
  6.7 0.3 squeeze_reshape_transpose_reshape_reshape.7.refs_2_
  7.1 78.0 %opening.1 = (bf16[8,512,128]{2,1,0:T(8,128)(2,1)}, bf16[8,512,128]{2,1,0:T(8,128)(2,1)}, bf16[8,512,128]{2,1,0:T(8,128)(2,1)}, bf16[512,1024]{1,0:T(8,128)(2,1)...) custom-call(bf16[512,1024]{1,0:T(8,128)(2,1)} %bitcast.43, ...), custom_call_target="tpu_custom_call" | custom-call | flops 3221225472 | bytes 20971520 | tf_op jit(solution)/shard_map/opening/pallas_call | solution.py:924
  85.2 0.6 fusion.14
  85.8 116.4 %attend.1 = (bf16[8,512,128]{2,1,0:T(8,128)(2,1)S(1)}, bf16[8,512,128]{2,1,0:T(8,128)(2,1)}, bf16[8,512,128]{2,1,0:T(8,128)(2,1)}, f32[8,128,512]{2,1,0:T(8,128)...) custom-call(bf16[8,512,128]{2,1,0:T(8,128)(2,1)} %get-tuple-element., ...), custom_call_target="tpu_custom_call" | custom-call | flops 17179869184 | bytes 8388608 | tf_op jit(solution)/shard_map/attend/pallas_call | solution.py:273
  202.2 1.0 copy-done.7
  203.2 0.6 copy-done.8
  203.8 45.0 %between.1 = (bf16[512,1024]{1,0:T(8,128)(2,1)}, f32[512,1024]{1,0:T(8,128)}, bf16[8,512,128]{2,1,0:T(8,128)(2,1)}, bf16[1024,1024]{1,0:T(8,128)(2,1)}, bf16[102...) custom-call(bf16[512,1024]{1,0:T(8,128)(2,1)} %bitcast.44, ...), custom_call_target="tpu_custom_call" | custom-call | flops 28991029248 | bytes 37748736 | tf_op jit(solution)/shard_map/between/pallas_call | solution.py:1548
  248.8 1.3 pad.24.gains
  250.1 110.5 %attend_back.1 = (bf16[8,512,128]{2,1,0:T(8,128)(2,1)}, bf16[8,512,128]{2,1,0:T(8,128)(2,1)}, bf16[8,512,128]{2,1,0:T(8,128)(2,1)}, bf16[4,32,1024]{2,1,0:T(8,12...) custom-call(bf16[8,512,128]{2,1,0:T(8,128)(2,1)} %get-tuple-element., ...), custom_call_target="tpu_custom_call" | custom-call | flops 42949672960 | bytes 10485760 | tf_op jit(solution)/shard_map/attend_back/pallas_call | solution.py:464
  360.6 82.2 %closing.1 = (bf16[512,1024]{1,0:T(8,128)(2,1)}, f32[512,1024]{1,0:T(8,128)}, f32[8,1024]{1,0:T(8,128)}, f32[32,1024]{1,0:T(8,128)}, f32[32,1024]{1,0:T(8,128)},...) custom-call(bf16[8,512,128]{2,1,0:T(8,128)(2,1)} %get-tuple-element., ...), custom_call_target="tpu_custom_call" | custom-call | flops 6442450944 | bytes 20971520 | tf_op jit(solution)/shard_map/closing/pallas_call | solution.py:1400
  442.8 0.8 fusion.13
  443.7 0.6 fusion.10
  444.3 5.9 %settle.1 = (f32[512,1024]{1,0:T(8,128)}, f32[512,1024]{1,0:T(8,128)}, f32[32,2816]{1,0:T(8,128)}, f32[32,2816]{1,0:T(8,128)}, f32[88,1024]{1,0:T(8,128)}, /*ind...) custom-call(bf16[512,1024]{1,0:T(8,128)(2,1)} %get-tuple-element.117.first, ...), custom_call_target="tpu_custom_call" | custom-call | tf_op jit(solution)/shard_map/settle/pallas_call | solution.py:1469
  (20 shorter events, 0.1 us)
Async XLA Ops:
  0.6 4.4 copy-start.9
  0.7 5.4 %copy-start.10 = (bf16[32,2816]{1,0:T(8,128)(2,1)S(1)}, bf16[32,2816]{1,0:T(8,128)(2,1)}, u32[]{:S(2)}) copy-start(bf16[32,2816]{1,0:T(8,128)(2,1)} %param.22) | copy-start | bytes 540676
  2.3 83.5 %copy-start.2 = (s32[4096]{0:T(1024)}, s32[4096]{0:T(1024)S(1)}, u32[]{:S(2)}) copy-start(s32[4096]{0:T(1024)S(1)} %select_reduce_fusion) | copy-start | bytes 49156
  3.7 81.4 %copy-start = (f32[512,128]{1,0:T(8,128)}, f32[512,128]{1,0:T(8,128)S(1)}, u32[]{:S(2)}) copy-start(f32[512,128]{1,0:T(8,128)S(1)} %copy.30.sine) | copy-start | bytes 786436
  3.7 3.4 copy-start.3
  3.8 3.3 copy-start.4
  3.8 3.3 copy-start.5
  3.8 3.3 copy-start.6
  5.1 80.1 %copy-start.1 = (f32[512,128]{1,0:T(8,128)}, f32[512,128]{1,0:T(8,128)S(1)}, u32[]{:S(2)}) copy-start(f32[512,128]{1,0:T(8,128)S(1)} %copy.29.cosine) | copy-start | bytes 786436
  202.2 1.0 copy-start.7
  203.2 0.6 copy-start.8

commit v6 on v5

--- a/solution.py
+++ b/solution.py
@@ -95,8 +95,9 @@
     q_in, k_in, v_in, start, *refs,
 ):
     helds, refs = refs[: len(pieces)], refs[len(pieces) :]
-    q_all, k_all, v_all, o_all, lse_all, attended = refs[:6]
-    fulls, refs = refs[6 : 6 + count], refs[6 + count :]
+    kept, (lse_all, attended), refs = refs[:4], refs[4:6], refs[6:]
+    fulls, refs = refs[:count], refs[count:]
+    q_all, k_all, v_all, o_all, keep, *refs = refs
     v_turn, total, o_send, in_send, in_recv, o_out, o_in, *sems = refs
     place = Place()
     _, tokens, width = q_in.shape
@@ -237,6 +238,12 @@
         return 0
 
     lax.fori_loop(0, 3 * half, tile_row, 0)
+    keeps = [
+        pltpu.make_async_copy(source, target, keep.at[n])
+        for n, (source, target) in enumerate(zip((q_all, k_all, v_all, o_all), kept))
+    ]
+    for copy in keeps:
+        copy.start()
     spread.finish()
     pl.when(own == 0)(lambda: sent_cross((0,)))
     pl.when(own == 1)(lambda: sent_cross((1, 2)))
@@ -257,6 +264,8 @@
 
     lax.fori_loop(1, parts, finish, 0)
     arrive(attended.at[me], o_in.at[me])
+    for copy in keeps:
+        copy.wait()
 
 
 def attend(q, k, v, start, helds, pieces, shapes):
@@ -272,8 +281,8 @@
     ]
     results = pl.pallas_call(
         functools.partial(forward_kernel, parts, heads, pieces, len(shapes)),
-        in_specs=[whole] * (4 + len(pieces)),
-        out_specs=[whole] * 6 + [far] * len(shapes),
+        in_specs=[far] * 3 + [whole] * (1 + len(pieces)),
+        out_specs=[far] * 4 + [whole] * 2 + [far] * len(shapes),
         out_shape=[
             split,
             split,
@@ -284,6 +293,9 @@
             *fulls,
         ],
         scratch_shapes=[
+            *[VMEM(split.shape, BF16)] * 3,
+            VMEM((parts, width, tokens), F32),
+            pltpu.SemaphoreType.DMA((4,)),
             VMEM((parts, width, tokens), BF16),
             VMEM((parts, heads, 1, tokens), F32),
             VMEM((parts, tokens, width), BF16),
@@ -308,11 +320,12 @@
 
 def backward_kernel(
     parts, heads, pieces, count,
-    d_in, q_all, k_all, v_all, o_all, lse_all, start, *refs,
+    d_in, q_kept, k_kept, v_kept, o_kept, lse_all, start, *refs,
 ):
     grads, refs = refs[:count], refs[count:]
     (dq_got, dk_got, dv_got), refs = refs[:3], refs[3:]
     results, refs = refs[: len(pieces)], refs[len(pieces) :]
+    q_all, k_all, v_all, o_all, keep, *refs = refs
     d_all, k_turn, delta, dq_turn, dk_sum, dv_sum, dq_send, dk_send, dv_send = refs[:9]
     in_send, in_recv, out_send, out_recv, *buffers = refs[9:]
     place = Place()
@@ -320,6 +333,14 @@
     half = parts // 2
     me = lax.axis_index("seq")
     own = me // half
+    keeps = [
+        pltpu.make_async_copy(source, target, keep.at[n])
+        for n, (source, target) in enumerate(
+            zip((q_kept, k_kept, v_kept, o_kept), (q_all, k_all, v_all, o_all))
+        )
+    ]
+    for copy in keeps:
+        copy.start()
     place.greet(greet(parts, me))
     adding = GradSums(place, pieces, grads, results, buffers)
 
@@ -432,6 +453,8 @@
         pl.when(jnp.logical_not(by_query))(lambda: give_keys(outer))
         return 0
 
+    for copy in keeps:
+        copy.wait()
     lax.fori_loop(0, 3 * half, tile_row, 0)
     pl.when(own == 0)(lambda: over(0, give_keys))
     pl.when(own == 1)(lambda: over(half, give_query))
@@ -463,10 +486,13 @@
     grads = [placed(place, grad) for grad in grads]
     results = pl.pallas_call(
         functools.partial(backward_kernel, parts, heads, pieces, len(grads)),
-        in_specs=[far] + [whole] * 6 + [far] * len(grads),
+        in_specs=[far] * 5 + [whole] * 2 + [far] * len(grads),
         out_specs=[far] * 3 + [far] * len(pieces),
         out_shape=[split] * 3 + sum_shapes,
         scratch_shapes=[
+            *[VMEM(split.shape, BF16)] * 3,
+            VMEM((parts, width, tokens), F32),
+            pltpu.SemaphoreType.DMA((4,)),
             VMEM((parts, tokens, width), BF16),
             VMEM((parts, width, tokens), BF16),
             VMEM((parts, heads, 1, tokens), F32),
@@ -796,13 +822,15 @@
 
 
 def opening_kernel(
-    plan, pieces, parted,
+    plan, pieces, parted, padded,
     x, first, cosine, sine, gains, w_query, w_key, w_value, *refs,
 ):
     shares, refs = refs[:parted], refs[parted:]
-    q_out, k_out, v_out, hidden, gains_total, *fulls = refs[:8]
-    helds, refs = refs[8 : 8 + len(pieces)], refs[8 + len(pieces) :]
-    got_gains, gain_sems, relay_sems, *sems = refs
+    (q_out, k_out, v_out, hidden, gains_total), kept, refs = refs[:5], refs[5:8], refs[8:]
+    helds, refs = refs[: len(pieces)], refs[len(pieces) :]
+    fulls, (keep, got_gains, gain_sems, relay_sems, *refs) = refs[:3], refs[3:]
+    spaced, sems = refs[:padded], refs[padded:]
+    given, shares = shares, [*shares[: parted - padded], *spaced]
     place = Place()
     parts, tokens, width = q_out.shape
     dim = parts * width
@@ -873,6 +901,18 @@
 
     step(relays, 0)
     total.start(0)
+    if padded:
+        *wides, tall = given[parted - padded :]
+        for source, target in zip(wides, spaced):
+            share = tall.shape[0]
+            gap = spaced[-1].shape[0] - share
+            value, gaps = source[...].astype(F32), jnp.zeros((source.shape[0], gap), F32)
+            parts_of = [value[:, n : n + share] for n in range(0, value.shape[1], share)]
+            target[...] = jnp.concatenate(
+                [part for value in parts_of for part in (value, gaps)], axis=1
+            ).astype(BF16)
+        gaps = jnp.zeros((gap, tall.shape[1]), F32)
+        spaced[-1][...] = jnp.concatenate([tall[...].astype(F32), gaps], axis=0).astype(BF16)
     step(relays, 1)
     tick(0)
     step(relays, 2)
@@ -895,17 +935,24 @@
     then(units[:half], 1)
     tick(5)
     then(units[half:], 1)
+    keeps = []
     for array in range(3):
         then([unit for unit, piece in zip(units, plan) if piece[0] == array], 2)
+        keeps.append(pltpu.make_async_copy(fulls[array], kept[array], keep.at[array]))
+        keeps[array].start()
         project(array)
         tick(6 + array)
     for number in range(9, len(line) + 3):
         tick(number)
     for unit in deep:
         unit.finish(0)
-
-
-def opening(x, first, cosine, sine, gains, weights, parted, pieces, parts, collective_id):
+    for copy in keeps:
+        copy.wait()
+
+
+def opening(
+    x, first, cosine, sine, gains, weights, parted, shapes, pieces, parts, collective_id
+):
     place = Place()
     xs, as_, bs = place.xs, place.as_, place.bs
     tokens, dim = x.shape
@@ -917,19 +964,24 @@
     near = [shape((parts, tokens, dim // parts), BF16)] * 3
     near += [shape((tokens, dim), BF16), shape(gains.shape, F32)]
     near += [shape((xs, 2, as_, bs, *array.shape), array.dtype) for array in weights]
-    held = [piece.held(place, parted[piece.array].shape[0]) for piece in pieces]
+    held = [piece.held(place, shapes[piece.array][0]) for piece in pieces]
+    padded = sum(array.shape != shape for array, shape in zip(parted, shapes))
+    ready = len(parted) - padded
     far, whole = pl.BlockSpec(memory_space=pl.ANY), pl.BlockSpec(memory_space=VMEM)
     count = len(plan) + len(pieces)
     peers = 1 + (xs - 1) + (bs - 1) + (as_ - 1)
     results = pl.pallas_call(
-        functools.partial(opening_kernel, plan, pieces, len(parted)),
-        in_specs=[whole] * 5 + [far] * (3 + len(parted)),
-        out_specs=[whole] * (len(near) + len(held)),
+        functools.partial(opening_kernel, plan, pieces, len(parted), padded),
+        in_specs=[whole] * 5 + [far] * (3 + ready) + [whole] * padded,
+        out_specs=[whole] * 5 + [far] * 3 + [whole] * len(held),
         out_shape=near + held,
         scratch_shapes=[
+            *[VMEM(each.shape, BF16) for each in near[5:]],
+            pltpu.SemaphoreType.DMA((3,)),
             VMEM((peers, *gains.shape), F32),
             pltpu.SemaphoreType.DMA((2, peers)),
             pltpu.SemaphoreType.DMA((count, *RELAY_SEMAPHORES)),
+            *[VMEM(shape, BF16) for shape in shapes[ready:]],
             *[spread_semaphores(place)] * count,
         ],
         compiler_params=pltpu.CompilerParams(
@@ -1238,10 +1290,10 @@
     dq, dk, dv, w_query, w_key, w_value, hidden, x, d_middle, gains, cosine, sine, gain, *refs,
 ):
     helds, refs = refs[: len(pieces)], refs[len(pieces) :]
-    grad_first, grad_x, gains_total, *refs = refs
+    first_out, x_out, gains_total, *refs = refs
     results, buffers = refs[: 3 + parted], refs[3 + parted :]
     slopes, weights, hidden_in, x_in, middle, hidden_turn, d_hidden, got_gains, gain_sems = buffers[:9]
-    loads, buffers = buffers[9], buffers[10:]
+    loads, grad_first, grad_x, *buffers = buffers[9:]
     place = Place()
     parts, tokens, width = dq.shape
     dim = parts * width
@@ -1337,6 +1389,12 @@
     copies[8].wait()
     grad_values, grad_gain = norm_back(d_hidden[...], x_in[...].astype(F32), gain[...])
     grad_x[...] = grad_values + middle[...]
+    keeps = [
+        pltpu.make_async_copy(grad_first, first_out, loads.at[0]),
+        pltpu.make_async_copy(grad_x, x_out, loads.at[1]),
+    ]
+    for copy in keeps:
+        copy.start()
     gains_total[...] = gains[...]
     gains_total[0:1] = grad_gain[None]
     total.start(0)
@@ -1367,6 +1425,8 @@
         relay.step(2)
     for relay in relays:
         relay.step(3)
+    for copy in keeps:
+        copy.wait()
 
 
 def closing(
@@ -1391,7 +1451,6 @@
     for piece in pieces:
         scratch += HeldSum.scratch(place, piece, shapes[piece.array][0])
     peers = 1 + (place.xs - 1) + (place.bs - 1) + (place.as_ - 1)
-    gains = jnp.pad(grad_gain[None], ((1, 6), (0, 0)))
     far, whole = pl.BlockSpec(memory_space=pl.ANY), pl.BlockSpec(memory_space=VMEM)
     shape = jax.ShapeDtypeStruct
     out = [shape((tokens, dim), BF16), shape((tokens, dim), F32), shape((8, dim), F32)]
@@ -1400,7 +1459,7 @@
     return pl.pallas_call(
         functools.partial(closing_kernel, plan, pieces, rows, fold, len(shapes)),
         in_specs=[far] * 9 + [whole] * 4 + [far] * len(helds),
-        out_specs=[whole] * len(out),
+        out_specs=[far] * 2 + [whole] * (len(out) - 2),
         out_shape=out,
         scratch_shapes=[
             VMEM((3, parts, tokens, width), BF16),
@@ -1413,6 +1472,8 @@
             VMEM((peers, 8, dim), F32),
             pltpu.SemaphoreType.DMA((2, peers)),
             pltpu.SemaphoreType.DMA((9,)),
+            VMEM((tokens, dim), BF16),
+            VMEM((tokens, dim), F32),
             *scratch,
         ],
         compiler_params=pltpu.CompilerParams(
@@ -1422,7 +1483,7 @@
             flops=12 * tokens * dim * dim, bytes_accessed=20 * dim * dim, transcendentals=0
         ),
         name="closing",
-    )(*slopes, *weights, hidden, x, d_middle, gains, cosine, sine, gain, *helds)
+    )(*slopes, *weights, hidden, x, d_middle, grad_gain, cosine, sine, gain, *helds)
 
 
 def stacked(value, devices):
@@ -1519,7 +1580,8 @@
         grad_values, grad_gain = norm_back(d_hidden[...], middle[...], gain[...])
         total = grad_values + dy[...].astype(F32)
         d_middle[...] = total
-        g_gain[...] = grad_gain[None]
+        g_gain[...] = jnp.zeros_like(g_gain)
+        g_gain[1:2] = grad_gain[None]
         d_branch = total.astype(BF16)
         g_out[...] = across(attended[...], d_branch).astype(BF16)
         back = against(d_branch, w_out[...]).astype(BF16)
@@ -1543,7 +1605,7 @@
         shape(w_gate.shape, BF16),
         shape(w_up.shape, BF16),
         shape(w_down.shape, BF16),
-        shape((1, dim), F32),
+        shape((8, dim), F32),
     ]
     return pl.pallas_call(
         functools.partial(middle_kernel, units // chunk),
@@ -1589,9 +1651,14 @@
     gains = jnp.pad(jnp.stack([gain_attn, gain_mlp]).astype(F32), ((0, 6), (0, width - rows)))
     gains = jnp.roll(gains, index * rows, axis=1)
     wide = lambda value: stacked(value, 1)[0]
-    padded_down = jnp.pad(w_down, ((0, down_padded - down_rows), (0, 0)))
-    parted = [wide(w_out), wide(spaced(w_gate)), wide(spaced(w_up)), wide(padded_down)]
-    shapes = [value.shape for value in parted]
+    padded_units = devices * down_padded
+    if rows % 16 == 0:
+        parted = [w_out, w_gate, w_up, w_down]
+        shapes = [w_out.shape, *[(rows, padded_units)] * 2, (down_padded, width)]
+    else:
+        padded_down = jnp.pad(w_down, ((0, down_padded - down_rows), (0, 0)))
+        parted = [wide(w_out), wide(spaced(w_gate)), wide(spaced(w_up)), wide(padded_down)]
+        shapes = [value.shape for value in parted]
     pieces = Piece.all(shapes)
     upto = jnp.arange(lengths.shape[1])
     ends = jnp.sum(jnp.where(upto[:, None] >= upto[None, :], lengths, 0), axis=1)
@@ -1611,7 +1678,7 @@
     x_low = inputs.reshape(tokens, width)
     (q, k, v, hidden_in), gains, fulls, helds = opening(
         x_low, first_values.reshape(tokens, width), cosine, sine, gains,
-        [wide(w_query), wide(w_key), wide(w_value)], parted, pieces, parts, 3,
+        [wide(w_query), wide(w_key), wide(w_value)], parted, shapes, pieces, parts, 3,
     )
     tall = lambda value: unstacked(value, rows)
     query_full, key_full, value_full = (tall(value) for value in fulls)
@@ -1625,7 +1692,6 @@
         x_low, attended, cotangent.reshape(tokens, width), out_full, gain_two[None],
         gate_full, up_full, down_full,
     )
-    grad_gain_two = grad_gain_two[0]
 
     share = lambda grad: stacked(grad.astype(BF16), devices)
     (dq, dk, dv), helds = attend_back(

time: 459 us -> 439 us (0.956); the launches traced: 450 us -> 437 us
  Pallas kernels: 438 us -> 429 us
where the time goes in v6:
time: 439 us; the launch traced here: 437 us
  Pallas kernels  429 us (98%)
    pallas_call x1, Pallas kernels, attend(): pl.pallas_call(functools.partial(forward_kernel, parts, heads, pieces, le...  113 us
    pallas_call x1, Pallas kernels, attend_back(): pl.pallas_call(functools.partial(backward_kernel, parts, heads, pieces, l...  111 us
    pallas_call x1, Pallas kernels, closing(): pl.pallas_call(functools.partial(closing_kernel, plan, pieces, rows, fold...  78.5 us
    pallas_call x1, Pallas kernels, opening(): pl.pallas_call(functools.partial(opening_kernel, plan, pieces, len(parted...  76.1 us
    pallas_call x1, Pallas kernels, between(): pl.pallas_call(functools.partial(middle_kernel, units // chunk), grid=(un...  45 us

profile of v6, /device:TPU:0, one launch (start us, length us, event | category | flops | bytes accessed | tf_op | source)
XLA Modules:
  0.0 437.3 jit_solution(10279282349856226675)
XLA Ops:
  0.6 0.0 copy-start.5
  0.7 0.0 copy-start.4
  0.7 0.0 copy-start.3
  0.7 0.0 copy-start.9
  0.7 0.0 copy-start.8
  0.7 0.0 copy-start.7
  0.7 0.0 copy-start.6
  0.7 0.9 select_reduce_fusion.1
  1.6 0.7 fusion.12
  2.3 0.1 select_reduce_fusion
  2.4 0.0 copy-start.2
  2.4 0.1 subtract_convert_fusion
  2.5 0.7 fusion.7
  3.2 0.1 fusion.9.gains
  3.4 0.3 fusion.6
  3.7 0.1 copy.30.sine
  3.8 0.0 copy-start
  3.9 0.1 copy.29.cosine
  4.0 0.0 copy-done.5
  4.0 0.0 copy-done.4
  4.1 0.0 copy-start.1
  4.1 76.1 %opening.1 = (bf16[8,512,128]{2,1,0:T(8,128)(2,1)}, bf16[8,512,128]{2,1,0:T(8,128)(2,1)}, bf16[8,512,128]{2,1,0:T(8,128)(2,1)}, bf16[512,1024]{1,0:T(8,128)(2,1)...) custom-call(bf16[512,1024]{1,0:T(8,128)(2,1)} %bitcast.43, ...), custom_call_target="tpu_custom_call" | custom-call | flops 3221225472 | bytes 20971520 | tf_op jit(solution)/shard_map/opening/pallas_call | solution.py:973
  80.3 0.6 fusion.14
  80.9 113.1 %attend.1 = (bf16[8,512,128]{2,1,0:T(8,128)(2,1)S(1)}, bf16[8,512,128]{2,1,0:T(8,128)(2,1)}, bf16[8,512,128]{2,1,0:T(8,128)(2,1)}, f32[8,128,512]{2,1,0:T(8,128)...) custom-call(bf16[8,512,128]{2,1,0:T(8,128)(2,1)} %get-tuple-element., ...), custom_call_target="tpu_custom_call" | custom-call | flops 17179869184 | bytes 8388608 | tf_op jit(solution)/shard_map/attend/pallas_call | solution.py:282
  194.0 1.0 copy-done.10
  194.9 0.6 copy-done.11
  195.6 45.0 %between.1 = (bf16[512,1024]{1,0:T(8,128)(2,1)}, f32[512,1024]{1,0:T(8,128)}, bf16[8,512,128]{2,1,0:T(8,128)(2,1)}, bf16[1024,1024]{1,0:T(8,128)(2,1)}, bf16[102...) custom-call(bf16[512,1024]{1,0:T(8,128)(2,1)} %bitcast.44, ...), custom_call_target="tpu_custom_call" | custom-call | flops 28991029248 | bytes 37748736 | tf_op jit(solution)/shard_map/between/pallas_call | solution.py:1610
  240.6 110.7 %attend_back.1 = (bf16[8,512,128]{2,1,0:T(8,128)(2,1)}, bf16[8,512,128]{2,1,0:T(8,128)(2,1)}, bf16[8,512,128]{2,1,0:T(8,128)(2,1)}, bf16[4,32,1024]{2,1,0:T(8,12...) custom-call(bf16[8,512,128]{2,1,0:T(8,128)(2,1)} %get-tuple-element., ...), custom_call_target="tpu_custom_call" | custom-call | flops 42949672960 | bytes 10485760 | tf_op jit(solution)/shard_map/attend_back/pallas_call | solution.py:487
  351.3 78.5 %closing.1 = (bf16[512,1024]{1,0:T(8,128)(2,1)}, f32[512,1024]{1,0:T(8,128)}, f32[8,1024]{1,0:T(8,128)}, f32[32,1024]{1,0:T(8,128)}, f32[32,1024]{1,0:T(8,128)},...) custom-call(bf16[8,512,128]{2,1,0:T(8,128)(2,1)} %get-tuple-element., ...), custom_call_target="tpu_custom_call" | custom-call | flops 6442450944 | bytes 20971520 | tf_op jit(solution)/shard_map/closing/pallas_call | solution.py:1459
  429.8 0.8 fusion.13
  430.7 0.6 fusion.10
  431.3 5.9 %settle.1 = (f32[512,1024]{1,0:T(8,128)}, f32[512,1024]{1,0:T(8,128)}, f32[32,2816]{1,0:T(8,128)}, f32[32,2816]{1,0:T(8,128)}, f32[88,1024]{1,0:T(8,128)}, /*ind...) custom-call(bf16[512,1024]{1,0:T(8,128)(2,1)} %get-tuple-element.117.first, ...), custom_call_target="tpu_custom_call" | custom-call | tf_op jit(solution)/shard_map/settle/pallas_call | solution.py:1530
  (14 shorter events, 0.1 us)
Async XLA Ops:
  0.6 3.4 copy-start.5
  0.7 3.4 copy-start.4
  0.7 3.4 copy-start.3
  0.7 3.4 copy-start.9
  0.7 3.4 copy-start.8
  0.7 3.4 copy-start.7
  0.7 3.4 copy-start.6
  2.4 78.4 %copy-start.2 = (s32[4096]{0:T(1024)}, s32[4096]{0:T(1024)S(1)}, u32[]{:S(2)}) copy-start(s32[4096]{0:T(1024)S(1)} %select_reduce_fusion) | copy-start | bytes 49156
  3.8 76.4 %copy-start = (f32[512,128]{1,0:T(8,128)}, f32[512,128]{1,0:T(8,128)S(1)}, u32[]{:S(2)}) copy-start(f32[512,128]{1,0:T(8,128)S(1)} %copy.30.sine) | copy-start | bytes 786436
  4.1 76.2 %copy-start.1 = (f32[512,128]{1,0:T(8,128)}, f32[512,128]{1,0:T(8,128)S(1)}, u32[]{:S(2)}) copy-start(f32[512,128]{1,0:T(8,128)S(1)} %copy.29.cosine) | copy-start | bytes 786436
  194.0 1.0 copy-start.10
  194.9 0.6 copy-start.11

commit v7 on v6

--- a/solution.py
+++ b/solution.py
@@ -1286,12 +1286,15 @@
 
 
 def closing_kernel(
-    plan, pieces, rows, fold, parted,
+    plan, pieces, rows, fold, parted, share,
     dq, dk, dv, w_query, w_key, w_value, hidden, x, d_middle, gains, cosine, sine, gain, *refs,
 ):
     helds, refs = refs[: len(pieces)], refs[len(pieces) :]
     first_out, x_out, gains_total, *refs = refs
     results, buffers = refs[: 3 + parted], refs[3 + parted :]
+    closed = results[4:6]
+    if share:
+        results, buffers = [*results[:4], *buffers[:2], *results[6:]], buffers[2:]
     slopes, weights, hidden_in, x_in, middle, hidden_turn, d_hidden, got_gains, gain_sems = buffers[:9]
     loads, grad_first, grad_x, *buffers = buffers[9:]
     place = Place()
@@ -1420,6 +1423,11 @@
     step(deep, 3)
     for relay in relays[count // 2 :]:
         relay.step(1)
+    for source, target in zip(results[4:6], closed) if share else ():
+        padded = source.shape[1] // devices
+        target[...] = jnp.concatenate(
+            [source[:, n * padded : n * padded + share] for n in range(devices)], axis=1
+        )
     total.then(3)
     for relay in relays:
         relay.step(2)
@@ -1431,7 +1439,7 @@
 
 def closing(
     slopes, weights, hidden, x, d_middle, grad_gain, cosine, sine, gain, rows, helds, pieces,
-    shapes, collective_id,
+    shapes, share, collective_id,
 ):
     place = Place()
     parts, tokens, width = slopes[0].shape
@@ -1455,13 +1463,17 @@
     shape = jax.ShapeDtypeStruct
     out = [shape((tokens, dim), BF16), shape((tokens, dim), F32), shape((8, dim), F32)]
     out += [shape((rows * fold, dim // fold), F32)] * 3
-    out += [shape(each, F32) for each in shapes]
+    final = list(shapes)
+    if share:
+        final[1:3] = [(rows, dim // rows * share)] * 2
+    out += [shape(each, F32) for each in final]
     return pl.pallas_call(
-        functools.partial(closing_kernel, plan, pieces, rows, fold, len(shapes)),
+        functools.partial(closing_kernel, plan, pieces, rows, fold, len(shapes), share),
         in_specs=[far] * 9 + [whole] * 4 + [far] * len(helds),
         out_specs=[far] * 2 + [whole] * (len(out) - 2),
         out_shape=out,
         scratch_shapes=[
+            *[VMEM(each, F32) for each in shapes[1:3] if share],
             VMEM((3, parts, tokens, width), BF16),
             VMEM((3, dim, dim), BF16),
             VMEM((tokens, dim), BF16),
@@ -1501,41 +1513,35 @@
     return value.reshape(devices * rows, high // rows * columns)
 
 
-def settle_kernel(share, padded, first, grad_x, gate, up, down, *refs):
-    others, (first_out, x_out, gate_out, up_out, down_out, *others_out) = refs[:4], refs[4:]
+def settle_kernel(share, first, grad_x, down, *refs):
+    count = len(refs) // 2 - 1
+    others, (first_out, x_out, down_out, *others_out) = refs[:count], refs[count:]
     first_out[...] = first[...].astype(F32)
     x_out[...] = grad_x[...]
 
     @pl.when(pl.program_id(0) == 0)
     def _():
-        for source, target in ((gate, gate_out), (up, up_out)):
-            count = source.shape[1] // padded
-            target[...] = jnp.concatenate(
-                [source[:, n * padded : n * padded + share] for n in range(count)], axis=1
-            )
         down_out[...] = down[:share]
         for source, target in zip(others, others_out):
             target[...] = source[...]
 
 
-def settle(first, grad_x, gate, up, down, others, share):
+def settle(first, grad_x, down, others, share):
     tokens, dim = grad_x.shape
-    padded = down.shape[0]
-    units = gate.shape[1] // padded * share
     block = pl.BlockSpec((tokens // 4, dim), lambda g: (g, 0))
     whole = lambda value: pl.BlockSpec(value.shape, lambda g: (0,) * len(value.shape))
     shape = lambda *dims: jax.ShapeDtypeStruct(dims, F32)
-    outs = [shape(gate.shape[0], units)] * 2 + [shape(share, dim)]
+    outs = [shape(share, dim)]
     outs += [shape(*value.shape) for value in others]
     return pl.pallas_call(
-        functools.partial(settle_kernel, share, padded),
+        functools.partial(settle_kernel, share),
         grid=(4,),
-        in_specs=[block, block] + [whole(value) for value in (gate, up, down, *others)],
+        in_specs=[block, block] + [whole(value) for value in (down, *others)],
         out_specs=[block, block] + [whole(value) for value in outs],
         out_shape=[shape(tokens, dim)] * 2 + outs,
         compiler_params=pltpu.CompilerParams(vmem_limit_bytes=62 * MIB),
         name="settle",
-    )(first, grad_x, gate, up, down, *others)
+    )(first, grad_x, down, *others)
 
 
 def middle_kernel(
@@ -1592,7 +1598,7 @@
 def between(x, att, dy, w_out, gain, w_gate, w_up, w_down):
     tokens, dim = x.shape
     units = w_gate.shape[1]
-    chunk = 512 if units % 512 == 0 else 128
+    chunk = 256 if units % 256 == 0 else 128
     whole = lambda value: pl.BlockSpec(value.shape, lambda g: (0,) * len(value.shape))
     wide = pl.BlockSpec((dim, chunk), lambda g: (0, g))
     tall = pl.BlockSpec((chunk, dim), lambda g: (g, 0))
@@ -1703,13 +1709,14 @@
         total_out, total_gate, total_up, total_down,
     ) = closing(
         (dq, dk, dv), (query_full, key_full, value_full), hidden_in, x_low, grad_middle,
-        grad_gain_two, cosine, sine, gain_one[None], rows, helds, pieces, shapes, 4,
+        grad_gain_two, cosine, sine, gain_one[None], rows, helds, pieces, shapes,
+        down_rows if rows % 16 == 0 else 0, 4,
     )
     own_gain = lambda n: lax.dynamic_slice_in_dim(gains_total[n], index * rows, rows)
     if rows % 16 == 0:
-        grad_first, grad_x, total_gate, total_up, total_down, *totals = settle(
-            grad_first, grad_x, total_gate, total_up, total_down,
-            (total_query, total_key, total_value, total_out), down_rows,
+        grad_first, grad_x, total_down, total_gate, total_up, *totals = settle(
+            grad_first, grad_x, total_down,
+            (total_gate, total_up, total_query, total_key, total_value, total_out), down_rows,
         )
     else:
         low = lambda total: unstacked(total[None], rows)

time: 439 us -> 438 us (level)
  no operation moved by 1% of the time
where the time goes in v7:
time: 438 us; the launch traced here: 436 us
  Pallas kernels  428 us (98%)
    pallas_call x1, Pallas kernels, attend(): pl.pallas_call(functools.partial(forward_kernel, parts, heads, pieces, le...  113 us
    pallas_call x1, Pallas kernels, attend_back(): pl.pallas_call(functools.partial(backward_kernel, parts, heads, pieces, l...  111 us
    pallas_call x1, Pallas kernels, closing(): pl.pallas_call(functools.partial(closing_kernel, plan, pieces, rows, fold...  78.2 us
    pallas_call x1, Pallas kernels, opening(): pl.pallas_call(functools.partial(opening_kernel, plan, pieces, len(parted...  76.1 us
    pallas_call x1, Pallas kernels, between(): pl.pallas_call(functools.partial(middle_kernel, units // chunk), grid=(un...  44.5 us

profile of v7, /device:TPU:0, one launch (start us, length us, event | category | flops | bytes accessed | tf_op | source)
XLA Modules:
  0.0 436.1 jit_solution(4889396968011345098)
XLA Ops:
  0.6 0.0 copy-start.5
  0.7 0.0 copy-start.4
  0.7 0.0 copy-start.3
  0.7 0.0 copy-start.9
  0.7 0.0 copy-start.8
  0.7 0.0 copy-start.7
  0.7 0.0 copy-start.6
  0.7 0.9 select_reduce_fusion.1
  1.6 0.7 fusion.12
  2.3 0.1 select_reduce_fusion
  2.4 0.0 copy-start.2
  2.4 0.1 subtract_convert_fusion
  2.5 0.7 fusion.7
  3.2 0.1 fusion.9.gains
  3.4 0.3 fusion.6
  3.7 0.1 copy.30.sine
  3.8 0.0 copy-start
  3.9 0.1 copy.29.cosine
  4.0 0.0 copy-done.5
  4.1 0.0 copy-start.1
  4.1 76.1 %opening.1 = (bf16[8,512,128]{2,1,0:T(8,128)(2,1)}, bf16[8,512,128]{2,1,0:T(8,128)(2,1)}, bf16[8,512,128]{2,1,0:T(8,128)(2,1)}, bf16[512,1024]{1,0:T(8,128)(2,1)...) custom-call(bf16[512,1024]{1,0:T(8,128)(2,1)} %bitcast.43, ...), custom_call_target="tpu_custom_call" | custom-call | flops 3221225472 | bytes 20971520 | tf_op jit(solution)/shard_map/opening/pallas_call | solution.py:973
  80.3 0.6 fusion.14
  80.9 113.1 %attend.1 = (bf16[8,512,128]{2,1,0:T(8,128)(2,1)S(1)}, bf16[8,512,128]{2,1,0:T(8,128)(2,1)}, bf16[8,512,128]{2,1,0:T(8,128)(2,1)}, f32[8,128,512]{2,1,0:T(8,128)...) custom-call(bf16[8,512,128]{2,1,0:T(8,128)(2,1)} %get-tuple-element., ...), custom_call_target="tpu_custom_call" | custom-call | flops 17179869184 | bytes 8388608 | tf_op jit(solution)/shard_map/attend/pallas_call | solution.py:282
  194.0 0.0 copy-start.10
  194.0 1.0 copy-done.10
  194.9 0.6 copy-done.11
  195.6 44.5 %between.1 = (bf16[512,1024]{1,0:T(8,128)(2,1)}, f32[512,1024]{1,0:T(8,128)}, bf16[8,512,128]{2,1,0:T(8,128)(2,1)}, bf16[1024,1024]{1,0:T(8,128)(2,1)}, bf16[102...) custom-call(bf16[512,1024]{1,0:T(8,128)(2,1)} %bitcast.44, ...), custom_call_target="tpu_custom_call" | custom-call | flops 28991029248 | bytes 37748736 | tf_op jit(solution)/shard_map/between/pallas_call | solution.py:1616
  240.0 110.7 %attend_back.1 = (bf16[8,512,128]{2,1,0:T(8,128)(2,1)}, bf16[8,512,128]{2,1,0:T(8,128)(2,1)}, bf16[8,512,128]{2,1,0:T(8,128)(2,1)}, bf16[4,32,1024]{2,1,0:T(8,12...) custom-call(bf16[8,512,128]{2,1,0:T(8,128)(2,1)} %get-tuple-element., ...), custom_call_target="tpu_custom_call" | custom-call | flops 42949672960 | bytes 10485760 | tf_op jit(solution)/shard_map/attend_back/pallas_call | solution.py:487
  350.8 78.2 %closing.1 = (bf16[512,1024]{1,0:T(8,128)(2,1)}, f32[512,1024]{1,0:T(8,128)}, f32[8,1024]{1,0:T(8,128)}, f32[32,1024]{1,0:T(8,128)}, f32[32,1024]{1,0:T(8,128)},...) custom-call(bf16[8,512,128]{2,1,0:T(8,128)(2,1)} %get-tuple-element., ...), custom_call_target="tpu_custom_call" | custom-call | flops 6442450944 | bytes 20971520 | tf_op jit(solution)/shard_map/closing/pallas_call | solution.py:1470
  429.0 0.8 fusion.13
  429.8 0.6 fusion.10
  430.4 5.5 %settle.1 = (f32[512,1024]{1,0:T(8,128)}, f32[512,1024]{1,0:T(8,128)}, f32[88,1024]{1,0:T(8,128)}, f32[32,2816]{1,0:T(8,128)}, f32[32,2816]{1,0:T(8,128)}, /*ind...) custom-call(bf16[512,1024]{1,0:T(8,128)(2,1)} %get-tuple-element.117.first, ...), custom_call_target="tpu_custom_call" | custom-call | tf_op jit(solution)/shard_map/settle/pallas_call | solution.py:1536
  (14 shorter events, 0.1 us)
Async XLA Ops:
  0.6 3.4 copy-start.5
  0.7 3.4 copy-start.4
  0.7 3.4 copy-start.3
  0.7 3.4 copy-start.9
  0.7 3.4 copy-start.8
  0.7 3.4 copy-start.7
  0.7 3.4 copy-start.6
  2.4 78.4 %copy-start.2 = (s32[4096]{0:T(1024)}, s32[4096]{0:T(1024)S(1)}, u32[]{:S(2)}) copy-start(s32[4096]{0:T(1024)S(1)} %select_reduce_fusion) | copy-start | bytes 49156
  3.8 76.4 %copy-start = (f32[512,128]{1,0:T(8,128)}, f32[512,128]{1,0:T(8,128)S(1)}, u32[]{:S(2)}) copy-start(f32[512,128]{1,0:T(8,128)S(1)} %copy.30.sine) | copy-start | bytes 786436
  4.1 76.2 %copy-start.1 = (f32[512,128]{1,0:T(8,128)}, f32[512,128]{1,0:T(8,128)S(1)}, u32[]{:S(2)}) copy-start(f32[512,128]{1,0:T(8,128)S(1)} %copy.29.cosine) | copy-start | bytes 786436
  194.0 1.0 copy-start.10
  194.9 0.6 copy-start.11
